TPU v7x, 32 devices: a whole 2x2x4 slice. The times are simulated.
32 devices in a mesh: member: 2 (over x), lon: 8 (over z, y), lat: 2 (over core).
Axes of the slice: x: 2, y: 2, z: 4, core: 2. Of those that a mesh axis runs over, the one named last changes fastest.
Arguments:
- iterate: float32 [4, 640, 1024], P('member', 'lat', 'lon'), parts along dimension 0, may hold values from -6 to 6
- residual: float32 [4, 640, 1024], P('member', 'lat', 'lon'), parts along dimension 0, may hold values from -6 to 6
- direction: float32 [4, 640, 1024], P('member', 'lat', 'lon'), parts along dimension 0, may hold values from -6 to 6
- land_sea: int32 [2, 640, 1024], P(None, 'lat', 'lon'), may hold values 0 or 1
- precision_weight: float32 [2, 640, 1024], P(None, 'lat', 'lon'), may hold values from 0.2 to 5
- east_kappa: float32 [640, 1024], P('lat', 'lon'), may hold values from 0.18 to 0.24
- north_kappa: float32 [640, 1024], P('lat', 'lon'), may hold values from 0.18 to 0.24
- fold_partner: int32 [1024], replicated, may hold values from 0 to 1023, as said below
Outputs:
- new_iterate: float32 [4, 640, 1024], P('member', 'lat', 'lon'), parts along dimension 0
- new_residual: float32 [4, 640, 1024], P('member', 'lat', 'lon'), parts along dimension 0
- new_direction: float32 [4, 640, 1024], P('member', 'lat', 'lon'), parts along dimension 0
There are 2 independent parts, one for each index of `member`. A program takes and returns all parts, laid end to end along the dimension named above; an argument that names none is the same for every part. Nothing has to cross between parts.
Inputs may be any that keep to these rules, and one draw needn't show every extreme that they name: fold_partner pairs the columns: fold_partner[fold_partner[i]] = i and fold_partner[i] != i.
All inputs are finite; a program needn't handle non-finite values. No bound on the sum of `land_sea` on one device may be relied on, other than what follows from the above.
Results may differ from a plain program's by a relative error of at most 0.00002.
Values sent between devices are 32-bit elements; how exact they have to be, the bound alone decides.
No kernel may reach another device: no remote copies, remote signals or barrier semaphores. Data moves between devices by JAX's collectives and lax.ppermute only.
A program may use at most 64 MiB of HBM per device.

v0:
```python
import jax
import jax.numpy as jnp
from jax import lax
from jax.sharding import PartitionSpec as P

STEPS = 4


def with_halo(block, sides, width, periodic):
    for axis, dim in sides:
        count = lax.axis_size(axis)
        forward = [(i, i + 1) for i in range(count - 1)]
        if periodic:
            forward.append((count - 1, 0))
        backward = [(target, source) for source, target in forward]
        low = lax.ppermute(
            lax.slice_in_dim(block, block.shape[dim] - width, None, axis=dim), axis, forward
        )
        high = lax.ppermute(lax.slice_in_dim(block, 0, width, axis=dim), axis, backward)
        block = jnp.concatenate([low, block, high], axis=dim)
    return block


def shifted(value, axis, steps):
    count = lax.axis_size(axis)
    pairs = [(source, (source + steps) % count) for source in range(count)]
    return lax.ppermute(value, axis, pairs)


def passed_along(block, axis, distance):
    devices = range(lax.axis_size(axis))
    route = [(i - distance, i) for i in devices if i - distance in devices]
    return lax.ppermute(block, axis, route)


def neighbours(field):
    widened = with_halo(field, (("lon", 2),), 1, True)
    padded = with_halo(widened, (("lat", 1),), 1, False)
    return padded


def diffuse(field, coeffs, local_partner, top_flag):
    east_face, west_face, north_face, south_face = coeffs
    padded = neighbours(field)
    east = padded[:, 1:-1, 2:]
    west = padded[:, 1:-1, :-2]
    north = padded[:, 2:, 1:-1]
    south = padded[:, :-2, 1:-1]
    whole_row = lax.all_gather(field[:, -1, :], "lon", axis=1, tiled=True)
    folded = jnp.take(whole_row, local_partner, axis=1)
    last_row = jnp.where(top_flag, folded, north[:, -1])
    north = jnp.concatenate([north[:, :-1], last_row[:, None]], axis=1)
    return (
        field
        + east_face * (east - field)
        - west_face * (field - west)
        + north_face * (north - field)
        - south_face * (field - south)
    )


def shards(
    iterate, residual, direction, land_sea, precision_weight, east_kappa, north_kappa, fold_partner
):
    levels, rows, columns = iterate.shape
    steps = STEPS
    lat_index = lax.axis_index("lat")
    top_flag = lat_index == lax.axis_size("lat") - 1
    bottom_flag = lat_index == 0
    local_partner = lax.dynamic_slice_in_dim(fold_partner, lax.axis_index("lon") * columns, columns)
    ocean = land_sea.astype(jnp.float32)
    east_column = shifted(ocean[:, :, :1], "lon", -1)
    north_row = passed_along(ocean[:, :1, :], "lat", -1)
    ocean_east = jnp.concatenate([ocean[:, :, 1:], east_column], axis=2)
    ocean_north = jnp.concatenate([ocean[:, 1:, :], north_row], axis=1)
    east_face = east_kappa[None] * ocean * ocean_east
    inner = north_kappa[None] * ocean * ocean_north
    top_mask, top_kappa = (
        lax.all_gather(ocean[:, -1, :], "lon", axis=1, tiled=True),
        lax.all_gather(north_kappa[-1:, :], "lon", axis=1, tiled=True),
    )
    mask_across = jnp.take(top_mask, local_partner, axis=1)
    kappa_across = jnp.take(top_kappa, local_partner, axis=1)
    fold_face = (0.5 * (north_kappa[-1] + kappa_across[0]))[None] * ocean[:, -1] * mask_across
    last_face = jnp.where(top_flag, fold_face, inner[:, -1])
    north_face = jnp.concatenate([inner[:, :-1], last_face[:, None]], axis=1)
    west_column = shifted(east_face[:, :, -1:], "lon", 1)
    south_row = passed_along(north_face[:, -1:, :], "lat", 1)
    west_face = jnp.concatenate([west_column, east_face[:, :, :-1]], axis=2)
    first_south = jnp.where(bottom_flag, jnp.zeros_like(south_row), south_row)
    south_face = jnp.concatenate([first_south, north_face[:, :-1]], axis=1)
    coeffs = (east_face, west_face, north_face, south_face)
    field = ocean * direction
    for step in range(steps):
        field = diffuse(field, coeffs, local_partner, top_flag)
    field = precision_weight * ocean * field
    for step in range(steps):
        field = diffuse(field, coeffs, local_partner, top_flag)
    image = direction + ocean * field
    old_norm = lax.psum(jnp.sum(residual * residual), ("lon", "lat"))
    curve = lax.psum(jnp.sum(direction * image), ("lon", "lat"))
    alpha = old_norm / curve
    new_iterate = iterate + alpha * direction
    new_residual = residual - alpha * image
    new_norm = lax.psum(jnp.sum(new_residual * new_residual), ("lon", "lat"))
    new_direction = new_residual + new_norm / old_norm * direction
    return (new_iterate, new_residual, new_direction)


def solution(mesh):
    placed = (
        P("member", "lat", "lon"),
        P("member", "lat", "lon"),
        P("member", "lat", "lon"),
        P(None, "lat", "lon"),
        P(None, "lat", "lon"),
        P("lat", "lon"),
        P("lat", "lon"),
        P(),
    )
    return jax.shard_map(
        shards,
        mesh=mesh,
        in_specs=placed,
        out_specs=(P("member", "lat", "lon"), P("member", "lat", "lon"), P("member", "lat", "lon")),
        check_vma=False,
    )
```

profile of v0, /device:TPU:0, one launch (start us, length us, event | category | flops | bytes accessed | tf_op | source)
XLA Modules:
  0.0 468.3 jit_solution(5107336976150682652)
XLA Ops:
  1.7 1.4 collective-permute-start.4
  3.3 6.1 %collective-permute-start = (f32[2,320,1]{2,0,1:T(2,128)S(1)}, f32[2,320,1]{2,0,1:T(2,128)S(1)}, u32[]{:S(2)}, u32[]{:S(2)}) collective-permute-start(f32[2,320,1]{2,0,1:T(2,128)S(1)} %bitcast.115), channel_id=1, source_target_pairs={{0,14},{2,0},{4,2},{6,4},{8,6},{10,8},{12,10},{14,12},{1,15},{3,1}... | collective-permute-start | bytes 7688 | tf_op jit(solution)/shard_map/ppermute | solution.py:27
  10.2 21.7 %all_gather.30 = f32[1,1024]{1,0:T(1,128)S(1)} all-gather(f32[1,128]{1,0:T(1,128)S(1)} %slice.363), channel_id=1, replica_groups=mesh['member'=2,'lon'=8,'lat'=2] {'lon'}, dimensions={1}, use_global_device_ids=true | all-gather | bytes 4608 | tf_op jit(solution)/shard_map/all_gather | solution.py:80
  36.6 2.0 collective-permute-start.3
  38.7 21.8 %all-gather = f32[2,1,1024]{2,0,1:T(2,128)S(1)} all-gather(f32[2,1,128]{2,0,1:T(2,128)S(1)} %slice.471), channel_id=2, replica_groups=mesh['member'=2,'lon'=8,'lat'=2] {'lon'}, dimensions={2}, use_global_device_ids=true | all-gather | bytes 9216 | tf_op jit(solution)/shard_map/all_gather | solution.py:79
  63.4 18.2 %all-gather.1 = f32[2,1,1024]{2,0,1:T(2,128)S(1)} all-gather(f32[2,1,128]{2,0,1:T(2,128)S(1)} %slice.474), channel_id=3, replica_groups=mesh['member'=2,'lon'=8,'lat'=2] {'lon'}, dimensions={2}, use_global_device_ids=true | all-gather | bytes 9216 | tf_op jit(solution)/shard_map/all_gather | solution.py:49
  85.9 8.5 %collective-permute-done.2 = f32[2,320,1]{2,0,1:T(2,128)S(1)} collective-permute-done((f32[2,320,1]{2,0,1:T(2,128)S(1)}, f32[2,320,1]{2,0,1:T(2,128)S(1)}, u32[]{:S(2)}, u32[]{:S(2)}) %collective-permute-start.2) | collective-permute-done | bytes 2592 | tf_op jit(solution)/shard_map/ppermute | solution.py:27
  94.3 2.5 fusion.75
  97.3 2.0 collective-permute-start.9
  99.3 10.9 %collective-permute-done.8 = f32[2,320,1]{2,0,1:T(2,128)S(1)} collective-permute-done((f32[2,320,1]{2,0,1:T(2,128)S(1)}, f32[2,320,1]{2,0,1:T(2,128)S(1)}, u32[]{:S(2)}, u32[]{:S(2)}) %collective-permute-start.8) | collective-permute-done | bytes 2592 | tf_op jit(solution)/shard_map/ppermute | solution.py:19
  111.6 17.3 %all-gather.2 = f32[2,1,1024]{2,0,1:T(2,128)S(1)} all-gather(f32[2,1,128]{2,0,1:T(2,128)S(1)} %slice.479), channel_id=4, replica_groups=mesh['member'=2,'lon'=8,'lat'=2] {'lon'}, dimensions={2}, use_global_device_ids=true | all-gather | bytes 9216 | tf_op jit(solution)/shard_map/all_gather | solution.py:49
  130.6 1.3 collective-permute-start.11
  132.7 3.1 pad_maximum_fusion.43
  138.3 14.9 %collective-permute-done.12 = f32[2,320,1]{2,0,1:T(2,128)S(1)} collective-permute-done((f32[2,320,1]{2,0,1:T(2,128)S(1)}, f32[2,320,1]{2,0,1:T(2,128)S(1)}, u32[]{:S(2)}, u32[]{:S(2)}) %collective-permute-start.12) | collective-permute-done | bytes 2592 | tf_op jit(solution)/shard_map/ppermute | solution.py:19
  154.6 18.0 %all-gather.3 = f32[2,1,1024]{2,0,1:T(2,128)S(1)} all-gather(f32[2,1,128]{2,0,1:T(2,128)S(1)} %slice.484), channel_id=5, replica_groups=mesh['member'=2,'lon'=8,'lat'=2] {'lon'}, dimensions={2}, use_global_device_ids=true | all-gather | bytes 9216 | tf_op jit(solution)/shard_map/all_gather | solution.py:49
  174.4 1.7 gather_fusion.4
  178.3 3.1 fusion.55
  182.1 1.7 collective-permute-start.17
  183.9 14.9 %collective-permute-done.16 = f32[2,320,1]{2,0,1:T(2,128)S(1)} collective-permute-done((f32[2,320,1]{2,0,1:T(2,128)S(1)}, f32[2,320,1]{2,0,1:T(2,128)S(1)}, u32[]{:S(2)}, u32[]{:S(2)}) %collective-permute-start.16) | collective-permute-done | bytes 2592 | tf_op jit(solution)/shard_map/ppermute | solution.py:19
  199.6 1.4 collective-permute-start.18
  201.0 17.4 %all-gather.4 = f32[2,1,1024]{2,0,1:T(2,128)S(1)} all-gather(f32[2,1,128]{2,0,1:T(2,128)S(1)} %slice-done.2), channel_id=6, replica_groups=mesh['member'=2,'lon'=8,'lat'=2] {'lon'}, dimensions={2}, use_global_device_ids=true | all-gather | bytes 9216 | tf_op jit(solution)/shard_map/all_gather | solution.py:49
  219.5 1.7 gather_fusion.5
  221.2 1.5 collective-permute-start.19
  223.3 4.6 fusion.45
  230.4 15.0 %collective-permute-done.20 = f32[2,320,1]{2,0,1:T(2,128)S(1)} collective-permute-done((f32[2,320,1]{2,0,1:T(2,128)S(1)}, f32[2,320,1]{2,0,1:T(2,128)S(1)}, u32[]{:S(2)}, u32[]{:S(2)}) %collective-permute-start.20) | collective-permute-done | bytes 2592 | tf_op jit(solution)/shard_map/ppermute | solution.py:19
  245.5 1.4 collective-permute-start.22
  246.9 18.0 %all-gather.5 = f32[2,1,1024]{2,0,1:T(2,128)S(1)} all-gather(f32[2,1,128]{2,0,1:T(2,128)S(1)} %slice-done.4), channel_id=7, replica_groups=mesh['member'=2,'lon'=8,'lat'=2] {'lon'}, dimensions={2}, use_global_device_ids=true | all-gather | bytes 9216 | tf_op jit(solution)/shard_map/all_gather | solution.py:49
  266.0 1.7 gather_fusion.6
  269.8 2.1 fusion.34
  272.7 1.7 collective-permute-start.25
  274.5 14.9 %collective-permute-done.24 = f32[2,320,1]{2,0,1:T(2,128)S(1)} collective-permute-done((f32[2,320,1]{2,0,1:T(2,128)S(1)}, f32[2,320,1]{2,0,1:T(2,128)S(1)}, u32[]{:S(2)}, u32[]{:S(2)}) %collective-permute-start.24) | collective-permute-done | bytes 2592 | tf_op jit(solution)/shard_map/ppermute | solution.py:19
  289.5 1.4 collective-permute-start.26
  290.9 17.4 %all-gather.6 = f32[2,1,1024]{2,0,1:T(2,128)S(1)} all-gather(f32[2,1,128]{2,0,1:T(2,128)S(1)} %slice-done.8), channel_id=8, replica_groups=mesh['member'=2,'lon'=8,'lat'=2] {'lon'}, dimensions={2}, use_global_device_ids=true | all-gather | bytes 9216 | tf_op jit(solution)/shard_map/all_gather | solution.py:49
  309.4 1.7 gather_fusion.7
  313.3 2.1 fusion.24
  317.9 14.9 %collective-permute-done.28 = f32[2,320,1]{2,0,1:T(2,128)S(1)} collective-permute-done((f32[2,320,1]{2,0,1:T(2,128)S(1)}, f32[2,320,1]{2,0,1:T(2,128)S(1)}, u32[]{:S(2)}, u32[]{:S(2)}) %collective-permute-start.28) | collective-permute-done | bytes 2592 | tf_op jit(solution)/shard_map/ppermute | solution.py:19
  333.0 1.4 collective-permute-start.30
  334.4 18.0 %all-gather.7 = f32[2,1,1024]{2,0,1:T(2,128)S(1)} all-gather(f32[2,1,128]{2,0,1:T(2,128)S(1)} %slice-done.6), channel_id=9, replica_groups=mesh['member'=2,'lon'=8,'lat'=2] {'lon'}, dimensions={2}, use_global_device_ids=true | all-gather | bytes 9216 | tf_op jit(solution)/shard_map/all_gather | solution.py:49
  353.4 1.7 gather_fusion.8
  355.2 1.3 collective-permute-start.31
  357.3 2.1 fusion.14
  360.2 1.7 collective-permute-start.33
  362.7 14.2 %collective-permute-done.32 = f32[2,320,1]{2,0,1:T(2,128)S(1)} collective-permute-done((f32[2,320,1]{2,0,1:T(2,128)S(1)}, f32[2,320,1]{2,0,1:T(2,128)S(1)}, u32[]{:S(2)}, u32[]{:S(2)}) %collective-permute-start.32) | collective-permute-done | bytes 2592 | tf_op jit(solution)/shard_map/ppermute | solution.py:19
  379.8 16.7 %all-gather.8 = f32[2,1,1024]{2,0,1:T(2,128)S(1)} all-gather(f32[2,1,128]{2,0,1:T(2,128)S(1)} %slice-done), channel_id=10, replica_groups=mesh['member'=2,'lon'=8,'lat'=2] {'lon'}, dimensions={2}, use_global_device_ids=true | all-gather | bytes 9216 | tf_op jit(solution)/shard_map/all_gather | solution.py:49
  397.5 1.7 gather_fusion.9
  400.7 2.2 fusion.8
  403.8 30.1 %all-reduce = (f32[]{:T(128)}, f32[]{:T(128)}) all-reduce(f32[]{:T(128)} %multiply_reduce_fusion.2, f32[]{:T(128)} %get-tuple-element.20), channel_id=1, replica_groups=mesh['member'=2,'lon'=8,'lat'=2] {'lon','lat'}, use_global_device_ids=true, to_apply=%region_1.2 | all-reduce | flops 2 | bytes 16 | tf_op jit(solution)/shard_map/psum | solution.py:100
  435.9 30.1 %psum.23 = f32[]{:T(128)} all-reduce(f32[]{:T(128)} %get-tuple-element.18), channel_id=1, replica_groups=mesh['member'=2,'lon'=8,'lat'=2] {'lon','lat'}, use_global_device_ids=true, to_apply=%region_5.7 | all-reduce | flops 1 | bytes 8 | tf_op jit(solution)/shard_map/psum | solution.py:105
  (191 shorter events, 52.5 us)
Async XLA Ops:
  1.6 8.5 %copy-start.21 = (f32[320,128]{1,0:T(8,128)S(1)}, f32[320,128]{1,0:T(8,128)}, u32[]{:S(2)}) copy-start(f32[320,128]{1,0:T(8,128)} %param.16) | copy-start | bytes 491524
  1.7 31.7 %collective-permute-start.4 = (f32[2,1,128]{2,1,0:T(1,128)S(1)}, f32[2,1,128]{2,1,0:T(1,128)S(1)}, u32[]{:S(2)}, u32[]{:S(2)}) collective-permute-start(f32[2,1,128]{2,1,0:T(1,128)S(1)} %slice.469), channel_id=1, source_target_pairs={{1,0},{3,2},{5,4},{7,6},{9,8},{11,10},{13,12},{15,14},{17,16},{19,... | collective-permute-start | bytes 3080 | tf_op jit(solution)/shard_map/ppermute | solution.py:33
  3.3 30.0 %collective-permute-start = (f32[2,320,1]{2,0,1:T(2,128)S(1)}, f32[2,320,1]{2,0,1:T(2,128)S(1)}, u32[]{:S(2)}, u32[]{:S(2)}) collective-permute-start(f32[2,320,1]{2,0,1:T(2,128)S(1)} %bitcast.115), channel_id=1, source_target_pairs={{0,14},{2,0},{4,2},{6,4},{8,6},{10,8},{12,10},{14,12},{1,15},{3,1}... | collective-permute-start | bytes 7688 | tf_op jit(solution)/shard_map/ppermute | solution.py:27
  36.6 24.7 %collective-permute-start.1 = (f32[2,320,1]{2,0,1:T(2,128)}, f32[2,320,1]{2,0,1:T(2,128)S(1)}, u32[]{:S(2)}, u32[]{:S(2)}) collective-permute-start(f32[2,320,1]{2,0,1:T(2,128)} %get-tuple-element.64), channel_id=1, source_target_pairs={{2,0},{4,2},{6,4},{8,6},{10,8},{12,10},{14,12},{0,14},{3,1},{5,3},... | collective-permute-start | bytes 7688 | tf_op jit(solution)/shard_map/ppermute | solution.py:19
  36.6 24.7 %collective-permute-start.3 = (f32[2,320,1]{2,0,1:T(2,128)}, f32[2,320,1]{2,0,1:T(2,128)S(1)}, u32[]{:S(2)}, u32[]{:S(2)}) collective-permute-start(f32[2,320,1]{2,0,1:T(2,128)} %get-tuple-element.63), channel_id=1, source_target_pairs={{0,2},{2,4},{4,6},{6,8},{8,10},{10,12},{12,14},{14,0},{1,3},{3,5},... | collective-permute-start | bytes 7688 | tf_op jit(solution)/shard_map/ppermute | solution.py:16
  62.1 20.5 %collective-permute-start.5 = (f32[2,1,130]{2,0,1:T(2,128)S(1)}, f32[2,1,130]{2,0,1:T(2,128)S(1)}, u32[]{:S(2)}, u32[]{:S(2)}) collective-permute-start(f32[2,1,130]{2,0,1:T(2,128)S(1)} %get-tuple-element.40), channel_id=1, source_target_pairs={{1,0},{3,2},{5,4},{7,6},{9,8},{11,10},{13,12},{15,14},{17,16},{19,... | collective-permute-start | bytes 3128 | tf_op jit(solution)/shard_map/ppermute | solution.py:19
  82.7 3.2 collective-permute-start.6
  84.0 10.3 %copy-start.18 = (f32[2,320,1]{2,0,1:T(2,128)S(1)}, f32[2,320,1]{2,0,1:T(2,128)}, u32[]{:S(2)}) copy-start(f32[2,320,1]{2,0,1:T(2,128)} %copy-done.17) | copy-start | bytes 7684
  84.4 9.9 %collective-permute-start.2 = (f32[2,320,1]{2,0,1:T(2,128)S(1)}, f32[2,320,1]{2,0,1:T(2,128)S(1)}, u32[]{:S(2)}, u32[]{:S(2)}) collective-permute-start(f32[2,320,1]{2,0,1:T(2,128)S(1)} %slice.465), channel_id=1, source_target_pairs={{0,2},{2,4},{4,6},{6,8},{8,10},{10,12},{12,14},{14,0},{1,3},{3,5},... | collective-permute-start | bytes 7688 | tf_op jit(solution)/shard_map/ppermute | solution.py:27
  84.6 9.8 %collective-permute-start.7 = (f32[2,1,130]{2,0,1:T(2,128)S(1)}, f32[2,1,130]{2,0,1:T(2,128)S(1)}, u32[]{:S(2)}, u32[]{:S(2)}) collective-permute-start(f32[2,1,130]{2,0,1:T(2,128)S(1)} %get-tuple-element.41), channel_id=1, source_target_pairs={{0,1},{2,3},{4,5},{6,7},{8,9},{10,11},{12,13},{14,15},{16,17},{18,... | collective-permute-start | bytes 3128 | tf_op jit(solution)/shard_map/ppermute | solution.py:16
  97.2 13.0 %collective-permute-start.8 = (f32[2,320,1]{2,0,1:T(2,128)S(1)}, f32[2,320,1]{2,0,1:T(2,128)S(1)}, u32[]{:S(2)}, u32[]{:S(2)}) collective-permute-start(f32[2,320,1]{2,0,1:T(2,128)S(1)} %get-tuple-element.59), channel_id=1, source_target_pairs={{2,0},{4,2},{6,4},{8,6},{10,8},{12,10},{14,12},{0,14},{3,1},{5,3},... | collective-permute-start | bytes 7688 | tf_op jit(solution)/shard_map/ppermute | solution.py:19
  97.3 12.9 %collective-permute-start.9 = (f32[2,320,1]{2,0,1:T(2,128)S(1)}, f32[2,320,1]{2,0,1:T(2,128)S(1)}, u32[]{:S(2)}, u32[]{:S(2)}) collective-permute-start(f32[2,320,1]{2,0,1:T(2,128)S(1)} %get-tuple-element.58), channel_id=1, source_target_pairs={{0,2},{2,4},{4,6},{6,8},{8,10},{10,12},{12,14},{14,0},{1,3},{3,5},... | collective-permute-start | bytes 7688 | tf_op jit(solution)/shard_map/ppermute | solution.py:16
  110.3 21.6 %collective-permute-start.10 = (f32[2,1,130]{2,0,1:T(2,128)S(1)}, f32[2,1,130]{2,0,1:T(2,128)S(1)}, u32[]{:S(2)}, u32[]{:S(2)}) collective-permute-start(f32[2,1,130]{2,0,1:T(2,128)S(1)} %get-tuple-element.38), channel_id=1, source_target_pairs={{1,0},{3,2},{5,4},{7,6},{9,8},{11,10},{13,12},{15,14},{17,16},{19,... | collective-permute-start | bytes 3128 | tf_op jit(solution)/shard_map/ppermute | solution.py:19
  130.6 2.1 collective-permute-start.11
  136.3 17.0 %collective-permute-start.12 = (f32[2,320,1]{2,0,1:T(2,128)S(1)}, f32[2,320,1]{2,0,1:T(2,128)S(1)}, u32[]{:S(2)}, u32[]{:S(2)}) collective-permute-start(f32[2,320,1]{2,0,1:T(2,128)S(1)} %get-tuple-element.57), channel_id=1, source_target_pairs={{2,0},{4,2},{6,4},{8,6},{10,8},{12,10},{14,12},{0,14},{3,1},{5,3},... | collective-permute-start | bytes 7688 | tf_op jit(solution)/shard_map/ppermute | solution.py:19
  137.3 16.0 %collective-permute-start.13 = (f32[2,320,1]{2,0,1:T(2,128)S(1)}, f32[2,320,1]{2,0,1:T(2,128)S(1)}, u32[]{:S(2)}, u32[]{:S(2)}) collective-permute-start(f32[2,320,1]{2,0,1:T(2,128)S(1)} %get-tuple-element.56), channel_id=1, source_target_pairs={{0,2},{2,4},{4,6},{6,8},{8,10},{10,12},{12,14},{14,0},{1,3},{3,5},... | collective-permute-start | bytes 7688 | tf_op jit(solution)/shard_map/ppermute | solution.py:16
  153.4 24.1 %collective-permute-start.14 = (f32[2,1,130]{2,0,1:T(2,128)S(1)}, f32[2,1,130]{2,0,1:T(2,128)S(1)}, u32[]{:S(2)}, u32[]{:S(2)}) collective-permute-start(f32[2,1,130]{2,0,1:T(2,128)S(1)} %get-tuple-element.36), channel_id=1, source_target_pairs={{1,0},{3,2},{5,4},{7,6},{9,8},{11,10},{13,12},{15,14},{17,16},{19,... | collective-permute-start | bytes 3128 | tf_op jit(solution)/shard_map/ppermute | solution.py:19
  176.2 2.1 collective-permute-start.15
  181.4 17.4 %copy-start.2 = (f32[2,320,128]{2,0,1:T(2,128)}, f32[2,320,128]{2,0,1:T(2,128)S(1)}, u32[]{:S(2)}) copy-start(f32[2,320,128]{2,0,1:T(2,128)S(1)} %fusion.55) | copy-start | bytes 983044
  181.8 17.0 %collective-permute-start.16 = (f32[2,320,1]{2,0,1:T(2,128)S(1)}, f32[2,320,1]{2,0,1:T(2,128)S(1)}, u32[]{:S(2)}, u32[]{:S(2)}) collective-permute-start(f32[2,320,1]{2,0,1:T(2,128)S(1)} %get-tuple-element.55), channel_id=1, source_target_pairs={{2,0},{4,2},{6,4},{8,6},{10,8},{12,10},{14,12},{0,14},{3,1},{5,3},... | collective-permute-start | bytes 7688 | tf_op jit(solution)/shard_map/ppermute | solution.py:19
  182.1 16.7 %collective-permute-start.17 = (f32[2,320,1]{2,0,1:T(2,128)S(1)}, f32[2,320,1]{2,0,1:T(2,128)S(1)}, u32[]{:S(2)}, u32[]{:S(2)}) collective-permute-start(f32[2,320,1]{2,0,1:T(2,128)S(1)} %get-tuple-element.54), channel_id=1, source_target_pairs={{0,2},{2,4},{4,6},{6,8},{8,10},{10,12},{12,14},{14,0},{1,3},{3,5},... | collective-permute-start | bytes 7688 | tf_op jit(solution)/shard_map/ppermute | solution.py:16
  199.6 23.2 %collective-permute-start.18 = (f32[2,1,130]{2,0,1:T(2,128)S(1)}, f32[2,1,130]{2,0,1:T(2,128)S(1)}, u32[]{:S(2)}, u32[]{:S(2)}) collective-permute-start(f32[2,1,130]{2,0,1:T(2,128)S(1)} %get-tuple-element.34), channel_id=1, source_target_pairs={{1,0},{3,2},{5,4},{7,6},{9,8},{11,10},{13,12},{15,14},{17,16},{19,... | collective-permute-start | bytes 3128 | tf_op jit(solution)/shard_map/ppermute | solution.py:19
  218.4 4.9 %slice-start.3 = ((f32[2,320,128]{2,0,1:T(2,128)}), f32[2,319,128]{2,0,1:T(2,128)S(1)}, s32[]{:S(2)}) async-start(f32[2,320,128]{2,0,1:T(2,128)} %copy-done.2), calls=%async_computation.3 | async-start | bytes 653312 | tf_op jit(solution)/shard_map/slice | solution.py:52
  221.2 2.1 collective-permute-start.19
  227.9 17.5 %copy-start.4 = (f32[2,320,128]{2,0,1:T(2,128)}, f32[2,320,128]{2,0,1:T(2,128)S(1)}, u32[]{:S(2)}) copy-start(f32[2,320,128]{2,0,1:T(2,128)S(1)} %fusion.45) | copy-start | bytes 983044
  228.4 17.0 %collective-permute-start.20 = (f32[2,320,1]{2,0,1:T(2,128)S(1)}, f32[2,320,1]{2,0,1:T(2,128)S(1)}, u32[]{:S(2)}, u32[]{:S(2)}) collective-permute-start(f32[2,320,1]{2,0,1:T(2,128)S(1)} %get-tuple-element.53), channel_id=1, source_target_pairs={{2,0},{4,2},{6,4},{8,6},{10,8},{12,10},{14,12},{0,14},{3,1},{5,3},... | collective-permute-start | bytes 7688 | tf_op jit(solution)/shard_map/ppermute | solution.py:19
  229.3 16.1 %collective-permute-start.21 = (f32[2,320,1]{2,0,1:T(2,128)S(1)}, f32[2,320,1]{2,0,1:T(2,128)S(1)}, u32[]{:S(2)}, u32[]{:S(2)}) collective-permute-start(f32[2,320,1]{2,0,1:T(2,128)S(1)} %get-tuple-element.52), channel_id=1, source_target_pairs={{0,2},{2,4},{4,6},{6,8},{8,10},{10,12},{12,14},{14,0},{1,3},{3,5},... | collective-permute-start | bytes 7688 | tf_op jit(solution)/shard_map/ppermute | solution.py:16
  245.5 23.5 %collective-permute-start.22 = (f32[2,1,130]{2,0,1:T(2,128)S(1)}, f32[2,1,130]{2,0,1:T(2,128)S(1)}, u32[]{:S(2)}, u32[]{:S(2)}) collective-permute-start(f32[2,1,130]{2,0,1:T(2,128)S(1)} %get-tuple-element.32), channel_id=1, source_target_pairs={{1,0},{3,2},{5,4},{7,6},{9,8},{11,10},{13,12},{15,14},{17,16},{19,... | collective-permute-start | bytes 3128 | tf_op jit(solution)/shard_map/ppermute | solution.py:19
  264.9 4.9 %slice-start.5 = ((f32[2,320,128]{2,0,1:T(2,128)}), f32[2,319,128]{2,0,1:T(2,128)S(1)}, s32[]{:S(2)}) async-start(f32[2,320,128]{2,0,1:T(2,128)} %copy-done.4), calls=%async_computation.5 | async-start | bytes 653312 | tf_op jit(solution)/shard_map/slice | solution.py:52
  267.7 2.1 collective-permute-start.23
  272.0 17.4 %copy-start.8 = (f32[2,320,128]{2,0,1:T(2,128)}, f32[2,320,128]{2,0,1:T(2,128)S(1)}, u32[]{:S(2)}) copy-start(f32[2,320,128]{2,0,1:T(2,128)S(1)} %fusion.34) | copy-start | bytes 983044
  272.4 17.0 %collective-permute-start.24 = (f32[2,320,1]{2,0,1:T(2,128)S(1)}, f32[2,320,1]{2,0,1:T(2,128)S(1)}, u32[]{:S(2)}, u32[]{:S(2)}) collective-permute-start(f32[2,320,1]{2,0,1:T(2,128)S(1)} %get-tuple-element.51), channel_id=1, source_target_pairs={{2,0},{4,2},{6,4},{8,6},{10,8},{12,10},{14,12},{0,14},{3,1},{5,3},... | collective-permute-start | bytes 7688 | tf_op jit(solution)/shard_map/ppermute | solution.py:19
  272.7 16.7 %collective-permute-start.25 = (f32[2,320,1]{2,0,1:T(2,128)S(1)}, f32[2,320,1]{2,0,1:T(2,128)S(1)}, u32[]{:S(2)}, u32[]{:S(2)}) collective-permute-start(f32[2,320,1]{2,0,1:T(2,128)S(1)} %get-tuple-element.50), channel_id=1, source_target_pairs={{0,2},{2,4},{4,6},{6,8},{8,10},{10,12},{12,14},{14,0},{1,3},{3,5},... | collective-permute-start | bytes 7688 | tf_op jit(solution)/shard_map/ppermute | solution.py:16
  289.5 23.0 %collective-permute-start.26 = (f32[2,1,130]{2,0,1:T(2,128)S(1)}, f32[2,1,130]{2,0,1:T(2,128)S(1)}, u32[]{:S(2)}, u32[]{:S(2)}) collective-permute-start(f32[2,1,130]{2,0,1:T(2,128)S(1)} %get-tuple-element.30), channel_id=1, source_target_pairs={{1,0},{3,2},{5,4},{7,6},{9,8},{11,10},{13,12},{15,14},{17,16},{19,... | collective-permute-start | bytes 3128 | tf_op jit(solution)/shard_map/ppermute | solution.py:19
  308.4 4.9 %slice-start.9 = ((f32[2,320,128]{2,0,1:T(2,128)}), f32[2,319,128]{2,0,1:T(2,128)S(1)}, s32[]{:S(2)}) async-start(f32[2,320,128]{2,0,1:T(2,128)} %copy-done.8), calls=%async_computation.9 | async-start | bytes 653312 | tf_op jit(solution)/shard_map/slice | solution.py:52
  311.2 2.1 collective-permute-start.27
  315.4 17.4 %copy-start.6 = (f32[2,320,128]{2,0,1:T(2,128)}, f32[2,320,128]{2,0,1:T(2,128)S(1)}, u32[]{:S(2)}) copy-start(f32[2,320,128]{2,0,1:T(2,128)S(1)} %fusion.24) | copy-start | bytes 983044
  315.9 17.0 %collective-permute-start.28 = (f32[2,320,1]{2,0,1:T(2,128)S(1)}, f32[2,320,1]{2,0,1:T(2,128)S(1)}, u32[]{:S(2)}, u32[]{:S(2)}) collective-permute-start(f32[2,320,1]{2,0,1:T(2,128)S(1)} %get-tuple-element.49), channel_id=1, source_target_pairs={{2,0},{4,2},{6,4},{8,6},{10,8},{12,10},{14,12},{0,14},{3,1},{5,3},... | collective-permute-start | bytes 7688 | tf_op jit(solution)/shard_map/ppermute | solution.py:19
  316.8 16.1 %collective-permute-start.29 = (f32[2,320,1]{2,0,1:T(2,128)S(1)}, f32[2,320,1]{2,0,1:T(2,128)S(1)}, u32[]{:S(2)}, u32[]{:S(2)}) collective-permute-start(f32[2,320,1]{2,0,1:T(2,128)S(1)} %get-tuple-element.48), channel_id=1, source_target_pairs={{0,2},{2,4},{4,6},{6,8},{8,10},{10,12},{12,14},{14,0},{1,3},{3,5},... | collective-permute-start | bytes 7688 | tf_op jit(solution)/shard_map/ppermute | solution.py:16
  333.0 23.5 %collective-permute-start.30 = (f32[2,1,130]{2,0,1:T(2,128)S(1)}, f32[2,1,130]{2,0,1:T(2,128)S(1)}, u32[]{:S(2)}, u32[]{:S(2)}) collective-permute-start(f32[2,1,130]{2,0,1:T(2,128)S(1)} %get-tuple-element.28), channel_id=1, source_target_pairs={{1,0},{3,2},{5,4},{7,6},{9,8},{11,10},{13,12},{15,14},{17,16},{19,... | collective-permute-start | bytes 3128 | tf_op jit(solution)/shard_map/ppermute | solution.py:19
  355.2 2.1 collective-permute-start.31
  359.9 17.0 %collective-permute-start.32 = (f32[2,320,1]{2,0,1:T(2,128)S(1)}, f32[2,320,1]{2,0,1:T(2,128)S(1)}, u32[]{:S(2)}, u32[]{:S(2)}) collective-permute-start(f32[2,320,1]{2,0,1:T(2,128)S(1)} %get-tuple-element.47), channel_id=1, source_target_pairs={{2,0},{4,2},{6,4},{8,6},{10,8},{12,10},{14,12},{0,14},{3,1},{5,3},... | collective-permute-start | bytes 7688 | tf_op jit(solution)/shard_map/ppermute | solution.py:19
  360.2 17.4 %collective-permute-start.33 = (f32[2,320,1]{2,0,1:T(2,128)S(1)}, f32[2,320,1]{2,0,1:T(2,128)S(1)}, u32[]{:S(2)}, u32[]{:S(2)}) collective-permute-start(f32[2,320,1]{2,0,1:T(2,128)S(1)} %get-tuple-element.46), channel_id=1, source_target_pairs={{0,2},{2,4},{4,6},{6,8},{8,10},{10,12},{12,14},{14,0},{1,3},{3,5},... | collective-permute-start | bytes 7688 | tf_op jit(solution)/shard_map/ppermute | solution.py:16
  378.5 22.1 %collective-permute-start.34 = (f32[2,1,130]{2,1,0:T(1,128)S(1)}, f32[2,1,130]{2,1,0:T(1,128)S(1)}, u32[]{:S(2)}, u32[]{:S(2)}) collective-permute-start(f32[2,1,130]{2,1,0:T(1,128)S(1)} %get-tuple-element.26), channel_id=1, source_target_pairs={{1,0},{3,2},{5,4},{7,6},{9,8},{11,10},{13,12},{15,14},{17,16},{19,... | collective-permute-start | bytes 3128 | tf_op jit(solution)/shard_map/ppermute | solution.py:19
  399.3 3.6 collective-permute-start.35
  402.9 32.3 %copy-start.15 = (f32[2,320,128]{2,1,0:T(8,128)S(1)}, f32[2,320,128]{2,1,0:T(8,128)}, u32[]{:S(2)}) copy-start(f32[2,320,128]{2,1,0:T(8,128)} %param.11) | copy-start | bytes 983044
  435.2 32.1 %copy-start.20 = (f32[2,320,128]{2,1,0:T(8,128)S(1)}, f32[2,320,128]{2,1,0:T(8,128)}, u32[]{:S(2)}) copy-start(f32[2,320,128]{2,1,0:T(8,128)} %param.10) | copy-start | bytes 983044
  435.9 32.3 %copy-start.16 = (f32[2,320,128]{2,1,0:T(8,128)}, f32[2,320,128]{2,1,0:T(8,128)S(1)}, u32[]{:S(2)}) copy-start(f32[2,320,128]{2,1,0:T(8,128)S(1)} %get-tuple-element.19) | copy-start | bytes 983044
  (21 other events, 52.8 us)
where the time goes:
time: 469 us; the launch traced here: 468 us
  blocking collectives  245 us (52%)
  waiting for transfers between devices  113 us (24%)
  starting transfers between devices  46.8 us (10%)
  local copies, waits for them, and re-layouts  31 us (7%)
  other arithmetic  29.1 us (6%)
    all_gather x8, blocking collectives, diffuse(): whole_row = lax.all_gather(field[:, -1, :], 'lon', axis=1, tiled=True)  141 us
    ppermute x16, waiting for transfers between devices, with_halo(): lax.ppermute(lax.slice_in_dim(block, 0, width, axis=dim), axis, backward)  99.9 us
    psum x1, blocking collectives, shards(): old_norm = lax.psum(jnp.sum(residual * residual), ('lon', 'lat'))  30.1 us
    psum x1, blocking collectives, shards(): new_norm = lax.psum(jnp.sum(new_residual * new_residual), ('lon', 'lat'))  30.1 us
    ppermute x16, starting transfers between devices, with_halo(): lax.ppermute(lax.slice_in_dim(block, block.shape[dim] - width, None, axis...  23.3 us
    all_gather x1, blocking collectives, shards(): lax.all_gather(ocean[:, -1, :], 'lon', axis=1, tiled=True)  21.8 us
    all_gather x1, blocking collectives, shards(): lax.all_gather(north_kappa[-1:, :], 'lon', axis=1, tiled=True)  21.7 us
    ppermute x16, starting transfers between devices, with_halo(): lax.ppermute(lax.slice_in_dim(block, 0, width, axis=dim), axis, backward)  14.7 us
  transfers between devices with their start and end apart: 36, of which 14 were waited for; matrix products, arithmetic and copies ran while one was open for 6% of the time, Pallas kernels for 0%

commit v1 on v0

v1 whole, which is shorter than its diff:
```python
import functools

import jax
import jax.numpy as jnp
from jax import lax
from jax.experimental import pallas as pl
from jax.experimental.pallas import tpu as pltpu
from jax.sharding import PartitionSpec as P

STEPS = 4
HALO = 2 * STEPS
LANES = 128
VMEM_LIMIT = 48 * 1024 * 1024
f32 = jnp.float32


def turn(value, shift, axis=1):
    shift = shift % value.shape[axis]
    return value if shift == 0 else pltpu.roll(value, shift, axis)


def lanes_of(shape):
    return lax.broadcasted_iota(jnp.int32, shape, 1)


def place(kind, level, half):
    return 8 * kind + 32 * half + 64 * level


def pack_kernel(lon_axis, lat_axis, d, sea, pw, ek, nk, strip, rows_out, pay1, pay2):
    rows = d.shape[1]
    groups = rows // 8
    half_groups = groups // 2
    even = lax.axis_index(lon_axis) % 2 == 0
    top = lax.axis_index(lat_axis) == 1

    def plane(index, row):
        at = pl.ds(row, 8)
        if index < 2:
            return d[index, at, :]
        if index < 4:
            return sea[index - 2, at, :].astype(f32)
        if index < 6:
            return pw[index - 4, at, :]
        return (ek, nk)[index - 6][at, :]

    for index in range(8):
        high = plane(index, rows - 8)
        strip[8 * index : 8 * index + 8, :] = high
        rows_out[8 * index : 8 * index + 8, :] = jnp.where(top, plane(index, 0), high)
    lane = lanes_of((8, LANES))
    for group in range(half_groups):
        east = jnp.zeros((8, LANES), f32)
        west = jnp.zeros((8, LANES), f32)
        for half in range(2):
            for kind in range(4):
                for level in range(2):
                    at = place(kind, level, half)
                    turned = turn(plane(2 * kind + level, 8 * (group + half * half_groups)), at + 8)
                    east = jnp.where((lane >= at) & (lane < at + 8), turned, east)
                    first = (at + 8) % LANES
                    west = jnp.where((lane >= first) & (lane < first + 8), turned, west)
        pay1[8 * group : 8 * group + 8, :] = jnp.where(even, east, west)
        pay2[8 * group : 8 * group + 8, :] = jnp.where(even, west, east)


def pack(d, sea, pw, ek, nk):
    rows = d.shape[1]
    full = pl.BlockSpec(memory_space=pltpu.VMEM)
    shapes = [(64, LANES), (64, LANES), (rows // 2, LANES), (rows // 2, LANES)]
    return pl.pallas_call(
        functools.partial(pack_kernel, "lon", "lat"),
        out_shape=[jax.ShapeDtypeStruct(s, f32) for s in shapes],
        in_specs=[full] * 5,
        out_specs=[full] * 4,
        compiler_params=pltpu.CompilerParams(vmem_limit_bytes=VMEM_LIMIT),
    )(d, sea, pw, ek, nk)


def image_kernel(
    offsets, lon_axis, lat_axis,
    d, sea, pw, ek, nk, res, gathered_pieces, halo1, halo2, rows_in, corner1, corner2, partner,
    image, stats,
    blocks, folds, face_fold, ocean, weight, field, other, east_c, west_c, north_c, centre,
):
    lon = lax.axis_index(lon_axis)
    lat = lax.axis_index(lat_axis)
    count = len(offsets)
    top = lat == 1
    even = lon % 2 == 0
    rows = d.shape[1]
    groups = rows // 8
    half_groups = groups // 2
    lane = lanes_of((8, LANES))
    zero = jnp.zeros((8, LANES), f32)

    slot = 0
    for piece in gathered_pieces:
        for inside in range(piece.shape[0] // 64):
            block = lax.bitwise_xor(lon, offsets[slot])
            blocks[pl.ds(pl.multiple_of(block * 64, 64), 64), :] = piece[64 * inside : 64 * inside + 64, :]
            slot += 1
    wide = lanes_of((count, LANES))

    def strip_row(index, row):
        return blocks[pl.ds(8 * index + row, count, stride=64), :]

    def strip_east(x):
        moved = turn(x, -1)
        return jnp.where(wide == LANES - 1, turn(moved, -1, 0), moved)

    def strip_west(x):
        moved = turn(x, 1)
        return jnp.where(wide == 0, turn(moved, 1, 0), moved)

    partner_block = partner[...] // LANES
    partner_lane = partner[...] % LANES

    def across(x):
        parts = []
        for first in range(0, count, 8):
            lanes_at = partner_lane[first : first + 8]
            block_at = partner_block[first : first + 8]
            total = jnp.zeros((8, LANES), f32)
            for block in range(count):
                source = jnp.broadcast_to(x[block : block + 1, :], (8, LANES))
                picked = jnp.take_along_axis(source, lanes_at, axis=1)
                total = jnp.where(block_at == block, picked, total)
            parts.append(total)
        return parts[0] if len(parts) == 1 else jnp.concatenate(parts, axis=0)

    @pl.when(top)
    def _():
        east_k = [strip_row(6, r) for r in range(HALO)]
        north_k = [strip_row(7, r) for r in range(HALO)]
        top_k = 0.5 * (north_k[-1] + across(north_k[-1]))
        for level in range(2):
            oc = [strip_row(2 + level, r) for r in range(HALO)]
            u = [strip_row(level, r) * oc[r] for r in range(HALO)]
            e = [east_k[r] * oc[r] * strip_east(oc[r]) for r in range(HALO)]
            w = [strip_west(x) for x in e]
            n = [north_k[r] * oc[r] * oc[r + 1] for r in range(HALO - 1)]
            n.append(top_k * oc[-1] * across(oc[-1]))
            face_fold[level] = n[-1]
            c = [None] + [1.0 - e[r] - w[r] - n[r] - n[r - 1] for r in range(1, HALO)]
            for t in range(HALO):
                if t == STEPS:
                    for r in range(t, HALO):
                        u[r] = strip_row(4 + level, r) * oc[r] * u[r]
                beyond = across(u[-1])
                folds[t, level] = beyond
                if t == HALO - 1:
                    break
                new = list(u)
                for r in range(t + 1, HALO):
                    north = u[r + 1] if r + 1 < HALO else beyond
                    new[r] = (
                        c[r] * u[r] + e[r] * strip_east(u[r]) + w[r] * strip_west(u[r]) + n[r] * north + n[r - 1] * u[r - 1]
                    )
                u = new

    right = (lane % 64) < 32

    def fold_rows(read):
        to_east = lax.rem(lon + 1, count)
        to_west = lax.rem(lon + count - 1, count)
        one = lanes_of((1, LANES))
        here0 = read(0, lon)
        here1 = turn(read(1, lon), 64)
        e0, w0 = read(0, to_east), read(0, to_west)
        e1, w1 = turn(read(1, to_east), 64), turn(read(1, to_west), 64)
        beside = jnp.where(one < 32, e0, jnp.where(one >= 96, w0, jnp.where(one >= 64, e1, w1)))
        return here0, here1, beside

    def east_of(x):
        a, b, s = (turn(v, -1) for v in x)
        return (
            jnp.where(lane == 127, s, a),
            jnp.where(lane == 63, s, b),
            jnp.where(lane == 127, a, jnp.where(lane == 63, b, s)),
        )

    def west_of(x):
        a, b, s = (turn(v, 1) for v in x)
        return (
            jnp.where(lane == 0, s, a),
            jnp.where(lane == 64, s, b),
            jnp.where(lane == 0, a, jnp.where(lane == 64, b, s)),
        )

    def at(group, shift=0):
        return slice(8 + 8 * group + shift, 16 + 8 * group + shift)

    def beside_slabs(from_east, from_west, half):
        out = []
        for kind in range(4):
            r = turn(from_east, -(place(kind, 0, half) + 8))
            w = turn(from_west, 120 - place(kind, 0, half))
            out.append(jnp.where(right, r, w))
        pair = out.pop()
        pair_turned = turn(pair, 64)
        low = (lane < 32) | (lane >= 96)
        out.append(jnp.where(low, pair, pair_turned))
        out.append(jnp.where(low, pair_turned, pair))
        near = (lane % 64 < 8) | (lane % 64 >= 56)
        out[1] = jnp.where(near, out[1], 0.0)
        return out

    def set_group(group, planes, side):
        ek_here, nk_here = planes[6], planes[7]
        d_s = (planes[0], turn(planes[1], 64), side[0])
        oc_s = (planes[2], turn(planes[3], 64), side[1])
        pw_s = (planes[4], turn(planes[5], 64), side[2])
        ek_s = (ek_here, turn(ek_here, 64), side[3])
        nk_s = (nk_here, turn(nk_here, 64), side[4])
        e = [k * o * oe for k, o, oe in zip(ek_s, oc_s, east_of(oc_s))]
        w = west_of(e)
        for s in range(3):
            ocean[s, at(group), :] = oc_s[s]
            field[s, at(group), :] = d_s[s] * oc_s[s]
            weight[s, at(group), :] = pw_s[s] * oc_s[s]
            east_c[s, at(group), :] = e[s]
            west_c[s, at(group), :] = w[s]
            north_c[s, at(group), :] = nk_s[s] * oc_s[s]

    last = groups + 2
    for s in range(3):
        for buffer in (ocean, field, other, north_c):
            buffer[s, 0:8, :] = zero
            buffer[s, 8 + 8 * last : 16 + 8 * last, :] = zero
    for group in range(groups):
        here = slice(8 * group, 8 * group + 8)
        half, inside = divmod(group, half_groups)
        there = slice(8 * inside, 8 * inside + 8)
        a, b = halo1[there, :], halo2[there, :]
        side = beside_slabs(jnp.where(even, a, b), jnp.where(even, b, a), half)
        planes = [d[0, here, :], d[1, here, :], sea[0, here, :].astype(f32), sea[1, here, :].astype(f32),
                  pw[0, here, :], pw[1, here, :], ek[here, :], nk[here, :]]
        set_group(group + 1, planes, side)
    planes = [rows_in[8 * i : 8 * i + 8, :] for i in range(8)]
    a, b = corner1[...], corner2[...]
    from_east, from_west = jnp.where(even, a, b), jnp.where(even, b, a)
    for group, half, used in ((0, 1, top), (groups + 1, 0, jnp.logical_not(top))):
        side = beside_slabs(from_east, from_west, half)
        masked = list(planes)
        masked[2] = jnp.where(used, planes[2], 0.0)
        masked[3] = jnp.where(used, planes[3], 0.0)
        side[1] = jnp.where(used, side[1], 0.0)
        set_group(group, masked, side)

    for group in range(groups + 2):
        for s in range(3):
            north_c[s, at(group), :] = north_c[s, at(group), :] * ocean[s, at(group, 1), :]
    fold_at = 8 + 8 * (groups + 1)

    @pl.when(top)
    def _():
        for s, row in enumerate(fold_rows(lambda level, b: face_fold[level, pl.ds(b, 1), :])):
            north_c[s, fold_at - 1 : fold_at, :] = row

    for group in range(groups + 2):
        for s in range(3):
            here = at(group)
            centre[s, here, :] = (
                1.0 - east_c[s, here, :] - west_c[s, here, :] - north_c[s, here, :] - north_c[s, at(group, -1), :]
            )

    def step(t, source, target):
        @pl.when(top)
        def _():
            for s, row in enumerate(fold_rows(lambda level, b: folds[t, level, pl.ds(b, 1), :])):
                source[s, fold_at : fold_at + 1, :] = row

        for group in range(groups + 2):
            here, up, down = at(group), at(group, 1), at(group, -1)
            u = [source[s, here, :] for s in range(3)]
            e, w = east_of(u), west_of(u)
            for s in range(3):
                target[s, here, :] = (
                    centre[s, here, :] * u[s]
                    + east_c[s, here, :] * e[s]
                    + west_c[s, here, :] * w[s]
                    + north_c[s, here, :] * source[s, up, :]
                    + north_c[s, down, :] * source[s, down, :]
                )

    def half_steps(first):
        def two(i, carry):
            step(first + 2 * i, field, other)
            step(first + 2 * i + 1, other, field)
            return carry

        lax.fori_loop(0, STEPS // 2, two, 0)

    half_steps(0)
    for group in range(groups + 2):
        for s in range(3):
            field[s, at(group), :] = field[s, at(group), :] * weight[s, at(group), :]
    half_steps(STEPS)

    rr = rq = dq = qq = zero
    for group in range(groups):
        here = slice(8 * group, 8 * group + 8)
        for level in range(2):
            u = turn(field[level, at(group + 1), :], 64 * level)
            o = sea[level, here, :].astype(f32)
            dv, rv = d[level, here, :], res[level, here, :]
            q = dv + o * u
            image[level, here, :] = q
            rr, rq, dq, qq = rr + rv * rv, rq + rv * q, dq + dv * q, qq + q * q
    rr, rq, dq, qq = (jnp.sum(x) for x in (rr, rq, dq, qq))
    a0 = jnp.where(qq > 0.0, rq / jnp.where(qq > 0.0, qq, 1.0), 0.0)
    ss = sq = zero
    for group in range(groups):
        here = slice(8 * group, 8 * group + 8)
        for level in range(2):
            q = image[level, here, :]
            s = res[level, here, :] - a0 * q
            ss, sq = ss + s * s, sq + s * q
    ss, sq = jnp.sum(ss), jnp.sum(sq)
    one = lanes_of((1, LANES))
    row = jnp.zeros((1, LANES), f32)
    for index, value in enumerate((rr, dq, ss, sq, qq, a0)):
        row = jnp.where(one == index, value, row)
    stats[...] = row


def image_and_stats(d, sea, pw, ek, nk, res, pieces, offsets, halo1, halo2, rows_in, corner1, corner2, partner):
    levels, rows, columns = d.shape
    count = len(offsets)
    full = pl.BlockSpec(memory_space=pltpu.VMEM)
    extended = (3, rows + 32, LANES)
    inputs = [d, sea, pw, ek, nk, res, *pieces, halo1, halo2, rows_in, corner1, corner2, partner]

    def kernel(*refs):
        head, tail = refs[:6], refs[6 + len(pieces) :]
        image_kernel(offsets, "lon", "lat", *head, refs[6 : 6 + len(pieces)], *tail)

    return pl.pallas_call(
        kernel,
        out_shape=[jax.ShapeDtypeStruct(d.shape, f32), jax.ShapeDtypeStruct((1, LANES), f32)],
        in_specs=[full] * len(inputs),
        out_specs=[full] * 2,
        scratch_shapes=[
            pltpu.VMEM((64 * count, LANES), f32),
            pltpu.VMEM((HALO, 2, count, LANES), f32),
            pltpu.VMEM((2, count, LANES), f32),
        ]
        + [pltpu.VMEM(extended, f32)] * 8,
        compiler_params=pltpu.CompilerParams(vmem_limit_bytes=VMEM_LIMIT),
    )(*inputs)


def swapped(value, axis, distance):
    return lax.ppermute(value, axis, [(i, i ^ distance) for i in range(lax.axis_size(axis))])


def odd_pairs(value, axis):
    count = lax.axis_size(axis)
    pairs = []
    for i in range(1, count, 2):
        pairs += [(i, (i + 1) % count), ((i + 1) % count, i)]
    return lax.ppermute(value, axis, pairs)


def distances(count):
    found = []
    while count > 1:
        count //= 2
        found.append(count)
    return found


def butterfly(value, axis, order):
    pieces, offsets = [value], [0]
    for distance in order:
        whole = pieces[0] if len(pieces) == 1 else jnp.concatenate(pieces, axis=0)
        pieces.append(swapped(whole, axis, distance))
        offsets += [o ^ distance for o in offsets]
    return pieces, offsets


def shards(iterate, residual, direction, land_sea, precision_weight, east_kappa, north_kappa, fold_partner):
    count = lax.axis_size("lon")
    rows = direction.shape[1]
    strip, edge_rows, pay1, pay2 = pack(direction, land_sea, precision_weight, east_kappa, north_kappa)
    halo2 = odd_pairs(pay2, "lon")
    halo1 = swapped(pay1, "lon", 1)
    rows_in = swapped(edge_rows, "lat", 1)
    pieces, offsets = butterfly(strip, "lon", distances(count))
    top = lax.axis_index("lat") == 1
    first = jnp.where(top, 0, rows // 2 - 8)
    edge = lambda halo: lax.dynamic_slice_in_dim(halo, first, 8, axis=0)
    corners = swapped(jnp.concatenate([edge(halo1), edge(halo2)], axis=0), "lat", 1)
    partner = fold_partner.reshape(count, LANES)
    image, stats = image_and_stats(
        direction, land_sea, precision_weight, east_kappa, north_kappa, residual,
        pieces, offsets, halo1, halo2, rows_in, corners[:8], corners[8:], partner,
    )
    both = jnp.concatenate([stats, swapped(stats, "lat", 1)], axis=0)
    parts, _ = butterfly(both, "lon", distances(count)[::-1])
    table = jnp.concatenate(parts, axis=0)
    rr, dq, ss, sq, qq, a0 = (table[:, i] for i in range(6))
    old_norm = jnp.sum(rr)
    alpha = old_norm / jnp.sum(dq)
    t = alpha - a0
    new_norm = jnp.sum(ss + t * (t * qq - 2.0 * sq))
    new_residual = residual - alpha * image
    return (
        iterate + alpha * direction,
        new_residual,
        new_residual + (new_norm / old_norm) * direction,
    )


def solution(mesh):
    field = P("member", "lat", "lon")
    level = P(None, "lat", "lon")
    flat = P("lat", "lon")
    return jax.shard_map(
        shards,
        mesh=mesh,
        in_specs=(field, field, field, level, level, flat, flat, P()),
        out_specs=(field, field, field),
        check_vma=False,
    )
```

time: 469 us -> 55.8 us (0.12)
  blocking collectives: 245 us -> 0 us
  waiting for transfers between devices: 113 us -> 23.2 us
  starting transfers between devices: 46.8 us -> 10.2 us
  other arithmetic: 29.1 us -> 2.56 us
  local copies, waits for them, and re-layouts: 31 us -> 4.8 us
  Pallas kernels: 0 us -> 11.3 us
    all_gather x10 -> x0, blocking collectives: 185 us -> none  [the longest x8 141 us: diffuse(): whole_row = lax.all_gather(field[:, -1, :], 'lon', axis=1, tiled=True)]
    ppermute x36 -> x11, waiting for transfers between devices: 113 us -> 23.2 us  [the longest x10 19.2 us: swapped(): lax.ppermute(value, axis, [(i, i ^ distance) for i in range(lax.axis_size...]
    psum x2 -> x0, blocking collectives: 60.2 us -> none  [the longest x1 30.1 us: shards(): old_norm = lax.psum(jnp.sum(residual * residual), ('lon', 'lat'))]
    ppermute x36 -> x11, starting transfers between devices: 46.8 us -> 10.2 us  [the longest x10 8.89 us: swapped(): lax.ppermute(value, axis, [(i, i ^ distance) for i in range(lax.axis_size...]
    gather x19 -> x0, local copies, waits for them, and re-layouts: 13.6 us -> none  [the longest x16 11.9 us: diffuse(): folded = jnp.take(whole_row, local_partner, axis=1)]
    sub x5 -> x0, other arithmetic: 12 us -> none  [diffuse(): field + east_face * (east - field) - west_face * (field - west)]
    pallas_call x0 -> x2, Pallas kernels: none -> 11.3 us  [the longest x1 10.9 us: image_and_stats(): pl.pallas_call(kernel, out_shape=[jax.ShapeDtypeStruct(d.shape, f32), jax...]
    all_gather x9 -> x0, local copies, waits for them, and re-layouts: 6.87 us -> none  [the longest x8 6.65 us: diffuse(): whole_row = lax.all_gather(field[:, -1, :], 'lon', axis=1, tiled=True)]
  transfers between devices with their start and end apart: 36 -> 11, of which waited for: 14 -> 8; matrix products, arithmetic and copies ran while one was open for 6% -> 0% of each run, Pallas kernels for 0% -> 0%
where the time goes in v1:
time: 55.8 us; the launch traced here: 55.5 us
  waiting for transfers between devices  23.2 us (42%)
  Pallas kernels  11.3 us (20%)
  starting transfers between devices  10.2 us (18%)
  local copies, waits for them, and re-layouts  4.8 us (9%)
  between operations  3.46 us (6%)
  other arithmetic  2.56 us (5%)
    ppermute x10, waiting for transfers between devices, swapped(): lax.ppermute(value, axis, [(i, i ^ distance) for i in range(lax.axis_size...  19.2 us
    pallas_call x1, Pallas kernels, image_and_stats(): pl.pallas_call(kernel, out_shape=[jax.ShapeDtypeStruct(d.shape, f32), jax...  10.9 us
    ppermute x10, starting transfers between devices, swapped(): lax.ppermute(value, axis, [(i, i ^ distance) for i in range(lax.axis_size...  8.89 us
    unnamed x26, local copies, waits for them, and re-layouts  4.78 us
    ppermute x1, waiting for transfers between devices, odd_pairs(): return lax.ppermute(value, axis, pairs)  4.07 us
    ppermute x1, starting transfers between devices, odd_pairs(): return lax.ppermute(value, axis, pairs)  1.29 us
  transfers between devices with their start and end apart: 11, of which 8 were waited for; matrix products, arithmetic and copies ran while one was open for 0% of the time, Pallas kernels for 0%

profile of v1, /device:TPU:0, one launch (start us, length us, event | category | flops | bytes accessed | tf_op | source)
XLA Modules:
  0.0 55.5 jit_solution(7076763798416069656)
XLA Ops:
  0.6 0.0 copy-start
  0.6 1.0 %copy-done = f32[2,320,128]{2,1,0:T(8,128)S(1)} copy-done((f32[2,320,128]{2,1,0:T(8,128)S(1)}, f32[2,320,128]{2,1,0:T(8,128)}, u32[]{:S(2)}) %copy-start) | copy-done | bytes 327704
  1.6 0.0 copy-start.2
  1.6 1.0 %copy-done.2 = s32[2,320,128]{2,1,0:T(8,128)S(1)} copy-done((s32[2,320,128]{2,1,0:T(8,128)S(1)}, s32[2,320,128]{2,1,0:T(8,128)}, u32[]{:S(2)}) %copy-start.2) | copy-done | bytes 327704
  2.6 0.0 copy-start.4
  2.6 1.0 %copy-done.4 = f32[2,320,128]{2,1,0:T(8,128)S(1)} copy-done((f32[2,320,128]{2,1,0:T(8,128)S(1)}, f32[2,320,128]{2,1,0:T(8,128)}, u32[]{:S(2)}) %copy-start.4) | copy-done | bytes 327704
  3.6 0.0 copy-start.7
  3.6 0.9 %copy-done.7 = f32[320,128]{1,0:T(8,128)S(1)} copy-done((f32[320,128]{1,0:T(8,128)S(1)}, f32[320,128]{1,0:T(8,128)}, u32[]{:S(2)}) %copy-start.7) | copy-done | bytes 163864
  4.5 0.9 %copy-done.9 = f32[320,128]{1,0:T(8,128)S(1)} copy-done((f32[320,128]{1,0:T(8,128)S(1)}, f32[320,128]{1,0:T(8,128)}, u32[]{:S(2)}) %copy-start.9) | copy-done | bytes 163864
  5.4 0.0 copy-start.10
  5.4 0.4 shard_map.103
  5.8 0.0 copy-start.1
  5.8 4.1 %collective-permute-start = (f32[64,128]{1,0:T(8,128)S(1)}, f32[64,128]{1,0:T(8,128)S(1)}, u32[]{:S(2)}, u32[]{:S(2)}) collective-permute-start(f32[64,128]{1,0:T(8,128)S(1)} %get-tuple-element.9.refs_6_), channel_id=1, source_target_pairs={{0,8},{2,10},{4,12},{6,14},{8,0},{10,2},{12,4},{14,6},{1,9},{3,11}... | collective-permute-start | bytes 98312 | tf_op jit(solution)/shard_map/ppermute | solution.py:355
  9.9 0.0 collective-permute-start.5
  9.9 1.5 %collective-permute-start.3 = (f32[160,128]{1,0:T(8,128)S(1)}, f32[160,128]{1,0:T(8,128)S(1)}, u32[]{:S(2)}, u32[]{:S(2)}) collective-permute-start(f32[160,128]{1,0:T(8,128)S(1)} %get-tuple-element.10), channel_id=1, source_target_pairs={{0,2},{2,0},{4,6},{6,4},{8,10},{10,8},{12,14},{14,12},{1,3},{3,1},... | collective-permute-start | bytes 245768 | tf_op jit(solution)/shard_map/ppermute | solution.py:355
  11.4 1.3 %collective-permute-start.4 = (f32[160,128]{1,0:T(8,128)S(1)}, f32[160,128]{1,0:T(8,128)S(1)}, u32[]{:S(2)}, u32[]{:S(2)}) collective-permute-start(f32[160,128]{1,0:T(8,128)S(1)} %get-tuple-element.11), channel_id=1, source_target_pairs={{2,4},{4,2},{6,8},{8,6},{10,12},{12,10},{14,0},{0,14},{3,5},{5,3},... | collective-permute-start | bytes 245768 | tf_op jit(solution)/shard_map/ppermute | solution.py:363
  12.7 0.0 collective-permute-done.refs_7_
  12.7 1.0 %collective-permute-start.1 = (f32[128,128]{1,0:T(8,128)S(1)}, f32[128,128]{1,0:T(8,128)S(1)}, u32[]{:S(2)}, u32[]{:S(2)}) collective-permute-start(f32[128,128]{1,0:T(8,128)S(1)} %pad_maximum_fusion.1), channel_id=1, source_target_pairs={{0,4},{2,6},{4,0},{6,2},{8,12},{10,14},{12,8},{14,10},{1,5},{3,7},... | collective-permute-start | bytes 196616 | tf_op jit(solution)/shard_map/ppermute | solution.py:355
  13.7 1.6 %collective-permute-done.3.refs_10_ = f32[160,128]{1,0:T(8,128)S(1)} collective-permute-done((f32[160,128]{1,0:T(8,128)S(1)}, f32[160,128]{1,0:T(8,128)S(1)}, u32[]{:S(2)}, u32[]{:S(2)}) %collective-permute-start.3) | collective-permute-done | bytes 81952 | tf_op jit(solution)/shard_map/ppermute | solution.py:355
  15.3 4.1 %collective-permute-done.4.refs_11_ = f32[160,128]{1,0:T(8,128)S(1)} collective-permute-done((f32[160,128]{1,0:T(8,128)S(1)}, f32[160,128]{1,0:T(8,128)S(1)}, u32[]{:S(2)}, u32[]{:S(2)}) %collective-permute-start.4) | collective-permute-done | bytes 81952 | tf_op jit(solution)/shard_map/ppermute | solution.py:363
  19.4 0.0 collective-permute-start.6
  19.4 0.0 collective-permute-done.1.refs_8_
  19.5 0.9 %collective-permute-start.2 = (f32[256,128]{1,0:T(8,128)S(1)}, f32[256,128]{1,0:T(8,128)S(1)}, u32[]{:S(2)}, u32[]{:S(2)}) collective-permute-start(f32[256,128]{1,0:T(8,128)S(1)} %pad_maximum_fusion), channel_id=1, source_target_pairs={{0,2},{2,0},{4,6},{6,4},{8,10},{10,8},{12,14},{14,12},{1,3},{3,1},... | collective-permute-start | bytes 393224 | tf_op jit(solution)/shard_map/ppermute | solution.py:355
  20.3 0.3 collective-permute-done.6
  20.6 0.0 collective-permute-done.5.refs_12_
  20.6 4.8 %collective-permute-done.2.refs_9_ = f32[256,128]{1,0:T(8,128)S(1)} collective-permute-done((f32[256,128]{1,0:T(8,128)S(1)}, f32[256,128]{1,0:T(8,128)S(1)}, u32[]{:S(2)}, u32[]{:S(2)}) %collective-permute-start.2) | collective-permute-done | bytes 131104 | tf_op jit(solution)/shard_map/ppermute | solution.py:355
  25.4 0.0 copy-done.3
  25.4 0.0 copy-done.5
  25.4 0.0 copy-done.6
  25.4 0.0 copy-done.8
  25.4 0.0 copy-done.10
  25.4 0.0 copy-done.1
  25.5 0.0 copy-done.11
  25.5 0.0 copy-start.12
  25.5 10.9 %shard_map.104 = (f32[2,320,128]{2,1,0:T(8,128)S(1)}, f32[1,128]{1,0:T(1,128)S(1)}) custom-call(f32[2,320,128]{2,1,0:T(8,128)S(1)} %copy-done.1, s32[2,320,128]{2,1,0:T(8,128)S(1)} %copy-done.3, f32[2,320,128]{2,1,0:T(8,128)S(1)} %copy-done.5, f32[320,128]{1,0:T(8,128)S(1)} %copy-done.8, f32[320,128]{1,0:T(8,128)S(1)} %copy-done.10, ...), custom_call_target="tpu_custom_call" | custom-call | tf_op jit(solution)/shard_map/pallas_call | solution.py:339
  36.4 1.3 %collective-permute-start.7 = (f32[1,128]{1,0:T(1,128)S(1)}, f32[1,128]{1,0:T(1,128)S(1)}, u32[]{:S(2)}, u32[]{:S(2)}) collective-permute-start(f32[1,128]{1,0:T(1,128)S(1)} %get-tuple-element.13), channel_id=1, source_target_pairs={{0,1},{1,0},{2,3},{3,2},{4,5},{5,4},{6,7},{7,6},{8,9},{9,8},{10,11... | collective-permute-start | bytes 1544 | tf_op jit(solution)/shard_map/ppermute | solution.py:355
  37.6 0.8 %collective-permute-done.7 = f32[1,128]{1,0:T(1,128)S(1)} collective-permute-done((f32[1,128]{1,0:T(1,128)S(1)}, f32[1,128]{1,0:T(1,128)S(1)}, u32[]{:S(2)}, u32[]{:S(2)}) %collective-permute-start.7) | collective-permute-done | bytes 544 | tf_op jit(solution)/shard_map/ppermute | solution.py:355
  38.5 0.0 collective-permute-start.8
  38.5 3.6 %collective-permute-done.8 = f32[2,128]{1,0:T(2,128)S(1)} collective-permute-done((f32[2,128]{1,0:T(2,128)S(1)}, f32[2,128]{1,0:T(2,128)S(1)}, u32[]{:S(2)}, u32[]{:S(2)}) %collective-permute-start.8) | collective-permute-done | bytes 1056 | tf_op jit(solution)/shard_map/ppermute | solution.py:355
  42.0 0.1 collective-permute-start.9
  42.1 3.6 %collective-permute-done.9 = f32[4,128]{1,0:T(4,128)S(1)} collective-permute-done((f32[4,128]{1,0:T(4,128)S(1)}, f32[4,128]{1,0:T(4,128)S(1)}, u32[]{:S(2)}, u32[]{:S(2)}) %collective-permute-start.9) | collective-permute-done | bytes 2080 | tf_op jit(solution)/shard_map/ppermute | solution.py:355
  45.7 0.1 collective-permute-start.10
  45.8 4.5 %collective-permute-done.10 = f32[8,128]{1,0:T(8,128)S(1)} collective-permute-done((f32[8,128]{1,0:T(8,128)S(1)}, f32[8,128]{1,0:T(8,128)S(1)}, u32[]{:S(2)}, u32[]{:S(2)}) %collective-permute-start.10) | collective-permute-done | bytes 4128 | tf_op jit(solution)/shard_map/ppermute | solution.py:355
  50.3 0.7 %slice_reduce_fusion.2 = (f32[]{:T(128)}, f32[]{:T(128)}) fusion(f32[16,128]{1,0:T(8,128)S(1)} %concatenate.30), kind=kLoop, calls=%fused_computation.11 | loop fusion | flops 30 | bytes 136 | tf_op jit(solution)/shard_map/reduce_sum | solution.py:405
  52.3 0.2 slice_reduce_fusion
  52.5 0.6 %add_reduce_fusion = f32[]{:T(128)} fusion(f32[16]{0:T(128)S(1)} %get-tuple-element.18, f32[16]{0:T(128)S(1)} %get-tuple-element.17, f32[16]{0:T(128)S(1)} %get-tuple-element.16, f32[16]{0:T(128)S(1)} %get-tuple-element.15), kind=kLoop, calls=%fused_computation.17 | loop fusion | flops 79 | bytes 260 | tf_op jit(solution)/shard_map/reduce_sum | solution.py:407
  54.5 0.0 copy-done.12
  54.5 1.0 %multiply_add_fusion = (f32[2,320,128]{2,1,0:T(8,128)}, f32[2,320,128]{2,1,0:T(8,128)}, f32[2,320,128]{2,1,0:T(8,128)}) fusion(f32[2,320,128]{2,1,0:T(8,128)S(1)} %copy-done.1, f32[]{:T(128)S(6)} %div.7, f32[2,320,128]{2,1,0:T(8,128)S(1)} %copy-done.6, f32[2,320,128]{2,1,0:T(8,128)S(1)} %get-tuple-element.14, f32[]{:T(128)S(6)} %div.6, ...), kind=kLoop, calls=%fused_computation | loop fusion | flops 491520 | bytes 2293768 | tf_op jit(solution)/shard_map/add | solution.py:412
  (16 shorter events, 0.1 us)
Async XLA Ops:
  0.6 1.0 %copy-start = (f32[2,320,128]{2,1,0:T(8,128)S(1)}, f32[2,320,128]{2,1,0:T(8,128)}, u32[]{:S(2)}) copy-start(f32[2,320,128]{2,1,0:T(8,128)} %refs_0_.1) | copy-start | bytes 983044
  1.6 1.0 %copy-start.2 = (s32[2,320,128]{2,1,0:T(8,128)S(1)}, s32[2,320,128]{2,1,0:T(8,128)}, u32[]{:S(2)}) copy-start(s32[2,320,128]{2,1,0:T(8,128)} %refs_1_.1) | copy-start | bytes 983044
  2.6 1.0 %copy-start.4 = (f32[2,320,128]{2,1,0:T(8,128)S(1)}, f32[2,320,128]{2,1,0:T(8,128)}, u32[]{:S(2)}) copy-start(f32[2,320,128]{2,1,0:T(8,128)} %refs_2_.1) | copy-start | bytes 983044
  3.6 0.9 %copy-start.7 = (f32[320,128]{1,0:T(8,128)S(1)}, f32[320,128]{1,0:T(8,128)}, u32[]{:S(2)}) copy-start(f32[320,128]{1,0:T(8,128)} %refs_3_.1) | copy-start | bytes 491524
  4.5 0.9 %copy-start.9 = (f32[320,128]{1,0:T(8,128)S(1)}, f32[320,128]{1,0:T(8,128)}, u32[]{:S(2)}) copy-start(f32[320,128]{1,0:T(8,128)} %refs_4_.1) | copy-start | bytes 491524
  5.4 20.0 %copy-start.3 = (s32[2,320,128]{2,1,0:T(8,128)S(1)}, s32[2,320,128]{2,1,0:T(8,128)}, u32[]{:S(2)}) copy-start(s32[2,320,128]{2,1,0:T(8,128)} %refs_1_.1) | copy-start | bytes 983044
  5.4 20.0 %copy-start.5 = (f32[2,320,128]{2,1,0:T(8,128)S(1)}, f32[2,320,128]{2,1,0:T(8,128)}, u32[]{:S(2)}) copy-start(f32[2,320,128]{2,1,0:T(8,128)} %refs_2_.1) | copy-start | bytes 983044
  5.4 20.0 %copy-start.6 = (f32[2,320,128]{2,1,0:T(8,128)S(1)}, f32[2,320,128]{2,1,0:T(8,128)}, u32[]{:S(2)}) copy-start(f32[2,320,128]{2,1,0:T(8,128)} %refs_5_.1) | copy-start | bytes 983044
  5.4 20.0 %copy-start.8 = (f32[320,128]{1,0:T(8,128)S(1)}, f32[320,128]{1,0:T(8,128)}, u32[]{:S(2)}) copy-start(f32[320,128]{1,0:T(8,128)} %refs_3_.1) | copy-start | bytes 491524
  5.4 20.0 %copy-start.10 = (f32[320,128]{1,0:T(8,128)S(1)}, f32[320,128]{1,0:T(8,128)}, u32[]{:S(2)}) copy-start(f32[320,128]{1,0:T(8,128)} %refs_4_.1) | copy-start | bytes 491524
  5.8 19.7 %copy-start.1 = (f32[2,320,128]{2,1,0:T(8,128)S(1)}, f32[2,320,128]{2,1,0:T(8,128)}, u32[]{:S(2)}) copy-start(f32[2,320,128]{2,1,0:T(8,128)} %refs_0_.1) | copy-start | bytes 983044
  5.8 6.9 %collective-permute-start = (f32[64,128]{1,0:T(8,128)S(1)}, f32[64,128]{1,0:T(8,128)S(1)}, u32[]{:S(2)}, u32[]{:S(2)}) collective-permute-start(f32[64,128]{1,0:T(8,128)S(1)} %get-tuple-element.9.refs_6_), channel_id=1, source_target_pairs={{0,8},{2,10},{4,12},{6,14},{8,0},{10,2},{12,4},{14,6},{1,9},{3,11}... | collective-permute-start | bytes 98312 | tf_op jit(solution)/shard_map/ppermute | solution.py:355
  9.9 10.7 %collective-permute-start.5 = (f32[64,128]{1,0:T(8,128)S(1)}, f32[64,128]{1,0:T(8,128)S(1)}, u32[]{:S(2)}, u32[]{:S(2)}) collective-permute-start(f32[64,128]{1,0:T(8,128)S(1)} %get-tuple-element.12), channel_id=1, source_target_pairs={{0,1},{1,0},{2,3},{3,2},{4,5},{5,4},{6,7},{7,6},{8,9},{9,8},{10,11... | collective-permute-start | bytes 98312 | tf_op jit(solution)/shard_map/ppermute | solution.py:355
  9.9 5.4 %collective-permute-start.3 = (f32[160,128]{1,0:T(8,128)S(1)}, f32[160,128]{1,0:T(8,128)S(1)}, u32[]{:S(2)}, u32[]{:S(2)}) collective-permute-start(f32[160,128]{1,0:T(8,128)S(1)} %get-tuple-element.10), channel_id=1, source_target_pairs={{0,2},{2,0},{4,6},{6,4},{8,10},{10,8},{12,14},{14,12},{1,3},{3,1},... | collective-permute-start | bytes 245768 | tf_op jit(solution)/shard_map/ppermute | solution.py:355
  11.4 8.0 %collective-permute-start.4 = (f32[160,128]{1,0:T(8,128)S(1)}, f32[160,128]{1,0:T(8,128)S(1)}, u32[]{:S(2)}, u32[]{:S(2)}) collective-permute-start(f32[160,128]{1,0:T(8,128)S(1)} %get-tuple-element.11), channel_id=1, source_target_pairs={{2,4},{4,2},{6,8},{8,6},{10,12},{12,10},{14,0},{0,14},{3,5},{5,3},... | collective-permute-start | bytes 245768 | tf_op jit(solution)/shard_map/ppermute | solution.py:363
  12.7 6.7 %collective-permute-start.1 = (f32[128,128]{1,0:T(8,128)S(1)}, f32[128,128]{1,0:T(8,128)S(1)}, u32[]{:S(2)}, u32[]{:S(2)}) collective-permute-start(f32[128,128]{1,0:T(8,128)S(1)} %pad_maximum_fusion.1), channel_id=1, source_target_pairs={{0,4},{2,6},{4,0},{6,2},{8,12},{10,14},{12,8},{14,10},{1,5},{3,7},... | collective-permute-start | bytes 196616 | tf_op jit(solution)/shard_map/ppermute | solution.py:355
  19.4 1.2 %collective-permute-start.6 = (f32[16,128]{1,0:T(8,128)S(1)}, f32[16,128]{1,0:T(8,128)S(1)}, u32[]{:S(2)}, u32[]{:S(2)}) collective-permute-start(f32[16,128]{1,0:T(8,128)S(1)} %pad_maximum_fusion.2), channel_id=1, source_target_pairs={{0,1},{1,0},{2,3},{3,2},{4,5},{5,4},{6,7},{7,6},{8,9},{9,8},{10,11... | collective-permute-start | bytes 24584 | tf_op jit(solution)/shard_map/ppermute | solution.py:355
  19.5 6.0 %collective-permute-start.2 = (f32[256,128]{1,0:T(8,128)S(1)}, f32[256,128]{1,0:T(8,128)S(1)}, u32[]{:S(2)}, u32[]{:S(2)}) collective-permute-start(f32[256,128]{1,0:T(8,128)S(1)} %pad_maximum_fusion), channel_id=1, source_target_pairs={{0,2},{2,0},{4,6},{6,4},{8,10},{10,8},{12,14},{14,12},{1,3},{3,1},... | collective-permute-start | bytes 393224 | tf_op jit(solution)/shard_map/ppermute | solution.py:355
  20.6 4.9 %copy-start.11 = (s32[1024]{0:T(1024)S(1)}, s32[1024]{0:T(1024)}, u32[]{:S(2)}) copy-start(s32[1024]{0:T(1024)} %param.15) | copy-start | bytes 12292
  25.5 29.0 %copy-start.12 = (f32[2,320,128]{2,1,0:T(8,128)S(1)}, f32[2,320,128]{2,1,0:T(8,128)}, u32[]{:S(2)}) copy-start(f32[2,320,128]{2,1,0:T(8,128)} %param.8) | copy-start | bytes 983044
  36.4 2.1 %collective-permute-start.7 = (f32[1,128]{1,0:T(1,128)S(1)}, f32[1,128]{1,0:T(1,128)S(1)}, u32[]{:S(2)}, u32[]{:S(2)}) collective-permute-start(f32[1,128]{1,0:T(1,128)S(1)} %get-tuple-element.13), channel_id=1, source_target_pairs={{0,1},{1,0},{2,3},{3,2},{4,5},{5,4},{6,7},{7,6},{8,9},{9,8},{10,11... | collective-permute-start | bytes 1544 | tf_op jit(solution)/shard_map/ppermute | solution.py:355
  38.5 3.6 %collective-permute-start.8 = (f32[2,128]{1,0:T(2,128)S(1)}, f32[2,128]{1,0:T(2,128)S(1)}, u32[]{:S(2)}, u32[]{:S(2)}) collective-permute-start(f32[2,128]{1,0:T(2,128)S(1)} %pad_maximum_fusion.5), channel_id=1, source_target_pairs={{0,2},{2,0},{4,6},{6,4},{8,10},{10,8},{12,14},{14,12},{1,3},{3,1},... | collective-permute-start | bytes 3080 | tf_op jit(solution)/shard_map/ppermute | solution.py:355
  42.0 3.7 %collective-permute-start.9 = (f32[4,128]{1,0:T(4,128)S(1)}, f32[4,128]{1,0:T(4,128)S(1)}, u32[]{:S(2)}, u32[]{:S(2)}) collective-permute-start(f32[4,128]{1,0:T(4,128)S(1)} %pad_maximum_fusion.4), channel_id=1, source_target_pairs={{0,4},{2,6},{4,0},{6,2},{8,12},{10,14},{12,8},{14,10},{1,5},{3,7},... | collective-permute-start | bytes 6152 | tf_op jit(solution)/shard_map/ppermute | solution.py:355
  45.7 4.6 %collective-permute-start.10 = (f32[8,128]{1,0:T(8,128)S(1)}, f32[8,128]{1,0:T(8,128)S(1)}, u32[]{:S(2)}, u32[]{:S(2)}) collective-permute-start(f32[8,128]{1,0:T(8,128)S(1)} %pad_maximum_fusion.3), channel_id=1, source_target_pairs={{0,8},{2,10},{4,12},{6,14},{8,0},{10,2},{12,4},{14,6},{1,9},{3,11}... | collective-permute-start | bytes 12296 | tf_op jit(solution)/shard_map/ppermute | solution.py:355

commit v2 on v1

--- a/solution.py
+++ b/solution.py
@@ -27,7 +27,16 @@
     return 8 * kind + 32 * half + 64 * level
 
 
-def pack_kernel(lon_axis, lat_axis, d, sea, pw, ek, nk, strip, rows_out, pay1, pay2):
+def pack_kernel(
+    lon_axis, lat_axis,
+    d_hbm, sea_hbm, pw_hbm, ek_hbm, nk_hbm, strip, rows_out, pay1, pay2, d, sea, pw, ek, nk, arrived,
+):
+    sources, targets = (d_hbm, sea_hbm, pw_hbm, ek_hbm, nk_hbm), (d, sea, pw, ek, nk)
+    copies = [pltpu.make_async_copy(a, b, arrived.at[i]) for i, (a, b) in enumerate(zip(sources, targets))]
+    for copy in copies:
+        copy.start()
+    for copy in copies:
+        copy.wait()
     rows = d.shape[1]
     groups = rows // 8
     half_groups = groups // 2
@@ -68,13 +77,15 @@
     rows = d.shape[1]
     full = pl.BlockSpec(memory_space=pltpu.VMEM)
     shapes = [(64, LANES), (64, LANES), (rows // 2, LANES), (rows // 2, LANES)]
+    inputs = [pltpu.with_memory_space_constraint(x, pltpu.HBM) for x in (d, sea, pw, ek, nk)]
     return pl.pallas_call(
         functools.partial(pack_kernel, "lon", "lat"),
         out_shape=[jax.ShapeDtypeStruct(s, f32) for s in shapes],
-        in_specs=[full] * 5,
+        in_specs=[pl.BlockSpec(memory_space=pltpu.HBM)] * 5,
         out_specs=[full] * 4,
+        scratch_shapes=[pltpu.VMEM(x.shape, x.dtype) for x in inputs] + [pltpu.SemaphoreType.DMA((5,))],
         compiler_params=pltpu.CompilerParams(vmem_limit_bytes=VMEM_LIMIT),
-    )(d, sea, pw, ek, nk)
+    )(*inputs)
 
 
 def image_kernel(
@@ -105,16 +116,14 @@
     def strip_row(index, row):
         return blocks[pl.ds(8 * index + row, count, stride=64), :]
 
-    def strip_east(x):
-        moved = turn(x, -1)
-        return jnp.where(wide == LANES - 1, turn(moved, -1, 0), moved)
-
-    def strip_west(x):
-        moved = turn(x, 1)
-        return jnp.where(wide == 0, turn(moved, 1, 0), moved)
-
-    partner_block = partner[...] // LANES
-    partner_lane = partner[...] % LANES
+    def strip_shift(values, to_east):
+        step, edge = (-1, LANES - 1) if to_east else (1, 0)
+        moved = [turn(x, step) for x in values]
+        beside = [turn(x, step, 0) for x in moved]
+        return [jnp.where(wide == edge, y, x) for x, y in zip(moved, beside)]
+
+    partner_block = partner[...] >> 7
+    partner_lane = partner[...] & (LANES - 1)
 
     def across(x):
         parts = []
@@ -134,32 +143,49 @@
         east_k = [strip_row(6, r) for r in range(HALO)]
         north_k = [strip_row(7, r) for r in range(HALO)]
         top_k = 0.5 * (north_k[-1] + across(north_k[-1]))
-        for level in range(2):
-            oc = [strip_row(2 + level, r) for r in range(HALO)]
-            u = [strip_row(level, r) * oc[r] for r in range(HALO)]
-            e = [east_k[r] * oc[r] * strip_east(oc[r]) for r in range(HALO)]
-            w = [strip_west(x) for x in e]
-            n = [north_k[r] * oc[r] * oc[r + 1] for r in range(HALO - 1)]
-            n.append(top_k * oc[-1] * across(oc[-1]))
-            face_fold[level] = n[-1]
-            c = [None] + [1.0 - e[r] - w[r] - n[r] - n[r - 1] for r in range(1, HALO)]
-            for t in range(HALO):
-                if t == STEPS:
+        both = range(2)
+        oc = [[strip_row(2 + level, r) for r in range(HALO)] for level in both]
+        u = [[strip_row(level, r) * oc[level][r] for r in range(HALO)] for level in both]
+        oc_east = strip_shift([x for level in both for x in oc[level]], True)
+        e = [[east_k[r] * oc[level][r] * oc_east[HALO * level + r] for r in range(HALO)] for level in both]
+        w = strip_shift([x for level in both for x in e[level]], False)
+        w = [w[:HALO], w[HALO:]]
+        n = [[north_k[r] * oc[level][r] * oc[level][r + 1] for r in range(HALO - 1)] for level in both]
+        for level in both:
+            n[level].append(top_k * oc[level][-1] * across(oc[level][-1]))
+            face_fold[level] = n[level][-1]
+        c = [
+            [None] + [1.0 - e[level][r] - w[level][r] - n[level][r] - n[level][r - 1] for r in range(1, HALO)]
+            for level in both
+        ]
+        for t in range(HALO):
+            if t == STEPS:
+                for level in both:
                     for r in range(t, HALO):
-                        u[r] = strip_row(4 + level, r) * oc[r] * u[r]
-                beyond = across(u[-1])
-                folds[t, level] = beyond
-                if t == HALO - 1:
-                    break
-                new = list(u)
-                for r in range(t + 1, HALO):
-                    north = u[r + 1] if r + 1 < HALO else beyond
-                    new[r] = (
-                        c[r] * u[r] + e[r] * strip_east(u[r]) + w[r] * strip_west(u[r]) + n[r] * north + n[r - 1] * u[r - 1]
-                    )
-                u = new
-
-    right = (lane % 64) < 32
+                        u[level][r] = strip_row(4 + level, r) * oc[level][r] * u[level][r]
+            beyond = [across(u[level][-1]) for level in both]
+            for level in both:
+                folds[t, level] = beyond[level]
+            if t == HALO - 1:
+                break
+            rest = [(level, r) for level in both for r in range(t + 1, HALO)]
+            east = strip_shift([u[level][r] for level, r in rest], True)
+            west = strip_shift([u[level][r] for level, r in rest], False)
+            new = [list(u[0]), list(u[1])]
+            for (level, r), ue, uw in zip(rest, east, west):
+                north = u[level][r + 1] if r + 1 < HALO else beyond[level]
+                new[level][r] = (
+                    c[level][r] * u[level][r]
+                    + e[level][r] * ue
+                    + w[level][r] * uw
+                    + n[level][r] * north
+                    + n[level][r - 1] * u[level][r - 1]
+                )
+            u = new
+
+    right = (lane & 63) < 32
+    low = (lane < 32) | (lane >= 96)
+    near = ((lane & 63) < 8) | ((lane & 63) >= 56)
 
     def fold_rows(read):
         to_east = lax.rem(lon + 1, count)
@@ -193,16 +219,12 @@
 
     def beside_slabs(from_east, from_west, half):
         out = []
-        for kind in range(4):
-            r = turn(from_east, -(place(kind, 0, half) + 8))
-            w = turn(from_west, 120 - place(kind, 0, half))
+        for kind, extra in ((0, 0), (1, 0), (2, 0), (3, 0), (3, 64)):
+            r = turn(from_east, extra - (place(kind, 0, half) + 8))
+            w = turn(from_west, extra + 120 - place(kind, 0, half))
             out.append(jnp.where(right, r, w))
-        pair = out.pop()
-        pair_turned = turn(pair, 64)
-        low = (lane < 32) | (lane >= 96)
-        out.append(jnp.where(low, pair, pair_turned))
-        out.append(jnp.where(low, pair_turned, pair))
-        near = (lane % 64 < 8) | (lane % 64 >= 56)
+        pair, pair_turned = out[3:]
+        out[3:] = [jnp.where(low, pair, pair_turned), jnp.where(low, pair_turned, pair)]
         out[1] = jnp.where(near, out[1], 0.0)
         return out
 
@@ -213,14 +235,11 @@
         pw_s = (planes[4], turn(planes[5], 64), side[2])
         ek_s = (ek_here, turn(ek_here, 64), side[3])
         nk_s = (nk_here, turn(nk_here, 64), side[4])
-        e = [k * o * oe for k, o, oe in zip(ek_s, oc_s, east_of(oc_s))]
-        w = west_of(e)
         for s in range(3):
             ocean[s, at(group), :] = oc_s[s]
             field[s, at(group), :] = d_s[s] * oc_s[s]
             weight[s, at(group), :] = pw_s[s] * oc_s[s]
-            east_c[s, at(group), :] = e[s]
-            west_c[s, at(group), :] = w[s]
+            east_c[s, at(group), :] = ek_s[s] * oc_s[s]
             north_c[s, at(group), :] = nk_s[s] * oc_s[s]
 
     last = groups + 2
@@ -248,10 +267,16 @@
         side[1] = jnp.where(used, side[1], 0.0)
         set_group(group, masked, side)
 
+    fold_at = 8 + 8 * (groups + 1)
     for group in range(groups + 2):
+        here = at(group)
+        oc = [ocean[s, here, :] for s in range(3)]
+        half_face = [east_c[s, here, :] for s in range(3)]
+        e, w = east_of(oc), west_of(half_face)
         for s in range(3):
-            north_c[s, at(group), :] = north_c[s, at(group), :] * ocean[s, at(group, 1), :]
-    fold_at = 8 + 8 * (groups + 1)
+            east_c[s, here, :] = half_face[s] * e[s]
+            west_c[s, here, :] = oc[s] * w[s]
+            north_c[s, here, :] = north_c[s, here, :] * ocean[s, at(group, 1), :]
 
     @pl.when(top)
     def _():
@@ -351,6 +376,55 @@
     )(*inputs)
 
 
+def update_kernel(count, *refs):
+    parts = refs[:count]
+    iterate, res, d, image, iterate_hbm, res_hbm, d_hbm, new_iterate, new_res, new_d, sent = refs[count:]
+    table = jnp.concatenate([part[...] for part in parts], axis=0)
+    lane = lanes_of(table.shape)
+    sums = jnp.sum(table, axis=0, keepdims=True)
+    one = lanes_of(sums.shape)
+    pick = lambda row, index: jnp.sum(jnp.where(one == index, row, 0.0), axis=1, keepdims=True)
+    old_norm = pick(sums, 0)
+    alpha = old_norm / pick(sums, 1)
+    t = alpha - turn(table, -3)
+    norms = table + t * (t * turn(table, -2) - 2.0 * turn(table, -1))
+    new_norm = pick(jnp.sum(norms, axis=0, keepdims=True), 2)
+    beta = new_norm / old_norm
+    rows = d.shape[1]
+    pieces = 2
+    alpha = jnp.broadcast_to(alpha, (8, LANES))
+    beta = jnp.broadcast_to(beta, (8, LANES))
+    copies = []
+    for level in range(2):
+        for piece in range(pieces):
+            first, size = piece * (rows // pieces), rows // pieces
+            for row in range(first, first + size, 8):
+                here = slice(row, row + 8)
+                dv = d[level, here, :]
+                rv = res[level, here, :] - alpha * image[level, here, :]
+                new_iterate[level, here, :] = iterate[level, here, :] + alpha * dv
+                new_res[level, here, :] = rv
+                new_d[level, here, :] = rv + beta * dv
+            for index, (a, b) in enumerate(((new_iterate, iterate_hbm), (new_res, res_hbm), (new_d, d_hbm))):
+                part = (level, pl.ds(first, size), slice(None))
+                copies.append(pltpu.make_async_copy(a.at[part], b.at[part], sent.at[len(copies)]))
+                copies[-1].start()
+    for copy in copies:
+        copy.wait()
+
+
+def update(parts, iterate, res, d, image):
+    full = pl.BlockSpec(memory_space=pltpu.VMEM)
+    return pl.pallas_call(
+        functools.partial(update_kernel, len(parts)),
+        out_shape=[jax.ShapeDtypeStruct(d.shape, f32)] * 3,
+        in_specs=[full] * (len(parts) + 4),
+        out_specs=[pl.BlockSpec(memory_space=pltpu.HBM)] * 3,
+        scratch_shapes=[pltpu.VMEM(d.shape, f32)] * 3 + [pltpu.SemaphoreType.DMA((12,))],
+        compiler_params=pltpu.CompilerParams(vmem_limit_bytes=VMEM_LIMIT),
+    )(*parts, iterate, res, d, image)
+
+
 def swapped(value, axis, distance):
     return lax.ppermute(value, axis, [(i, i ^ distance) for i in range(lax.axis_size(axis))])
 
@@ -399,18 +473,7 @@
     )
     both = jnp.concatenate([stats, swapped(stats, "lat", 1)], axis=0)
     parts, _ = butterfly(both, "lon", distances(count)[::-1])
-    table = jnp.concatenate(parts, axis=0)
-    rr, dq, ss, sq, qq, a0 = (table[:, i] for i in range(6))
-    old_norm = jnp.sum(rr)
-    alpha = old_norm / jnp.sum(dq)
-    t = alpha - a0
-    new_norm = jnp.sum(ss + t * (t * qq - 2.0 * sq))
-    new_residual = residual - alpha * image
-    return (
-        iterate + alpha * direction,
-        new_residual,
-        new_residual + (new_norm / old_norm) * direction,
-    )
+    return tuple(update(parts, iterate, residual, direction, image))
 
 
 def solution(mesh):

time: 55.8 us -> 42 us (0.75)
  local copies, waits for them, and re-layouts: 4.8 us -> 0.04 us
  Pallas kernels: 11.3 us -> 7.59 us
  between operations: 3.46 us -> 0.79 us
  other arithmetic: 2.56 us -> 0.05 us
    pallas_call x1, Pallas kernels: 10.9 us -> 4.62 us  [image_and_stats(): pl.pallas_call(kernel, out_shape=[jax.ShapeDtypeStruct(d.shape, f32), jax...]
    unnamed x26 -> x16, local copies, waits for them, and re-layouts: 4.78 us -> 0.04 us
    pallas_call x1, Pallas kernels: 0.38 us -> 1.79 us  [pack(): pl.pallas_call(functools.partial(pack_kernel, 'lon', 'lat'), out_shape=[j...]
    reduce_sum x2 -> x0, other arithmetic: 1.29 us -> none  [the longest x1 0.68 us: shards(): alpha = old_norm / jnp.sum(dq)]
    pallas_call x0 -> x1, Pallas kernels: none -> 1.19 us  [update(): pl.pallas_call(functools.partial(update_kernel, len(parts)), out_shape=[j...]
    add x1 -> x0, other arithmetic: 1 us -> none  [shards(): new_residual + new_norm / old_norm * direction]
where the time goes in v2:
time: 42 us; the launch traced here: 41.9 us
  waiting for transfers between devices  23.2 us (55%)
  starting transfers between devices  10.2 us (24%)
  Pallas kernels  7.59 us (18%)
  between operations  0.79 us (2%)
    ppermute x10, waiting for transfers between devices, swapped(): lax.ppermute(value, axis, [(i, i ^ distance) for i in range(lax.axis_size...  19.2 us
    ppermute x10, starting transfers between devices, swapped(): lax.ppermute(value, axis, [(i, i ^ distance) for i in range(lax.axis_size...  8.89 us
    pallas_call x1, Pallas kernels, image_and_stats(): pl.pallas_call(kernel, out_shape=[jax.ShapeDtypeStruct(d.shape, f32), jax...  4.62 us
    ppermute x1, waiting for transfers between devices, odd_pairs(): return lax.ppermute(value, axis, pairs)  4.07 us
    pallas_call x1, Pallas kernels, pack(): pl.pallas_call(functools.partial(pack_kernel, 'lon', 'lat'), out_shape=[j...  1.79 us
    ppermute x1, starting transfers between devices, odd_pairs(): return lax.ppermute(value, axis, pairs)  1.29 us
    pallas_call x1, Pallas kernels, update(): pl.pallas_call(functools.partial(update_kernel, len(parts)), out_shape=[j...  1.19 us
  transfers between devices with their start and end apart: 11, of which 8 were waited for; matrix products, arithmetic and copies ran while one was open for 0% of the time, Pallas kernels for 0%

profile of v2, /device:TPU:0, one launch (start us, length us, event | category | flops | bytes accessed | tf_op | source)
XLA Modules:
  0.0 41.9 jit_solution(4562513178782472671)
XLA Ops:
  0.6 0.0 copy-start.1
  0.6 0.0 copy-start.2
  0.7 0.0 copy-start.3
  0.7 0.0 copy-start.4
  0.7 0.0 copy-start.5
  0.7 1.8 %shard_map.103 = (f32[64,128]{1,0:T(8,128)S(1)}, f32[64,128]{1,0:T(8,128)S(1)}, f32[160,128]{1,0:T(8,128)S(1)}, f32[160,128]{1,0:T(8,128)S(1)}) custom-call(f32[2,320,128]{2,1,0:T(8,128)} %refs_6_.1, s32[2,320,128]{2,1,0:T(8,128)} %refs_1_.1, f32[2,320,128]{2,1,0:T(8,128)} %refs_2_.1, f32[320,128]{1,0:T(8,128)} %refs_3_.1, f32[320,128]{1,0:T(8,128)} %refs_4_.2), custom_call_target="tpu_custom_call" | custom-call | tf_op jit(solution)/shard_map/pallas_call | solution.py:81
  2.5 0.0 copy-start
  2.5 4.1 %collective-permute-start = (f32[64,128]{1,0:T(8,128)S(1)}, f32[64,128]{1,0:T(8,128)S(1)}, u32[]{:S(2)}, u32[]{:S(2)}) collective-permute-start(f32[64,128]{1,0:T(8,128)S(1)} %get-tuple-element.9.refs_6_), channel_id=1, source_target_pairs={{0,8},{2,10},{4,12},{6,14},{8,0},{10,2},{12,4},{14,6},{1,9},{3,11}... | collective-permute-start | bytes 98312 | tf_op jit(solution)/shard_map/ppermute | solution.py:429
  6.6 0.0 collective-permute-start.5
  6.6 1.5 %collective-permute-start.3 = (f32[160,128]{1,0:T(8,128)S(1)}, f32[160,128]{1,0:T(8,128)S(1)}, u32[]{:S(2)}, u32[]{:S(2)}) collective-permute-start(f32[160,128]{1,0:T(8,128)S(1)} %get-tuple-element.10), channel_id=1, source_target_pairs={{0,2},{2,0},{4,6},{6,4},{8,10},{10,8},{12,14},{14,12},{1,3},{3,1},... | collective-permute-start | bytes 245768 | tf_op jit(solution)/shard_map/ppermute | solution.py:429
  8.1 1.3 %collective-permute-start.4 = (f32[160,128]{1,0:T(8,128)S(1)}, f32[160,128]{1,0:T(8,128)S(1)}, u32[]{:S(2)}, u32[]{:S(2)}) collective-permute-start(f32[160,128]{1,0:T(8,128)S(1)} %get-tuple-element.11), channel_id=1, source_target_pairs={{2,4},{4,2},{6,8},{8,6},{10,12},{12,10},{14,0},{0,14},{3,5},{5,3},... | collective-permute-start | bytes 245768 | tf_op jit(solution)/shard_map/ppermute | solution.py:437
  9.4 0.0 collective-permute-done.refs_7_
  9.4 1.0 %collective-permute-start.1 = (f32[128,128]{1,0:T(8,128)S(1)}, f32[128,128]{1,0:T(8,128)S(1)}, u32[]{:S(2)}, u32[]{:S(2)}) collective-permute-start(f32[128,128]{1,0:T(8,128)S(1)} %pad_maximum_fusion.1), channel_id=1, source_target_pairs={{0,4},{2,6},{4,0},{6,2},{8,12},{10,14},{12,8},{14,10},{1,5},{3,7},... | collective-permute-start | bytes 196616 | tf_op jit(solution)/shard_map/ppermute | solution.py:429
  10.4 1.6 %collective-permute-done.3.refs_10_ = f32[160,128]{1,0:T(8,128)S(1)} collective-permute-done((f32[160,128]{1,0:T(8,128)S(1)}, f32[160,128]{1,0:T(8,128)S(1)}, u32[]{:S(2)}, u32[]{:S(2)}) %collective-permute-start.3) | collective-permute-done | bytes 81952 | tf_op jit(solution)/shard_map/ppermute | solution.py:429
  12.0 4.1 %collective-permute-done.4.refs_11_ = f32[160,128]{1,0:T(8,128)S(1)} collective-permute-done((f32[160,128]{1,0:T(8,128)S(1)}, f32[160,128]{1,0:T(8,128)S(1)}, u32[]{:S(2)}, u32[]{:S(2)}) %collective-permute-start.4) | collective-permute-done | bytes 81952 | tf_op jit(solution)/shard_map/ppermute | solution.py:437
  16.1 0.0 collective-permute-start.6
  16.1 0.0 collective-permute-done.1.refs_8_
  16.1 0.9 %collective-permute-start.2 = (f32[256,128]{1,0:T(8,128)S(1)}, f32[256,128]{1,0:T(8,128)S(1)}, u32[]{:S(2)}, u32[]{:S(2)}) collective-permute-start(f32[256,128]{1,0:T(8,128)S(1)} %pad_maximum_fusion), channel_id=1, source_target_pairs={{0,2},{2,0},{4,6},{6,4},{8,10},{10,8},{12,14},{14,12},{1,3},{3,1},... | collective-permute-start | bytes 393224 | tf_op jit(solution)/shard_map/ppermute | solution.py:429
  17.0 0.3 collective-permute-done.6
  17.3 0.0 copy-start.7
  17.3 0.0 collective-permute-done.5.refs_12_
  17.3 4.8 %collective-permute-done.2.refs_9_ = f32[256,128]{1,0:T(8,128)S(1)} collective-permute-done((f32[256,128]{1,0:T(8,128)S(1)}, f32[256,128]{1,0:T(8,128)S(1)}, u32[]{:S(2)}, u32[]{:S(2)}) %collective-permute-start.2) | collective-permute-done | bytes 131104 | tf_op jit(solution)/shard_map/ppermute | solution.py:429
  22.1 0.0 copy-done.1
  22.1 0.0 copy-done.2
  22.1 0.0 copy-done.3
  22.1 0.0 copy-done.4
  22.1 0.0 copy-done.5
  22.1 0.0 copy-done
  22.1 0.0 copy-done.7
  22.1 0.0 copy-start.6
  22.2 4.6 %shard_map.104 = (f32[2,320,128]{2,1,0:T(8,128)S(1)}, f32[1,128]{1,0:T(1,128)S(1)}) custom-call(f32[2,320,128]{2,1,0:T(8,128)S(1)} %copy-done, s32[2,320,128]{2,1,0:T(8,128)S(1)} %copy-done.1, f32[2,320,128]{2,1,0:T(8,128)S(1)} %copy-done.2, f32[320,128]{1,0:T(8,128)S(1)} %copy-done.4, f32[320,128]{1,0:T(8,128)S(1)} %copy-done.5, ...), custom_call_target="tpu_custom_call" | custom-call | tf_op jit(solution)/shard_map/pallas_call | solution.py:364
  26.8 1.3 %collective-permute-start.7 = (f32[1,128]{1,0:T(1,128)S(1)}, f32[1,128]{1,0:T(1,128)S(1)}, u32[]{:S(2)}, u32[]{:S(2)}) collective-permute-start(f32[1,128]{1,0:T(1,128)S(1)} %get-tuple-element.13), channel_id=1, source_target_pairs={{0,1},{1,0},{2,3},{3,2},{4,5},{5,4},{6,7},{7,6},{8,9},{9,8},{10,11... | collective-permute-start | bytes 1544 | tf_op jit(solution)/shard_map/ppermute | solution.py:429
  28.0 0.8 %collective-permute-done.7 = f32[1,128]{1,0:T(1,128)S(1)} collective-permute-done((f32[1,128]{1,0:T(1,128)S(1)}, f32[1,128]{1,0:T(1,128)S(1)}, u32[]{:S(2)}, u32[]{:S(2)}) %collective-permute-start.7) | collective-permute-done | bytes 544 | tf_op jit(solution)/shard_map/ppermute | solution.py:429
  28.9 0.0 collective-permute-start.8
  28.9 3.6 %collective-permute-done.8.refs_1_ = f32[2,128]{1,0:T(2,128)S(1)} collective-permute-done((f32[2,128]{1,0:T(2,128)S(1)}, f32[2,128]{1,0:T(2,128)S(1)}, u32[]{:S(2)}, u32[]{:S(2)}) %collective-permute-start.8) | collective-permute-done | bytes 1056 | tf_op jit(solution)/shard_map/ppermute | solution.py:429
  32.4 0.1 collective-permute-start.9
  32.5 3.6 %collective-permute-done.9.refs_2_ = f32[4,128]{1,0:T(4,128)S(1)} collective-permute-done((f32[4,128]{1,0:T(4,128)S(1)}, f32[4,128]{1,0:T(4,128)S(1)}, u32[]{:S(2)}, u32[]{:S(2)}) %collective-permute-start.9) | collective-permute-done | bytes 2080 | tf_op jit(solution)/shard_map/ppermute | solution.py:429
  36.1 0.1 collective-permute-start.10
  36.2 4.5 %collective-permute-done.10.refs_3_ = f32[8,128]{1,0:T(8,128)S(1)} collective-permute-done((f32[8,128]{1,0:T(8,128)S(1)}, f32[8,128]{1,0:T(8,128)S(1)}, u32[]{:S(2)}, u32[]{:S(2)}) %collective-permute-start.10) | collective-permute-done | bytes 4128 | tf_op jit(solution)/shard_map/ppermute | solution.py:429
  40.7 0.0 copy-done.6
  40.7 1.2 %shard_map.105 = (f32[2,320,128]{2,1,0:T(8,128)}, f32[2,320,128]{2,1,0:T(8,128)}, f32[2,320,128]{2,1,0:T(8,128)}) custom-call(f32[2,128]{1,0:T(2,128)S(1)} %pad_maximum_fusion.5.refs_0_, f32[2,128]{1,0:T(2,128)S(1)} %collective-permute-done.8.refs_1_, f32[4,128]{1,0:T(4,128)S(1)} %collective-permute-done.9.refs_2_, ...), custom_call_target="tpu_custom_call" | custom-call | tf_op jit(solution)/shard_map/pallas_call | solution.py:418
  (9 shorter events, 0.1 us)
Async XLA Ops:
  0.6 21.5 %copy-start.1 = (s32[2,320,128]{2,1,0:T(8,128)S(1)}, s32[2,320,128]{2,1,0:T(8,128)}, u32[]{:S(2)}) copy-start(s32[2,320,128]{2,1,0:T(8,128)} %refs_1_.1) | copy-start | bytes 983044
  0.6 21.5 %copy-start.2 = (f32[2,320,128]{2,1,0:T(8,128)S(1)}, f32[2,320,128]{2,1,0:T(8,128)}, u32[]{:S(2)}) copy-start(f32[2,320,128]{2,1,0:T(8,128)} %refs_2_.1) | copy-start | bytes 983044
  0.7 21.5 %copy-start.3 = (f32[2,320,128]{2,1,0:T(8,128)S(1)}, f32[2,320,128]{2,1,0:T(8,128)}, u32[]{:S(2)}) copy-start(f32[2,320,128]{2,1,0:T(8,128)} %refs_5_.3) | copy-start | bytes 983044
  0.7 21.4 %copy-start.4 = (f32[320,128]{1,0:T(8,128)S(1)}, f32[320,128]{1,0:T(8,128)}, u32[]{:S(2)}) copy-start(f32[320,128]{1,0:T(8,128)} %refs_3_.1) | copy-start | bytes 491524
  0.7 21.4 %copy-start.5 = (f32[320,128]{1,0:T(8,128)S(1)}, f32[320,128]{1,0:T(8,128)}, u32[]{:S(2)}) copy-start(f32[320,128]{1,0:T(8,128)} %refs_4_.2) | copy-start | bytes 491524
  2.5 19.7 %copy-start = (f32[2,320,128]{2,1,0:T(8,128)S(1)}, f32[2,320,128]{2,1,0:T(8,128)}, u32[]{:S(2)}) copy-start(f32[2,320,128]{2,1,0:T(8,128)} %refs_6_.1) | copy-start | bytes 983044
  2.5 6.9 %collective-permute-start = (f32[64,128]{1,0:T(8,128)S(1)}, f32[64,128]{1,0:T(8,128)S(1)}, u32[]{:S(2)}, u32[]{:S(2)}) collective-permute-start(f32[64,128]{1,0:T(8,128)S(1)} %get-tuple-element.9.refs_6_), channel_id=1, source_target_pairs={{0,8},{2,10},{4,12},{6,14},{8,0},{10,2},{12,4},{14,6},{1,9},{3,11}... | collective-permute-start | bytes 98312 | tf_op jit(solution)/shard_map/ppermute | solution.py:429
  6.6 10.7 %collective-permute-start.5 = (f32[64,128]{1,0:T(8,128)S(1)}, f32[64,128]{1,0:T(8,128)S(1)}, u32[]{:S(2)}, u32[]{:S(2)}) collective-permute-start(f32[64,128]{1,0:T(8,128)S(1)} %get-tuple-element.12), channel_id=1, source_target_pairs={{0,1},{1,0},{2,3},{3,2},{4,5},{5,4},{6,7},{7,6},{8,9},{9,8},{10,11... | collective-permute-start | bytes 98312 | tf_op jit(solution)/shard_map/ppermute | solution.py:429
  6.6 5.4 %collective-permute-start.3 = (f32[160,128]{1,0:T(8,128)S(1)}, f32[160,128]{1,0:T(8,128)S(1)}, u32[]{:S(2)}, u32[]{:S(2)}) collective-permute-start(f32[160,128]{1,0:T(8,128)S(1)} %get-tuple-element.10), channel_id=1, source_target_pairs={{0,2},{2,0},{4,6},{6,4},{8,10},{10,8},{12,14},{14,12},{1,3},{3,1},... | collective-permute-start | bytes 245768 | tf_op jit(solution)/shard_map/ppermute | solution.py:429
  8.1 8.0 %collective-permute-start.4 = (f32[160,128]{1,0:T(8,128)S(1)}, f32[160,128]{1,0:T(8,128)S(1)}, u32[]{:S(2)}, u32[]{:S(2)}) collective-permute-start(f32[160,128]{1,0:T(8,128)S(1)} %get-tuple-element.11), channel_id=1, source_target_pairs={{2,4},{4,2},{6,8},{8,6},{10,12},{12,10},{14,0},{0,14},{3,5},{5,3},... | collective-permute-start | bytes 245768 | tf_op jit(solution)/shard_map/ppermute | solution.py:437
  9.4 6.7 %collective-permute-start.1 = (f32[128,128]{1,0:T(8,128)S(1)}, f32[128,128]{1,0:T(8,128)S(1)}, u32[]{:S(2)}, u32[]{:S(2)}) collective-permute-start(f32[128,128]{1,0:T(8,128)S(1)} %pad_maximum_fusion.1), channel_id=1, source_target_pairs={{0,4},{2,6},{4,0},{6,2},{8,12},{10,14},{12,8},{14,10},{1,5},{3,7},... | collective-permute-start | bytes 196616 | tf_op jit(solution)/shard_map/ppermute | solution.py:429
  16.1 1.2 %collective-permute-start.6 = (f32[16,128]{1,0:T(8,128)S(1)}, f32[16,128]{1,0:T(8,128)S(1)}, u32[]{:S(2)}, u32[]{:S(2)}) collective-permute-start(f32[16,128]{1,0:T(8,128)S(1)} %pad_maximum_fusion.2), channel_id=1, source_target_pairs={{0,1},{1,0},{2,3},{3,2},{4,5},{5,4},{6,7},{7,6},{8,9},{9,8},{10,11... | collective-permute-start | bytes 24584 | tf_op jit(solution)/shard_map/ppermute | solution.py:429
  16.1 6.0 %collective-permute-start.2 = (f32[256,128]{1,0:T(8,128)S(1)}, f32[256,128]{1,0:T(8,128)S(1)}, u32[]{:S(2)}, u32[]{:S(2)}) collective-permute-start(f32[256,128]{1,0:T(8,128)S(1)} %pad_maximum_fusion), channel_id=1, source_target_pairs={{0,2},{2,0},{4,6},{6,4},{8,10},{10,8},{12,14},{14,12},{1,3},{3,1},... | collective-permute-start | bytes 393224 | tf_op jit(solution)/shard_map/ppermute | solution.py:429
  17.3 4.9 %copy-start.7 = (s32[1024]{0:T(1024)S(1)}, s32[1024]{0:T(1024)}, u32[]{:S(2)}) copy-start(s32[1024]{0:T(1024)} %param.15) | copy-start | bytes 12292
  22.1 18.5 %copy-start.6 = (f32[2,320,128]{2,1,0:T(8,128)S(1)}, f32[2,320,128]{2,1,0:T(8,128)}, u32[]{:S(2)}) copy-start(f32[2,320,128]{2,1,0:T(8,128)} %refs_4_.3) | copy-start | bytes 983044
  26.8 2.1 %collective-permute-start.7 = (f32[1,128]{1,0:T(1,128)S(1)}, f32[1,128]{1,0:T(1,128)S(1)}, u32[]{:S(2)}, u32[]{:S(2)}) collective-permute-start(f32[1,128]{1,0:T(1,128)S(1)} %get-tuple-element.13), channel_id=1, source_target_pairs={{0,1},{1,0},{2,3},{3,2},{4,5},{5,4},{6,7},{7,6},{8,9},{9,8},{10,11... | collective-permute-start | bytes 1544 | tf_op jit(solution)/shard_map/ppermute | solution.py:429
  28.9 3.6 %collective-permute-start.8 = (f32[2,128]{1,0:T(2,128)S(1)}, f32[2,128]{1,0:T(2,128)S(1)}, u32[]{:S(2)}, u32[]{:S(2)}) collective-permute-start(f32[2,128]{1,0:T(2,128)S(1)} %pad_maximum_fusion.5.refs_0_), channel_id=1, source_target_pairs={{0,2},{2,0},{4,6},{6,4},{8,10},{10,8},{12,14},{14,12},{1,3},{3,1},... | collective-permute-start | bytes 3080 | tf_op jit(solution)/shard_map/ppermute | solution.py:429
  32.4 3.7 %collective-permute-start.9 = (f32[4,128]{1,0:T(4,128)S(1)}, f32[4,128]{1,0:T(4,128)S(1)}, u32[]{:S(2)}, u32[]{:S(2)}) collective-permute-start(f32[4,128]{1,0:T(4,128)S(1)} %pad_maximum_fusion.4), channel_id=1, source_target_pairs={{0,4},{2,6},{4,0},{6,2},{8,12},{10,14},{12,8},{14,10},{1,5},{3,7},... | collective-permute-start | bytes 6152 | tf_op jit(solution)/shard_map/ppermute | solution.py:429
  36.1 4.6 %collective-permute-start.10 = (f32[8,128]{1,0:T(8,128)S(1)}, f32[8,128]{1,0:T(8,128)S(1)}, u32[]{:S(2)}, u32[]{:S(2)}) collective-permute-start(f32[8,128]{1,0:T(8,128)S(1)} %pad_maximum_fusion.3), channel_id=1, source_target_pairs={{0,8},{2,10},{4,12},{6,14},{8,0},{10,2},{12,4},{14,6},{1,9},{3,11}... | collective-permute-start | bytes 12296 | tf_op jit(solution)/shard_map/ppermute | solution.py:429

commit v3 on v2

v3 whole, which is shorter than its diff:
```python
import functools

import jax
import jax.numpy as jnp
from jax import lax
from jax.experimental import pallas as pl
from jax.experimental.pallas import tpu as pltpu
from jax.sharding import PartitionSpec as P

STEPS = 4
HALO = 2 * STEPS
LANES = 128
VMEM_LIMIT = 24 * 1024 * 1024
PAY_ROWS = 168
STEP_CHUNK = 42
f32 = jnp.float32


def turn(value, shift, axis=1):
    shift = shift % value.shape[axis]
    return value if shift == 0 else pltpu.roll(value, shift, axis)


def lanes_of(shape):
    return lax.broadcasted_iota(jnp.int32, shape, 1)


def place(kind, level, half):
    return 8 * kind + 32 * half + 64 * level


STRIP = 56
STRIP_AT = (0, 8, 16, 24, 48 - STEPS, 52 - STEPS, 32, 40)


def rows_kernel(lat_axis, d, sea, pw, ek, nk, fold, strip, edge, partner, sea_strip, sea_edge, pw_strip, arrived):
    rows = d.shape[1]
    top_rows = pl.ds(rows - 8, 8)
    first = jnp.where(lax.axis_index(lat_axis) == 1, 0, rows - 8)
    edge_rows = pl.ds(pl.multiple_of(first, 8), 8)
    moves = [
        (sea.at[:, top_rows, :], sea_strip),
        (pw.at[:, top_rows, :], pw_strip),
        (sea.at[:, edge_rows, :], sea_edge),
        (d.at[0, top_rows, :], strip.at[0:8]),
        (d.at[1, top_rows, :], strip.at[8:16]),
        (ek.at[top_rows, :], strip.at[32:40]),
        (nk.at[top_rows, :], strip.at[40:48]),
        (d.at[:, edge_rows, :], edge.at[0:2]),
        (pw.at[:, edge_rows, :], edge.at[4:6]),
        (ek.at[edge_rows, :], edge.at[6]),
        (nk.at[edge_rows, :], edge.at[7]),
        (fold, partner),
    ]
    copies = [pltpu.make_async_copy(a, b, arrived.at[i]) for i, (a, b) in enumerate(moves)]
    for copy in copies:
        copy.start()
    for copy in copies:
        copy.wait()
    for level in range(2):
        strip[16 + 8 * level : 24 + 8 * level, :] = sea_strip[level].astype(f32)
    strip[48:56, :] = jnp.concatenate([pw_strip[0, STEPS:, :], pw_strip[1, STEPS:, :]], axis=0)
    edge[2:4] = sea_edge[...].astype(f32)


def rows_to_send(d, sea, pw, ek, nk, fold):
    full = pl.BlockSpec(memory_space=pltpu.VMEM)
    inputs = [pltpu.with_memory_space_constraint(x, pltpu.HBM) for x in (d, sea, pw, ek, nk, fold)]
    return pl.pallas_call(
        functools.partial(rows_kernel, "lat"),
        out_shape=[
            jax.ShapeDtypeStruct((STRIP, LANES), f32),
            jax.ShapeDtypeStruct((8, 8, LANES), f32),
            jax.ShapeDtypeStruct(fold.shape, jnp.int32),
        ],
        in_specs=[pl.BlockSpec(memory_space=pltpu.HBM)] * 6,
        out_specs=[full] * 3,
        scratch_shapes=[
            pltpu.VMEM((2, 8, LANES), jnp.int32),
            pltpu.VMEM((2, 8, LANES), jnp.int32),
            pltpu.VMEM((2, 8, LANES), f32),
            pltpu.SemaphoreType.DMA((12,)),
        ],
        compiler_params=pltpu.CompilerParams(vmem_limit_bytes=VMEM_LIMIT),
    )(*inputs)


def pack_kernel(lon_axis, d, sea, pw, ek, nk, rows_in, strip1, strip2, pay1, pay2, strips):
    strips[:STRIP, :] = strip1[...]
    strips[STRIP:, :] = strip2[...]
    rows = d.shape[1]
    groups = rows // 8
    half_groups = groups // 2
    even = lax.axis_index(lon_axis) % 2 == 0

    def plane(index, group):
        if group == groups:
            return rows_in[index]
        at = pl.ds(8 * group, 8)
        if index < 2:
            return d[index, at, :]
        if index < 4:
            return sea[index - 2, at, :].astype(f32)
        if index < 6:
            return pw[index - 4, at, :]
        return (ek, nk)[index - 6][at, :]

    lane = lanes_of((8, LANES))
    for line in range(half_groups + 1):
        east = jnp.zeros((8, LANES), f32)
        west = jnp.zeros((8, LANES), f32)
        for half, group in enumerate((line, line + half_groups) if line < half_groups else (groups,)):
            for kind in range(4):
                for level in range(2):
                    at = place(kind, level, half)
                    turned = turn(plane(2 * kind + level, group), at + 8)
                    east = jnp.where((lane >= at) & (lane < at + 8), turned, east)
                    first = (at + 8) % LANES
                    west = jnp.where((lane >= first) & (lane < first + 8), turned, west)
        pay1[8 * line : 8 * line + 8, :] = jnp.where(even, east, west)
        pay2[8 * line : 8 * line + 8, :] = jnp.where(even, west, east)


def columns_to_send(d, sea, pw, ek, nk, rows_in, strip1, strip2):
    size = PAY_ROWS
    full = pl.BlockSpec(memory_space=pltpu.VMEM)
    return pl.pallas_call(
        functools.partial(pack_kernel, "lon"),
        out_shape=[jax.ShapeDtypeStruct((size, LANES), f32) for size in (size, size, 2 * STRIP)],
        in_specs=[full] * 8,
        out_specs=[full] * 3,
        compiler_params=pltpu.CompilerParams(vmem_limit_bytes=VMEM_LIMIT),
    )(d, sea, pw, ek, nk, rows_in, strip1, strip2)


def slab_index(group, shift=0):
    if isinstance(group, int):
        return slice(8 + 8 * group + shift, 16 + 8 * group + shift)
    return pl.ds(pl.multiple_of(8 * group, 8) + 8 + shift, 8)


def over_groups(count, chunk, body):
    def turn_of(i, carry):
        for k in range(chunk):
            body(i * chunk + k)
        return carry

    lax.fori_loop(0, count // chunk, turn_of, 0)
    for group in range(count - count % chunk, count):
        body(group)


def east_of(x):
    lane = lanes_of(x[0].shape)
    a, b, s = (turn(v, -1) for v in x)
    return (
        jnp.where(lane == 127, s, a),
        jnp.where(lane == 63, s, b),
        jnp.where(lane == 127, a, jnp.where(lane == 63, b, s)),
    )


def west_of(x):
    lane = lanes_of(x[0].shape)
    a, b, s = (turn(v, 1) for v in x)
    return (
        jnp.where(lane == 0, s, a),
        jnp.where(lane == 64, s, b),
        jnp.where(lane == 0, a, jnp.where(lane == 64, b, s)),
    )


def coefficient_kernel(
    lon_axis, lat_axis, d, sea, pw, ek, nk, halo1, halo2, rows_in, field, weight, east_c, west_c, north_c, centre, ocean
):
    top = lax.axis_index(lat_axis) == 1
    even = lax.axis_index(lon_axis) % 2 == 0
    groups = d.shape[1] // 8
    half_groups = groups // 2
    lane = lanes_of((8, LANES))
    zero = jnp.zeros((8, LANES), f32)
    right = (lane & 63) < 32
    low = (lane < 32) | (lane >= 96)
    near = ((lane & 63) < 8) | ((lane & 63) >= 56)
    at = slab_index

    def beside_slabs(from_east, from_west, half):
        out = []
        for kind, extra in ((0, 0), (1, 0), (2, 0), (3, 0), (3, 64)):
            r = turn(from_east, extra - (place(kind, 0, half) + 8))
            w = turn(from_west, extra + 120 - place(kind, 0, half))
            out.append(jnp.where(right, r, w))
        pair, pair_turned = out[3:]
        out[3:] = [jnp.where(low, pair, pair_turned), jnp.where(low, pair_turned, pair)]
        out[1] = jnp.where(near, out[1], 0.0)
        return out

    def set_group(group, planes, side):
        ek_here, nk_here = planes[6], planes[7]
        d_s = (planes[0], turn(planes[1], 64), side[0])
        oc_s = (planes[2], turn(planes[3], 64), side[1])
        pw_s = (planes[4], turn(planes[5], 64), side[2])
        ek_s = (ek_here, turn(ek_here, 64), side[3])
        nk_s = (nk_here, turn(nk_here, 64), side[4])
        for s in range(3):
            ocean[s, at(group), :] = oc_s[s]
            field[s, at(group), :] = d_s[s] * oc_s[s]
            weight[s, at(group), :] = pw_s[s] * oc_s[s]
            east_c[s, at(group), :] = ek_s[s] * oc_s[s]
            north_c[s, at(group), :] = nk_s[s] * oc_s[s]

    last = groups + 2
    for s in range(3):
        for buffer in (ocean, north_c):
            buffer[s, 0:8, :] = zero
            buffer[s, 8 + 8 * last : 16 + 8 * last, :] = zero
    for group in range(groups):
        here = slice(8 * group, 8 * group + 8)
        half, inside = divmod(group, half_groups)
        there = slice(8 * inside, 8 * inside + 8)
        a, b = halo1[there, :], halo2[there, :]
        side = beside_slabs(jnp.where(even, a, b), jnp.where(even, b, a), half)
        planes = [d[0, here, :], d[1, here, :], sea[0, here, :].astype(f32), sea[1, here, :].astype(f32),
                  pw[0, here, :], pw[1, here, :], ek[here, :], nk[here, :]]
        set_group(group + 1, planes, side)
    planes = [rows_in[i] for i in range(8)]
    corner = slice(8 * half_groups, 8 * half_groups + 8)
    a, b = halo1[corner, :], halo2[corner, :]
    side = beside_slabs(jnp.where(even, a, b), jnp.where(even, b, a), 0)
    for group, used in ((0, top), (groups + 1, jnp.logical_not(top))):
        masked, masked_side = list(planes), list(side)
        masked[2] = jnp.where(used, planes[2], 0.0)
        masked[3] = jnp.where(used, planes[3], 0.0)
        masked_side[1] = jnp.where(used, side[1], 0.0)
        set_group(group, masked, masked_side)

    for group in range(groups + 2):
        here = at(group)
        oc = [ocean[s, here, :] for s in range(3)]
        half_face = [east_c[s, here, :] for s in range(3)]
        e, w = east_of(oc), west_of(half_face)
        for s in range(3):
            east_c[s, here, :] = half_face[s] * e[s]
            west_c[s, here, :] = oc[s] * w[s]
            north_c[s, here, :] = north_c[s, here, :] * ocean[s, at(group, 1), :]

    for group in range(groups + 2):
        for s in range(3):
            here = at(group)
            centre[s, here, :] = (
                1.0 - east_c[s, here, :] - west_c[s, here, :] - north_c[s, here, :] - north_c[s, at(group, -1), :]
            )


def coefficients(d, sea, pw, ek, nk, halo1, halo2, rows_in):
    full = pl.BlockSpec(memory_space=pltpu.VMEM)
    extended = (3, d.shape[1] + 32, LANES)
    return pl.pallas_call(
        functools.partial(coefficient_kernel, "lon", "lat"),
        out_shape=[jax.ShapeDtypeStruct(extended, f32)] * 6,
        in_specs=[full] * 8,
        out_specs=[full] * 6,
        scratch_shapes=[pltpu.VMEM(extended, f32)],
        compiler_params=pltpu.CompilerParams(vmem_limit_bytes=VMEM_LIMIT),
    )(d, sea, pw, ek, nk, halo1, halo2, rows_in)


def image_kernel(
    offsets, lon_axis, lat_axis,
    d, sea, res, first_field, weight, east_c, west_c, north_c, centre, partner, gathered_pieces,
    image, stats,
    blocks, folds, face_fold, field, other,
):
    lon = lax.axis_index(lon_axis)
    count = len(offsets)
    top = lax.axis_index(lat_axis) == 1
    groups = d.shape[1] // 8
    zero = jnp.zeros((8, LANES), f32)
    at = slab_index

    slot = 0
    for piece in gathered_pieces:
        for inside in range(piece.shape[0] // STRIP):
            block = lax.bitwise_xor(lon, offsets[slot])
            blocks[pl.ds(pl.multiple_of(block * STRIP, 8), STRIP), :] = piece[STRIP * inside : STRIP * (inside + 1), :]
            slot += 1
    wide = lanes_of((count, LANES))

    def strip_row(index, row):
        return blocks[pl.ds(STRIP_AT[index] + row, count, stride=STRIP), :]

    def strip_shift(values, to_east):
        step, edge = (-1, LANES - 1) if to_east else (1, 0)
        moved = [turn(x, step) for x in values]
        beside = [turn(x, step, 0) for x in moved]
        return [jnp.where(wide == edge, y, x) for x, y in zip(moved, beside)]

    partner_block = partner[...] >> 7
    partner_lane = partner[...] & (LANES - 1)

    def across(x):
        parts = []
        for first in range(0, count, 8):
            lanes_at = partner_lane[first : first + 8]
            block_at = partner_block[first : first + 8]
            total = jnp.zeros((8, LANES), f32)
            for block in range(count):
                source = jnp.broadcast_to(x[block : block + 1, :], (8, LANES))
                picked = jnp.take_along_axis(source, lanes_at, axis=1)
                total = jnp.where(block_at == block, picked, total)
            parts.append(total)
        return parts[0] if len(parts) == 1 else jnp.concatenate(parts, axis=0)

    @pl.when(top)
    def _():
        east_k = [strip_row(6, r) for r in range(HALO)]
        north_k = [strip_row(7, r) for r in range(HALO)]
        top_k = 0.5 * (north_k[-1] + across(north_k[-1]))
        both = range(2)
        oc = [[strip_row(2 + level, r) for r in range(HALO)] for level in both]
        u = [[strip_row(level, r) * oc[level][r] for r in range(HALO)] for level in both]
        oc_east = strip_shift([x for level in both for x in oc[level]], True)
        e = [[east_k[r] * oc[level][r] * oc_east[HALO * level + r] for r in range(HALO)] for level in both]
        w = strip_shift([x for level in both for x in e[level]], False)
        w = [w[:HALO], w[HALO:]]
        n = [[north_k[r] * oc[level][r] * oc[level][r + 1] for r in range(HALO - 1)] for level in both]
        for level in both:
            n[level].append(top_k * oc[level][-1] * across(oc[level][-1]))
            face_fold[level] = n[level][-1]
        c = [
            [None] + [1.0 - e[level][r] - w[level][r] - n[level][r] - n[level][r - 1] for r in range(1, HALO)]
            for level in both
        ]
        for t in range(HALO):
            if t == STEPS:
                for level in both:
                    for r in range(t, HALO):
                        u[level][r] = strip_row(4 + level, r) * oc[level][r] * u[level][r]
            beyond = [across(u[level][-1]) for level in both]
            for level in both:
                folds[t, level] = beyond[level]
            if t == HALO - 1:
                break
            rest = [(level, r) for level in both for r in range(t + 1, HALO)]
            east = strip_shift([u[level][r] for level, r in rest], True)
            west = strip_shift([u[level][r] for level, r in rest], False)
            new = [list(u[0]), list(u[1])]
            for (level, r), ue, uw in zip(rest, east, west):
                north = u[level][r + 1] if r + 1 < HALO else beyond[level]
                new[level][r] = (
                    c[level][r] * u[level][r]
                    + e[level][r] * ue
                    + w[level][r] * uw
                    + n[level][r] * north
                    + n[level][r - 1] * u[level][r - 1]
                )
            u = new

    def fold_rows(read):
        to_east = lax.rem(lon + 1, count)
        to_west = lax.rem(lon + count - 1, count)
        one = lanes_of((1, LANES))
        here0 = read(0, lon)
        here1 = turn(read(1, lon), 64)
        e0, w0 = read(0, to_east), read(0, to_west)
        e1, w1 = turn(read(1, to_east), 64), turn(read(1, to_west), 64)
        beside = jnp.where(one < 32, e0, jnp.where(one >= 96, w0, jnp.where(one >= 64, e1, w1)))
        return here0, here1, beside

    last = groups + 2
    fold_at = 8 + 8 * (groups + 1)
    for s in range(3):
        for buffer in (field, other):
            buffer[s, 0:8, :] = zero
            buffer[s, 8 + 8 * last : 16 + 8 * last, :] = zero
        for group in range(groups + 2):
            field[s, at(group), :] = first_field[s, at(group), :]

    def step(t, source, target):
        def one_group(group):
            here, up, down = at(group), at(group, 1), at(group, -1)
            u = [source[s, here, :] for s in range(3)]
            e, w = east_of(u), west_of(u)
            for s in range(3):
                target[s, here, :] = (
                    centre[s, here, :] * u[s]
                    + east_c[s, here, :] * e[s]
                    + west_c[s, here, :] * w[s]
                    + north_c[s, here, :] * source[s, up, :]
                    + north_c[s, down, :] * source[s, down, :]
                )

        over_groups(groups + 2, STEP_CHUNK, one_group)

        @pl.when(top)
        def _():
            face = fold_rows(lambda level, b: face_fold[level, pl.ds(b, 1), :])
            beyond = fold_rows(lambda level, b: folds[t, level, pl.ds(b, 1), :])
            row = slice(fold_at - 1, fold_at)
            for s in range(3):
                target[s, row, :] = target[s, row, :] + face[s] * (beyond[s] - source[s, row, :])

    def two_steps(i, carry):
        @pl.when(2 * i == STEPS)
        def _():
            for group in range(groups + 2):
                for s in range(3):
                    field[s, at(group), :] = field[s, at(group), :] * weight[s, at(group), :]

        step(2 * i, field, other)
        step(2 * i + 1, other, field)
        return carry

    lax.fori_loop(0, STEPS, two_steps, 0)

    rr = rq = dq = qq = zero
    for group in range(groups):
        here = slice(8 * group, 8 * group + 8)
        for level in range(2):
            u = turn(field[level, at(group + 1), :], 64 * level)
            o = sea[level, here, :].astype(f32)
            dv, rv = d[level, here, :], res[level, here, :]
            q = dv + o * u
            image[level, here, :] = q
            rr, rq, dq, qq = rr + rv * rv, rq + rv * q, dq + dv * q, qq + q * q
    rr, rq, dq, qq = (jnp.sum(x) for x in (rr, rq, dq, qq))
    a0 = jnp.where(qq > 0.0, rq / jnp.where(qq > 0.0, qq, 1.0), 0.0)
    ss = sq = zero
    for group in range(groups):
        here = slice(8 * group, 8 * group + 8)
        for level in range(2):
            q = image[level, here, :]
            s = res[level, here, :] - a0 * q
            ss, sq = ss + s * s, sq + s * q
    ss, sq = jnp.sum(ss), jnp.sum(sq)
    one = lanes_of((1, LANES))
    row = jnp.zeros((1, LANES), f32)
    for index, value in enumerate((rr, dq, ss, sq, qq, a0)):
        row = jnp.where(one == index, value, row)
    stats[...] = row


def image_and_stats(d, sea, res, coeffs, partner, pieces, offsets):
    count = len(offsets)
    full = pl.BlockSpec(memory_space=pltpu.VMEM)
    extended = coeffs[0].shape
    inputs = [d, sea, res, *coeffs, partner, *pieces]

    def kernel(*refs):
        image_kernel(offsets, "lon", "lat", *refs[:10], refs[10 : len(inputs)], *refs[len(inputs) :])

    return pl.pallas_call(
        kernel,
        out_shape=[jax.ShapeDtypeStruct(d.shape, f32), jax.ShapeDtypeStruct((1, LANES), f32)],
        in_specs=[full] * len(inputs),
        out_specs=[full] * 2,
        scratch_shapes=[
            pltpu.VMEM((STRIP * count, LANES), f32),
            pltpu.VMEM((HALO, 2, count, LANES), f32),
            pltpu.VMEM((2, count, LANES), f32),
            pltpu.VMEM(extended, f32),
            pltpu.VMEM(extended, f32),
        ],
        compiler_params=pltpu.CompilerParams(vmem_limit_bytes=VMEM_LIMIT),
    )(*inputs)


def update_kernel(count, *refs):
    parts = refs[:count]
    iterate, res, d, image, iterate_hbm, res_hbm, d_hbm, new_iterate, new_res, new_d, sent = refs[count:]
    table = jnp.concatenate([part[...] for part in parts], axis=0)
    lane = lanes_of(table.shape)
    sums = jnp.sum(table, axis=0, keepdims=True)
    one = lanes_of(sums.shape)
    pick = lambda row, index: jnp.sum(jnp.where(one == index, row, 0.0), axis=1, keepdims=True)
    old_norm = pick(sums, 0)
    alpha = old_norm / pick(sums, 1)
    t = alpha - turn(table, -3)
    norms = table + t * (t * turn(table, -2) - 2.0 * turn(table, -1))
    new_norm = pick(jnp.sum(norms, axis=0, keepdims=True), 2)
    beta = new_norm / old_norm
    rows = d.shape[1]
    pieces = 2
    alpha = jnp.broadcast_to(alpha, (8, LANES))
    beta = jnp.broadcast_to(beta, (8, LANES))
    copies = []
    for level in range(2):
        for piece in range(pieces):
            first, size = piece * (rows // pieces), rows // pieces
            for row in range(first, first + size, 8):
                here = slice(row, row + 8)
                dv = d[level, here, :]
                rv = res[level, here, :] - alpha * image[level, here, :]
                new_iterate[level, here, :] = iterate[level, here, :] + alpha * dv
                new_res[level, here, :] = rv
                new_d[level, here, :] = rv + beta * dv
            for index, (a, b) in enumerate(((new_iterate, iterate_hbm), (new_res, res_hbm), (new_d, d_hbm))):
                part = (level, pl.ds(first, size), slice(None))
                copies.append(pltpu.make_async_copy(a.at[part], b.at[part], sent.at[len(copies)]))
                copies[-1].start()
    for copy in copies:
        copy.wait()


def update(parts, iterate, res, d, image):
    full = pl.BlockSpec(memory_space=pltpu.VMEM)
    return pl.pallas_call(
        functools.partial(update_kernel, len(parts)),
        out_shape=[jax.ShapeDtypeStruct(d.shape, f32)] * 3,
        in_specs=[full] * (len(parts) + 4),
        out_specs=[pl.BlockSpec(memory_space=pltpu.HBM)] * 3,
        scratch_shapes=[pltpu.VMEM(d.shape, f32)] * 3 + [pltpu.SemaphoreType.DMA((12,))],
        compiler_params=pltpu.CompilerParams(vmem_limit_bytes=VMEM_LIMIT),
    )(*parts, iterate, res, d, image)


def swapped(value, axis, distance):
    return lax.ppermute(value, axis, [(i, i ^ distance) for i in range(lax.axis_size(axis))])


def odd_pairs(value, axis):
    count = lax.axis_size(axis)
    pairs = []
    for i in range(1, count, 2):
        pairs += [(i, (i + 1) % count), ((i + 1) % count, i)]
    return lax.ppermute(value, axis, pairs)


def distances(count):
    found = []
    while count > 1:
        count //= 2
        found.append(count)
    return found


def strip_swap(value, distance):
    members, count, halves = (lax.axis_size(axis) for axis in ("member", "lon", "lat"))
    number = lambda m, i, t: (m * count + i) * halves + t
    other = lambda m, i, t: number(m, i ^ distance, t) if t or members % 2 else number(m ^ 1, i, t)
    places = [(m, i, t) for m in range(members) for i in range(count) for t in range(halves)]
    return lax.ppermute(value, ("member", "lon", "lat"), [(number(*p), other(*p)) for p in places])


def butterfly(pieces, offsets, swap, order):
    pieces, offsets = list(pieces), list(offsets)
    for distance in order:
        whole = pieces[0] if len(pieces) == 1 else jnp.concatenate(pieces, axis=0)
        pieces.append(swap(whole, distance))
        offsets += [o ^ distance for o in offsets]
    return pieces, offsets


def shards(iterate, residual, direction, land_sea, precision_weight, east_kappa, north_kappa, fold_partner):
    count = lax.axis_size("lon")
    fields = (direction, land_sea, precision_weight, east_kappa, north_kappa)
    strip, edge, partner = rows_to_send(*fields, fold_partner.reshape(count, LANES))
    rows_in = swapped(edge, "lat", 1)
    strip2 = strip_swap(strip, count // 2)
    pay1, pay2, strips = columns_to_send(*fields, rows_in, strip, strip2)
    halo2 = odd_pairs(pay2, "lon")
    halo1 = swapped(pay1, "lon", 1)
    rest = distances(count)[1:]
    pieces, offsets = butterfly([strips], [0, count // 2], strip_swap, rest[:-1])
    pieces += [strip_swap(piece, rest[-1]) for piece in pieces]
    offsets += [o ^ rest[-1] for o in offsets]
    coeffs = coefficients(*fields, halo1, halo2, rows_in)
    image, stats = image_and_stats(direction, land_sea, residual, coeffs, partner, pieces, offsets)
    parts, _ = butterfly([stats], [0], lambda value, distance: swapped(value, "lon", distance), distances(count)[::-1])
    parts.append(swapped(jnp.concatenate(parts, axis=0), "lat", 1))
    return tuple(update(parts, iterate, residual, direction, image))


def solution(mesh):
    field = P("member", "lat", "lon")
    level = P(None, "lat", "lon")
    flat = P("lat", "lon")
    return jax.shard_map(
        shards,
        mesh=mesh,
        in_specs=(field, field, field, level, level, flat, flat, P()),
        out_specs=(field, field, field),
        check_vma=False,
    )
```

time: 42 us -> 38.3 us (0.912)
  waiting for transfers between devices: 23.2 us -> 15.4 us
  starting transfers between devices: 10.2 us -> 13.4 us
  Pallas kernels: 7.59 us -> 8.5 us
    ppermute x10 -> x6, waiting for transfers between devices: 19.2 us -> 11.8 us  [swapped(): lax.ppermute(value, axis, [(i, i ^ distance) for i in range(lax.axis_size...]
    ppermute x0 -> x4, starting transfers between devices: none -> 6.68 us  [strip_swap(): lax.ppermute(value, ('member', 'lon', 'lat'), [(number(*p), other(*p)) fo...]
    ppermute x10 -> x6, starting transfers between devices: 8.89 us -> 3.14 us  [swapped(): lax.ppermute(value, axis, [(i, i ^ distance) for i in range(lax.axis_size...]
    ppermute x1, waiting for transfers between devices: 4.07 us -> 1.66 us  [odd_pairs(): return lax.ppermute(value, axis, pairs)]
    ppermute x1, starting transfers between devices: 1.29 us -> 3.54 us  [odd_pairs(): return lax.ppermute(value, axis, pairs)]
    ppermute x0 -> x4, waiting for transfers between devices: none -> 1.86 us  [strip_swap(): lax.ppermute(value, ('member', 'lon', 'lat'), [(number(*p), other(*p)) fo...]
    pallas_call x1 -> x3, Pallas kernels: 1.79 us -> 2.54 us  [the longest x1 1.17 us: coefficients(): pl.pallas_call(functools.partial(coefficient_kernel, 'lon', 'lat'), out_s...]
  transfers between devices with their start and end apart: 11 -> 11, of which waited for: 8 -> 6; matrix products, arithmetic and copies ran while one was open for 0% -> 0% of each run, Pallas kernels for 0% -> 3%
where the time goes in v3:
time: 38.3 us; the launch traced here: 38.1 us
  waiting for transfers between devices  15.4 us (40%)
  starting transfers between devices  13.4 us (35%)
  Pallas kernels  8.5 us (22%)
  between operations  0.79 us (2%)
    ppermute x6, waiting for transfers between devices, swapped(): lax.ppermute(value, axis, [(i, i ^ distance) for i in range(lax.axis_size...  11.8 us
    ppermute x4, starting transfers between devices, strip_swap(): lax.ppermute(value, ('member', 'lon', 'lat'), [(number(*p), other(*p)) fo...  6.68 us
    pallas_call x1, Pallas kernels, image_and_stats(): pl.pallas_call(kernel, out_shape=[jax.ShapeDtypeStruct(d.shape, f32), jax...  4.77 us
    ppermute x1, starting transfers between devices, odd_pairs(): return lax.ppermute(value, axis, pairs)  3.54 us
    ppermute x6, starting transfers between devices, swapped(): lax.ppermute(value, axis, [(i, i ^ distance) for i in range(lax.axis_size...  3.14 us
    ppermute x4, waiting for transfers between devices, strip_swap(): lax.ppermute(value, ('member', 'lon', 'lat'), [(number(*p), other(*p)) fo...  1.86 us
    ppermute x1, waiting for transfers between devices, odd_pairs(): return lax.ppermute(value, axis, pairs)  1.66 us
    pallas_call x1, Pallas kernels, update(): pl.pallas_call(functools.partial(update_kernel, len(parts)), out_shape=[j...  1.19 us
  transfers between devices with their start and end apart: 11, of which 6 were waited for; matrix products, arithmetic and copies ran while one was open for 0% of the time, Pallas kernels for 3%

profile of v3, /device:TPU:0, one launch (start us, length us, event | category | flops | bytes accessed | tf_op | source)
XLA Modules:
  0.0 38.1 jit_solution(10243699561170694397)
XLA Ops:
  0.6 0.0 copy-start
  0.6 0.0 copy-start.1
  0.7 0.0 copy-start.2
  0.7 0.0 copy-start.3
  0.7 0.0 copy-start.4
  0.7 1.0 %shard_map.103 = (f32[56,128]{1,0:T(8,128)S(1)}, f32[8,8,128]{2,1,0:T(8,128)S(1)}, s32[8,128]{1,0:T(8,128)S(1)}) custom-call(f32[2,320,128]{2,1,0:T(8,128)} %refs_7_.1, s32[2,320,128]{2,1,0:T(8,128)} %refs_1_.1, f32[2,320,128]{2,1,0:T(8,128)} %pw.5, f32[320,128]{1,0:T(8,128)} %ek.5, f32[320,128]{1,0:T(8,128)} %nk.5, s32[8,128]{1,0:T(8,128)} %bitcast.1), custom_call_target="tpu_custom_call" | custom-call | tf_op jit(solution)/shard_map/pallas_call | solution.py:69
  1.7 0.5 %collective-permute-start = (f32[8,8,128]{2,1,0:T(8,128)S(1)}, f32[8,8,128]{2,1,0:T(8,128)S(1)}, u32[]{:S(2)}, u32[]{:S(2)}) collective-permute-start(f32[8,8,128]{2,1,0:T(8,128)S(1)} %get-tuple-element.17), channel_id=1, source_target_pairs={{0,1},{1,0},{2,3},{3,2},{4,5},{5,4},{6,7},{7,6},{8,9},{9,8},{10,11... | collective-permute-start | bytes 98312 | tf_op jit(solution)/shard_map/ppermute | solution.py:518
  2.2 2.6 %collective-permute-start.1 = (f32[56,128]{1,0:T(8,128)S(1)}, f32[56,128]{1,0:T(8,128)S(1)}, u32[]{:S(2)}, u32[]{:S(2)}) collective-permute-start(f32[56,128]{1,0:T(8,128)S(1)} %get-tuple-element.18.strip1), channel_id=1, source_target_pairs={{0,16},{1,9},{2,18},{3,11},{4,20},{5,13},{6,22},{7,15},{8,24},{9,1... | collective-permute-start | bytes 86024 | tf_op jit(solution)/shard_map/ppermute | solution.py:542
  4.7 1.9 %collective-permute-done.1.strip2 = f32[56,128]{1,0:T(8,128)S(1)} collective-permute-done((f32[56,128]{1,0:T(8,128)S(1)}, f32[56,128]{1,0:T(8,128)S(1)}, u32[]{:S(2)}, u32[]{:S(2)}) %collective-permute-start.1) | collective-permute-done | bytes 28704 | tf_op jit(solution)/shard_map/ppermute | solution.py:542
  6.6 0.0 collective-permute-done.rows_in
  6.6 0.0 copy-done
  6.6 0.0 copy-done.1
  6.6 0.0 copy-done.2
  6.6 0.0 copy-done.3
  6.6 0.0 copy-done.4
  6.6 0.4 %shard_map.104 = (f32[168,128]{1,0:T(8,128)S(1)}, f32[168,128]{1,0:T(8,128)S(1)}, f32[112,128]{1,0:T(8,128)S(1)}) custom-call(f32[2,320,128]{2,1,0:T(8,128)S(1)} %copy-done, s32[2,320,128]{2,1,0:T(8,128)S(1)} %copy-done.1, f32[2,320,128]{2,1,0:T(8,128)S(1)} %copy-done.2, f32[320,128]{1,0:T(8,128)S(1)} %copy-done.3, f32[320,128]{1,0:T(8,128)S(1)} %copy-done.4, ...), custom_call_target="tpu_custom_call" | custom-call | tf_op jit(solution)/shard_map/pallas_call | solution.py:127
  7.0 2.1 %collective-permute-start.4 = (f32[112,128]{1,0:T(8,128)S(1)}, f32[112,128]{1,0:T(8,128)S(1)}, u32[]{:S(2)}, u32[]{:S(2)}) collective-permute-start(f32[112,128]{1,0:T(8,128)S(1)} %get-tuple-element.28.refs_10_), channel_id=1, source_target_pairs={{0,16},{1,5},{2,18},{3,7},{4,20},{5,1},{6,22},{7,3},{8,24},{9,13},... | collective-permute-start | bytes 172040 | tf_op jit(solution)/shard_map/ppermute | solution.py:542
  9.1 1.5 %collective-permute-start.2 = (f32[168,128]{1,0:T(8,128)S(1)}, f32[168,128]{1,0:T(8,128)S(1)}, u32[]{:S(2)}, u32[]{:S(2)}) collective-permute-start(f32[168,128]{1,0:T(8,128)S(1)} %get-tuple-element.19), channel_id=1, source_target_pairs={{0,2},{2,0},{4,6},{6,4},{8,10},{10,8},{12,14},{14,12},{1,3},{3,1},... | collective-permute-start | bytes 258056 | tf_op jit(solution)/shard_map/ppermute | solution.py:518
  10.6 0.0 copy-start.5
  10.6 3.5 %collective-permute-start.3 = (f32[168,128]{1,0:T(8,128)S(1)}, f32[168,128]{1,0:T(8,128)S(1)}, u32[]{:S(2)}, u32[]{:S(2)}) collective-permute-start(f32[168,128]{1,0:T(8,128)S(1)} %get-tuple-element.20), channel_id=1, source_target_pairs={{2,4},{4,2},{6,8},{8,6},{10,12},{12,10},{14,0},{0,14},{3,5},{5,3},... | collective-permute-start | bytes 258056 | tf_op jit(solution)/shard_map/ppermute | solution.py:526
  14.2 0.5 %collective-permute-start.5 = (f32[112,128]{1,0:T(8,128)S(1)}, f32[112,128]{1,0:T(8,128)S(1)}, u32[]{:S(2)}, u32[]{:S(2)}) collective-permute-start(f32[112,128]{1,0:T(8,128)S(1)} %get-tuple-element.28.refs_10_), channel_id=1, source_target_pairs={{0,16},{1,3},{2,18},{3,1},{4,20},{5,7},{6,22},{7,5},{8,24},{9,11},... | collective-permute-start | bytes 172040 | tf_op jit(solution)/shard_map/ppermute | solution.py:542
  14.7 0.0 collective-permute-done.4.refs_11_
  14.7 1.5 %collective-permute-start.6 = (f32[112,128]{1,0:T(8,128)S(1)}, f32[112,128]{1,0:T(8,128)S(1)}, u32[]{:S(2)}, u32[]{:S(2)}) collective-permute-start(f32[112,128]{1,0:T(8,128)S(1)} %collective-permute-done.4.refs_11_), channel_id=1, source_target_pairs={{0,16},{1,3},{2,18},{3,1},{4,20},{5,7},{6,22},{7,5},{8,24},{9,11},... | collective-permute-start | bytes 172040 | tf_op jit(solution)/shard_map/ppermute | solution.py:542
  16.2 0.0 collective-permute-done.2.halo1
  16.2 1.7 %collective-permute-done.3.halo2 = f32[168,128]{1,0:T(8,128)S(1)} collective-permute-done((f32[168,128]{1,0:T(8,128)S(1)}, f32[168,128]{1,0:T(8,128)S(1)}, u32[]{:S(2)}, u32[]{:S(2)}) %collective-permute-start.3) | collective-permute-done | bytes 86048 | tf_op jit(solution)/shard_map/ppermute | solution.py:526
  17.9 1.2 %shard_map.105 = (f32[3,352,128]{2,1,0:T(8,128)S(1)}, f32[3,352,128]{2,1,0:T(8,128)S(1)}, f32[3,352,128]{2,1,0:T(8,128)S(1)}, f32[3,352,128]{2,1,0:T(8,128)S(1)}...) custom-call(f32[2,320,128]{2,1,0:T(8,128)S(1)} %copy-done, s32[2,320,128]{2,1,0:T(8,128)S(1)} %copy-done.1, ...), custom_call_target="tpu_custom_call" | custom-call | tf_op jit(solution)/shard_map/pallas_call | solution.py:258
  19.1 0.0 collective-permute-done.5.refs_12_
  19.1 0.0 collective-permute-done.6.refs_13_
  19.1 0.0 copy-done.5
  19.1 0.0 copy-start.6
  19.1 4.8 %shard_map.106 = (f32[2,320,128]{2,1,0:T(8,128)S(1)}, f32[1,128]{1,0:T(1,128)S(1)}) custom-call(f32[2,320,128]{2,1,0:T(8,128)S(1)} %copy-done, s32[2,320,128]{2,1,0:T(8,128)S(1)} %copy-done.1, f32[2,320,128]{2,1,0:T(8,128)S(1)} %copy-done.5, f32[3,352,128]{2,1,0:T(8,128)S(1)} %get-tuple-element.21.refs_3_, f32[3,352,128]{2,1,0:T(8,128)S(1)} %get-tuple-element.22.refs_4_, ...), custom_call_target="tpu_custom_call" | custom-call | tf_op jit(solution)/shard_map/pallas_call | solution.py:452
  23.9 0.1 collective-permute-start.7
  24.0 3.5 %collective-permute-done.7.refs_1_ = f32[1,128]{1,0:T(1,128)S(1)} collective-permute-done((f32[1,128]{1,0:T(1,128)S(1)}, f32[1,128]{1,0:T(1,128)S(1)}, u32[]{:S(2)}, u32[]{:S(2)}) %collective-permute-start.7) | collective-permute-done | bytes 544 | tf_op jit(solution)/shard_map/ppermute | solution.py:518
  27.5 0.0 collective-permute-start.8
  27.5 3.6 %collective-permute-done.8.refs_2_ = f32[2,128]{1,0:T(2,128)S(1)} collective-permute-done((f32[2,128]{1,0:T(2,128)S(1)}, f32[2,128]{1,0:T(2,128)S(1)}, u32[]{:S(2)}, u32[]{:S(2)}) %collective-permute-start.8) | collective-permute-done | bytes 1056 | tf_op jit(solution)/shard_map/ppermute | solution.py:518
  31.1 1.0 %collective-permute-start.9 = (f32[4,128]{1,0:T(4,128)S(1)}, f32[4,128]{1,0:T(4,128)S(1)}, u32[]{:S(2)}, u32[]{:S(2)}) collective-permute-start(f32[4,128]{1,0:T(4,128)S(1)} %pad_maximum_fusion.1), channel_id=1, source_target_pairs={{0,8},{2,10},{4,12},{6,14},{8,0},{10,2},{12,4},{14,6},{1,9},{3,11}... | collective-permute-start | bytes 6152 | tf_op jit(solution)/shard_map/ppermute | solution.py:518
  32.0 3.6 %collective-permute-done.9.refs_3_ = f32[4,128]{1,0:T(4,128)S(1)} collective-permute-done((f32[4,128]{1,0:T(4,128)S(1)}, f32[4,128]{1,0:T(4,128)S(1)}, u32[]{:S(2)}, u32[]{:S(2)}) %collective-permute-start.9) | collective-permute-done | bytes 2080 | tf_op jit(solution)/shard_map/ppermute | solution.py:518
  35.6 0.1 collective-permute-start.10
  35.7 1.2 %collective-permute-done.10.refs_4_ = f32[8,128]{1,0:T(8,128)S(1)} collective-permute-done((f32[8,128]{1,0:T(8,128)S(1)}, f32[8,128]{1,0:T(8,128)S(1)}, u32[]{:S(2)}, u32[]{:S(2)}) %collective-permute-start.10) | collective-permute-done | bytes 4128 | tf_op jit(solution)/shard_map/ppermute | solution.py:518
  36.9 0.0 copy-done.6
  36.9 1.2 %shard_map.107 = (f32[2,320,128]{2,1,0:T(8,128)}, f32[2,320,128]{2,1,0:T(8,128)}, f32[2,320,128]{2,1,0:T(8,128)}) custom-call(f32[1,128]{1,0:T(1,128)S(1)} %get-tuple-element.29.refs_0_, f32[1,128]{1,0:T(1,128)S(1)} %collective-permute-done.7.refs_1_, f32[2,128]{1,0:T(2,128)S(1)} %collective-permute-done.8.refs_2_, ...), custom_call_target="tpu_custom_call" | custom-call | tf_op jit(solution)/shard_map/pallas_call | solution.py:507
  (3 shorter events, 0.0 us)
Async XLA Ops:
  0.6 6.0 %copy-start = (f32[2,320,128]{2,1,0:T(8,128)S(1)}, f32[2,320,128]{2,1,0:T(8,128)}, u32[]{:S(2)}) copy-start(f32[2,320,128]{2,1,0:T(8,128)} %refs_7_.1) | copy-start | bytes 983044
  0.6 6.0 %copy-start.1 = (s32[2,320,128]{2,1,0:T(8,128)S(1)}, s32[2,320,128]{2,1,0:T(8,128)}, u32[]{:S(2)}) copy-start(s32[2,320,128]{2,1,0:T(8,128)} %refs_1_.1) | copy-start | bytes 983044
  0.7 6.0 %copy-start.2 = (f32[2,320,128]{2,1,0:T(8,128)S(1)}, f32[2,320,128]{2,1,0:T(8,128)}, u32[]{:S(2)}) copy-start(f32[2,320,128]{2,1,0:T(8,128)} %pw.5) | copy-start | bytes 983044
  0.7 6.0 %copy-start.3 = (f32[320,128]{1,0:T(8,128)S(1)}, f32[320,128]{1,0:T(8,128)}, u32[]{:S(2)}) copy-start(f32[320,128]{1,0:T(8,128)} %ek.5) | copy-start | bytes 491524
  0.7 6.0 %copy-start.4 = (f32[320,128]{1,0:T(8,128)S(1)}, f32[320,128]{1,0:T(8,128)}, u32[]{:S(2)}) copy-start(f32[320,128]{1,0:T(8,128)} %nk.5) | copy-start | bytes 491524
  1.7 4.9 %collective-permute-start = (f32[8,8,128]{2,1,0:T(8,128)S(1)}, f32[8,8,128]{2,1,0:T(8,128)S(1)}, u32[]{:S(2)}, u32[]{:S(2)}) collective-permute-start(f32[8,8,128]{2,1,0:T(8,128)S(1)} %get-tuple-element.17), channel_id=1, source_target_pairs={{0,1},{1,0},{2,3},{3,2},{4,5},{5,4},{6,7},{7,6},{8,9},{9,8},{10,11... | collective-permute-start | bytes 98312 | tf_op jit(solution)/shard_map/ppermute | solution.py:518
  2.2 4.4 %collective-permute-start.1 = (f32[56,128]{1,0:T(8,128)S(1)}, f32[56,128]{1,0:T(8,128)S(1)}, u32[]{:S(2)}, u32[]{:S(2)}) collective-permute-start(f32[56,128]{1,0:T(8,128)S(1)} %get-tuple-element.18.strip1), channel_id=1, source_target_pairs={{0,16},{1,9},{2,18},{3,11},{4,20},{5,13},{6,22},{7,15},{8,24},{9,1... | collective-permute-start | bytes 86024 | tf_op jit(solution)/shard_map/ppermute | solution.py:542
  7.0 7.7 %collective-permute-start.4 = (f32[112,128]{1,0:T(8,128)S(1)}, f32[112,128]{1,0:T(8,128)S(1)}, u32[]{:S(2)}, u32[]{:S(2)}) collective-permute-start(f32[112,128]{1,0:T(8,128)S(1)} %get-tuple-element.28.refs_10_), channel_id=1, source_target_pairs={{0,16},{1,5},{2,18},{3,7},{4,20},{5,1},{6,22},{7,3},{8,24},{9,13},... | collective-permute-start | bytes 172040 | tf_op jit(solution)/shard_map/ppermute | solution.py:542
  9.1 7.1 %collective-permute-start.2 = (f32[168,128]{1,0:T(8,128)S(1)}, f32[168,128]{1,0:T(8,128)S(1)}, u32[]{:S(2)}, u32[]{:S(2)}) collective-permute-start(f32[168,128]{1,0:T(8,128)S(1)} %get-tuple-element.19), channel_id=1, source_target_pairs={{0,2},{2,0},{4,6},{6,4},{8,10},{10,8},{12,14},{14,12},{1,3},{3,1},... | collective-permute-start | bytes 258056 | tf_op jit(solution)/shard_map/ppermute | solution.py:518
  10.6 8.4 %copy-start.5 = (f32[2,320,128]{2,1,0:T(8,128)S(1)}, f32[2,320,128]{2,1,0:T(8,128)}, u32[]{:S(2)}) copy-start(f32[2,320,128]{2,1,0:T(8,128)} %refs_6_.1) | copy-start | bytes 983044
  10.6 7.2 %collective-permute-start.3 = (f32[168,128]{1,0:T(8,128)S(1)}, f32[168,128]{1,0:T(8,128)S(1)}, u32[]{:S(2)}, u32[]{:S(2)}) collective-permute-start(f32[168,128]{1,0:T(8,128)S(1)} %get-tuple-element.20), channel_id=1, source_target_pairs={{2,4},{4,2},{6,8},{8,6},{10,12},{12,10},{14,0},{0,14},{3,5},{5,3},... | collective-permute-start | bytes 258056 | tf_op jit(solution)/shard_map/ppermute | solution.py:526
  14.2 4.9 %collective-permute-start.5 = (f32[112,128]{1,0:T(8,128)S(1)}, f32[112,128]{1,0:T(8,128)S(1)}, u32[]{:S(2)}, u32[]{:S(2)}) collective-permute-start(f32[112,128]{1,0:T(8,128)S(1)} %get-tuple-element.28.refs_10_), channel_id=1, source_target_pairs={{0,16},{1,3},{2,18},{3,1},{4,20},{5,7},{6,22},{7,5},{8,24},{9,11},... | collective-permute-start | bytes 172040 | tf_op jit(solution)/shard_map/ppermute | solution.py:542
  14.7 4.4 %collective-permute-start.6 = (f32[112,128]{1,0:T(8,128)S(1)}, f32[112,128]{1,0:T(8,128)S(1)}, u32[]{:S(2)}, u32[]{:S(2)}) collective-permute-start(f32[112,128]{1,0:T(8,128)S(1)} %collective-permute-done.4.refs_11_), channel_id=1, source_target_pairs={{0,16},{1,3},{2,18},{3,1},{4,20},{5,7},{6,22},{7,5},{8,24},{9,11},... | collective-permute-start | bytes 172040 | tf_op jit(solution)/shard_map/ppermute | solution.py:542
  19.1 17.8 %copy-start.6 = (f32[2,320,128]{2,1,0:T(8,128)S(1)}, f32[2,320,128]{2,1,0:T(8,128)}, u32[]{:S(2)}) copy-start(f32[2,320,128]{2,1,0:T(8,128)} %refs_5_.1) | copy-start | bytes 983044
  23.9 3.6 %collective-permute-start.7 = (f32[1,128]{1,0:T(1,128)S(1)}, f32[1,128]{1,0:T(1,128)S(1)}, u32[]{:S(2)}, u32[]{:S(2)}) collective-permute-start(f32[1,128]{1,0:T(1,128)S(1)} %get-tuple-element.29.refs_0_), channel_id=1, source_target_pairs={{0,2},{2,0},{4,6},{6,4},{8,10},{10,8},{12,14},{14,12},{1,3},{3,1},... | collective-permute-start | bytes 1544 | tf_op jit(solution)/shard_map/ppermute | solution.py:518
  27.5 3.6 %collective-permute-start.8 = (f32[2,128]{1,0:T(2,128)S(1)}, f32[2,128]{1,0:T(2,128)S(1)}, u32[]{:S(2)}, u32[]{:S(2)}) collective-permute-start(f32[2,128]{1,0:T(2,128)S(1)} %pad_maximum_fusion.2), channel_id=1, source_target_pairs={{0,4},{2,6},{4,0},{6,2},{8,12},{10,14},{12,8},{14,10},{1,5},{3,7},... | collective-permute-start | bytes 3080 | tf_op jit(solution)/shard_map/ppermute | solution.py:518
  31.1 4.5 %collective-permute-start.9 = (f32[4,128]{1,0:T(4,128)S(1)}, f32[4,128]{1,0:T(4,128)S(1)}, u32[]{:S(2)}, u32[]{:S(2)}) collective-permute-start(f32[4,128]{1,0:T(4,128)S(1)} %pad_maximum_fusion.1), channel_id=1, source_target_pairs={{0,8},{2,10},{4,12},{6,14},{8,0},{10,2},{12,4},{14,6},{1,9},{3,11}... | collective-permute-start | bytes 6152 | tf_op jit(solution)/shard_map/ppermute | solution.py:518
  35.6 1.2 %collective-permute-start.10 = (f32[8,128]{1,0:T(8,128)S(1)}, f32[8,128]{1,0:T(8,128)S(1)}, u32[]{:S(2)}, u32[]{:S(2)}) collective-permute-start(f32[8,128]{1,0:T(8,128)S(1)} %pad_maximum_fusion), channel_id=1, source_target_pairs={{0,1},{1,0},{2,3},{3,2},{4,5},{5,4},{6,7},{7,6},{8,9},{9,8},{10,11... | collective-permute-start | bytes 12296 | tf_op jit(solution)/shard_map/ppermute | solution.py:518

commit v4 on v3

--- a/solution.py
+++ b/solution.py
@@ -534,11 +534,11 @@
     return found
 
 
-def strip_swap(value, distance):
+def strip_swap(value, distance, alone=False):
     members, count, halves = (lax.axis_size(axis) for axis in ("member", "lon", "lat"))
     number = lambda m, i, t: (m * count + i) * halves + t
     other = lambda m, i, t: number(m, i ^ distance, t) if t or members % 2 else number(m ^ 1, i, t)
-    places = [(m, i, t) for m in range(members) for i in range(count) for t in range(halves)]
+    places = [(m, i, t) for m in range(members) for i in range(count) for t in range(int(alone), halves)]
     return lax.ppermute(value, ("member", "lon", "lat"), [(number(*p), other(*p)) for p in places])
 
 
@@ -556,7 +556,7 @@
     fields = (direction, land_sea, precision_weight, east_kappa, north_kappa)
     strip, edge, partner = rows_to_send(*fields, fold_partner.reshape(count, LANES))
     rows_in = swapped(edge, "lat", 1)
-    strip2 = strip_swap(strip, count // 2)
+    strip2 = strip_swap(strip, count // 2, True)
     pay1, pay2, strips = columns_to_send(*fields, rows_in, strip, strip2)
     halo2 = odd_pairs(pay2, "lon")
     halo1 = swapped(pay1, "lon", 1)

time: 38.3 us -> 36.4 us (0.950)
  waiting for transfers between devices: 15.4 us -> 13.6 us
    ppermute x4, waiting for transfers between devices: 1.86 us -> 0.01 us  [strip_swap(): lax.ppermute(value, ('member', 'lon', 'lat'), [(number(*p), other(*p)) fo...]
    ppermute x4, starting transfers between devices: 6.68 us -> 5.58 us  [strip_swap(): lax.ppermute(value, ('member', 'lon', 'lat'), [(number(*p), other(*p)) fo...]
    ppermute x6, starting transfers between devices: 3.14 us -> 4.1 us  [swapped(): lax.ppermute(value, axis, [(i, i ^ distance) for i in range(lax.axis_size...]
where the time goes in v4:
time: 36.4 us; the launch traced here: 36.2 us
  waiting for transfers between devices  13.6 us (37%)
  starting transfers between devices  13.2 us (36%)
  Pallas kernels  8.5 us (23%)
  between operations  0.79 us (2%)
    ppermute x6, waiting for transfers between devices, swapped(): lax.ppermute(value, axis, [(i, i ^ distance) for i in range(lax.axis_size...  11.9 us
    ppermute x4, starting transfers between devices, strip_swap(): lax.ppermute(value, ('member', 'lon', 'lat'), [(number(*p), other(*p)) fo...  5.58 us
    pallas_call x1, Pallas kernels, image_and_stats(): pl.pallas_call(kernel, out_shape=[jax.ShapeDtypeStruct(d.shape, f32), jax...  4.77 us
    ppermute x6, starting transfers between devices, swapped(): lax.ppermute(value, axis, [(i, i ^ distance) for i in range(lax.axis_size...  4.1 us
    ppermute x1, starting transfers between devices, odd_pairs(): return lax.ppermute(value, axis, pairs)  3.54 us
    ppermute x1, waiting for transfers between devices, odd_pairs(): return lax.ppermute(value, axis, pairs)  1.71 us
    pallas_call x1, Pallas kernels, update(): pl.pallas_call(functools.partial(update_kernel, len(parts)), out_shape=[j...  1.19 us
    pallas_call x1, Pallas kernels, coefficients(): pl.pallas_call(functools.partial(coefficient_kernel, 'lon', 'lat'), out_s...  1.17 us
  transfers between devices with their start and end apart: 11, of which 6 were waited for; matrix products, arithmetic and copies ran while one was open for 0% of the time, Pallas kernels for 3%

profile of v4, /device:TPU:0, one launch (start us, length us, event | category | flops | bytes accessed | tf_op | source)
XLA Modules:
  0.0 36.2 jit_solution(14214556257552537526)
XLA Ops:
  0.6 0.0 copy-start
  0.6 0.0 copy-start.1
  0.7 0.0 copy-start.2
  0.7 0.0 copy-start.3
  0.7 0.0 copy-start.4
  0.7 1.0 %shard_map.103 = (f32[56,128]{1,0:T(8,128)S(1)}, f32[8,8,128]{2,1,0:T(8,128)S(1)}, s32[8,128]{1,0:T(8,128)S(1)}) custom-call(f32[2,320,128]{2,1,0:T(8,128)} %refs_7_.1, s32[2,320,128]{2,1,0:T(8,128)} %refs_1_.1, f32[2,320,128]{2,1,0:T(8,128)} %pw.5, f32[320,128]{1,0:T(8,128)} %ek.5, f32[320,128]{1,0:T(8,128)} %nk.5, s32[8,128]{1,0:T(8,128)} %bitcast.1), custom_call_target="tpu_custom_call" | custom-call | tf_op jit(solution)/shard_map/pallas_call | solution.py:69
  1.7 0.5 %collective-permute-start = (f32[8,8,128]{2,1,0:T(8,128)S(1)}, f32[8,8,128]{2,1,0:T(8,128)S(1)}, u32[]{:S(2)}, u32[]{:S(2)}) collective-permute-start(f32[8,8,128]{2,1,0:T(8,128)S(1)} %get-tuple-element.17), channel_id=1, source_target_pairs={{0,1},{1,0},{2,3},{3,2},{4,5},{5,4},{6,7},{7,6},{8,9},{9,8},{10,11... | collective-permute-start | bytes 98312 | tf_op jit(solution)/shard_map/ppermute | solution.py:518
  2.2 0.7 %collective-permute-start.1 = (f32[56,128]{1,0:T(8,128)S(1)}, f32[56,128]{1,0:T(8,128)S(1)}, u32[]{:S(2)}, u32[]{:S(2)}) collective-permute-start(f32[56,128]{1,0:T(8,128)S(1)} %get-tuple-element.18.strip1), channel_id=1, source_target_pairs={{1,9},{3,11},{5,13},{7,15},{9,1},{11,3},{13,5},{15,7},{17,25},{19,... | collective-permute-start | bytes 86024 | tf_op jit(solution)/shard_map/ppermute | solution.py:542
  2.8 0.0 collective-permute-done.1.strip2
  2.9 0.2 collective-permute-done.rows_in
  3.0 0.0 copy-done
  3.0 0.0 copy-done.1
  3.0 0.0 copy-done.2
  3.1 0.0 copy-done.3
  3.1 0.0 copy-done.4
  3.1 0.4 %shard_map.104 = (f32[168,128]{1,0:T(8,128)S(1)}, f32[168,128]{1,0:T(8,128)S(1)}, f32[112,128]{1,0:T(8,128)S(1)}) custom-call(f32[2,320,128]{2,1,0:T(8,128)S(1)} %copy-done, s32[2,320,128]{2,1,0:T(8,128)S(1)} %copy-done.1, f32[2,320,128]{2,1,0:T(8,128)S(1)} %copy-done.2, f32[320,128]{1,0:T(8,128)S(1)} %copy-done.3, f32[320,128]{1,0:T(8,128)S(1)} %copy-done.4, ...), custom_call_target="tpu_custom_call" | custom-call | tf_op jit(solution)/shard_map/pallas_call | solution.py:127
  3.5 2.9 %collective-permute-start.4 = (f32[112,128]{1,0:T(8,128)S(1)}, f32[112,128]{1,0:T(8,128)S(1)}, u32[]{:S(2)}, u32[]{:S(2)}) collective-permute-start(f32[112,128]{1,0:T(8,128)S(1)} %get-tuple-element.28.refs_10_), channel_id=1, source_target_pairs={{0,16},{1,5},{2,18},{3,7},{4,20},{5,1},{6,22},{7,3},{8,24},{9,13},... | collective-permute-start | bytes 172040 | tf_op jit(solution)/shard_map/ppermute | solution.py:542
  6.4 1.5 %collective-permute-start.2 = (f32[168,128]{1,0:T(8,128)S(1)}, f32[168,128]{1,0:T(8,128)S(1)}, u32[]{:S(2)}, u32[]{:S(2)}) collective-permute-start(f32[168,128]{1,0:T(8,128)S(1)} %get-tuple-element.19), channel_id=1, source_target_pairs={{0,2},{2,0},{4,6},{6,4},{8,10},{10,8},{12,14},{14,12},{1,3},{3,1},... | collective-permute-start | bytes 258056 | tf_op jit(solution)/shard_map/ppermute | solution.py:518
  7.9 0.0 copy-start.5
  7.9 3.5 %collective-permute-start.3 = (f32[168,128]{1,0:T(8,128)S(1)}, f32[168,128]{1,0:T(8,128)S(1)}, u32[]{:S(2)}, u32[]{:S(2)}) collective-permute-start(f32[168,128]{1,0:T(8,128)S(1)} %get-tuple-element.20), channel_id=1, source_target_pairs={{2,4},{4,2},{6,8},{8,6},{10,12},{12,10},{14,0},{0,14},{3,5},{5,3},... | collective-permute-start | bytes 258056 | tf_op jit(solution)/shard_map/ppermute | solution.py:526
  11.4 0.5 %collective-permute-start.5 = (f32[112,128]{1,0:T(8,128)S(1)}, f32[112,128]{1,0:T(8,128)S(1)}, u32[]{:S(2)}, u32[]{:S(2)}) collective-permute-start(f32[112,128]{1,0:T(8,128)S(1)} %get-tuple-element.28.refs_10_), channel_id=1, source_target_pairs={{0,16},{1,3},{2,18},{3,1},{4,20},{5,7},{6,22},{7,5},{8,24},{9,11},... | collective-permute-start | bytes 172040 | tf_op jit(solution)/shard_map/ppermute | solution.py:542
  12.0 0.0 collective-permute-done.4.refs_11_
  12.0 1.5 %collective-permute-start.6 = (f32[112,128]{1,0:T(8,128)S(1)}, f32[112,128]{1,0:T(8,128)S(1)}, u32[]{:S(2)}, u32[]{:S(2)}) collective-permute-start(f32[112,128]{1,0:T(8,128)S(1)} %collective-permute-done.4.refs_11_), channel_id=1, source_target_pairs={{0,16},{1,3},{2,18},{3,1},{4,20},{5,7},{6,22},{7,5},{8,24},{9,11},... | collective-permute-start | bytes 172040 | tf_op jit(solution)/shard_map/ppermute | solution.py:542
  13.5 0.0 collective-permute-done.2.halo1
  13.5 1.7 %collective-permute-done.3.halo2 = f32[168,128]{1,0:T(8,128)S(1)} collective-permute-done((f32[168,128]{1,0:T(8,128)S(1)}, f32[168,128]{1,0:T(8,128)S(1)}, u32[]{:S(2)}, u32[]{:S(2)}) %collective-permute-start.3) | collective-permute-done | bytes 86048 | tf_op jit(solution)/shard_map/ppermute | solution.py:526
  15.2 1.2 %shard_map.105 = (f32[3,352,128]{2,1,0:T(8,128)S(1)}, f32[3,352,128]{2,1,0:T(8,128)S(1)}, f32[3,352,128]{2,1,0:T(8,128)S(1)}, f32[3,352,128]{2,1,0:T(8,128)S(1)}...) custom-call(f32[2,320,128]{2,1,0:T(8,128)S(1)} %copy-done, s32[2,320,128]{2,1,0:T(8,128)S(1)} %copy-done.1, ...), custom_call_target="tpu_custom_call" | custom-call | tf_op jit(solution)/shard_map/pallas_call | solution.py:258
  16.4 0.0 collective-permute-done.5.refs_12_
  16.4 0.0 collective-permute-done.6.refs_13_
  16.4 0.0 copy-done.5
  16.4 0.0 copy-start.6
  16.4 4.8 %shard_map.106 = (f32[2,320,128]{2,1,0:T(8,128)S(1)}, f32[1,128]{1,0:T(1,128)S(1)}) custom-call(f32[2,320,128]{2,1,0:T(8,128)S(1)} %copy-done, s32[2,320,128]{2,1,0:T(8,128)S(1)} %copy-done.1, f32[2,320,128]{2,1,0:T(8,128)S(1)} %copy-done.5, f32[3,352,128]{2,1,0:T(8,128)S(1)} %get-tuple-element.21.refs_3_, f32[3,352,128]{2,1,0:T(8,128)S(1)} %get-tuple-element.22.refs_4_, ...), custom_call_target="tpu_custom_call" | custom-call | tf_op jit(solution)/shard_map/pallas_call | solution.py:452
  21.2 0.1 collective-permute-start.7
  21.3 3.5 %collective-permute-done.7.refs_1_ = f32[1,128]{1,0:T(1,128)S(1)} collective-permute-done((f32[1,128]{1,0:T(1,128)S(1)}, f32[1,128]{1,0:T(1,128)S(1)}, u32[]{:S(2)}, u32[]{:S(2)}) %collective-permute-start.7) | collective-permute-done | bytes 544 | tf_op jit(solution)/shard_map/ppermute | solution.py:518
  24.8 0.0 collective-permute-start.8
  24.8 3.6 %collective-permute-done.8.refs_2_ = f32[2,128]{1,0:T(2,128)S(1)} collective-permute-done((f32[2,128]{1,0:T(2,128)S(1)}, f32[2,128]{1,0:T(2,128)S(1)}, u32[]{:S(2)}, u32[]{:S(2)}) %collective-permute-start.8) | collective-permute-done | bytes 1056 | tf_op jit(solution)/shard_map/ppermute | solution.py:518
  28.4 0.8 %collective-permute-start.9 = (f32[4,128]{1,0:T(4,128)S(1)}, f32[4,128]{1,0:T(4,128)S(1)}, u32[]{:S(2)}, u32[]{:S(2)}) collective-permute-start(f32[4,128]{1,0:T(4,128)S(1)} %pad_maximum_fusion.1), channel_id=1, source_target_pairs={{0,8},{2,10},{4,12},{6,14},{8,0},{10,2},{12,4},{14,6},{1,9},{3,11}... | collective-permute-start | bytes 6152 | tf_op jit(solution)/shard_map/ppermute | solution.py:518
  29.1 3.8 %collective-permute-done.9.refs_3_ = f32[4,128]{1,0:T(4,128)S(1)} collective-permute-done((f32[4,128]{1,0:T(4,128)S(1)}, f32[4,128]{1,0:T(4,128)S(1)}, u32[]{:S(2)}, u32[]{:S(2)}) %collective-permute-start.9) | collective-permute-done | bytes 2080 | tf_op jit(solution)/shard_map/ppermute | solution.py:518
  32.9 1.2 %collective-permute-start.10 = (f32[8,128]{1,0:T(8,128)S(1)}, f32[8,128]{1,0:T(8,128)S(1)}, u32[]{:S(2)}, u32[]{:S(2)}) collective-permute-start(f32[8,128]{1,0:T(8,128)S(1)} %pad_maximum_fusion), channel_id=1, source_target_pairs={{0,1},{1,0},{2,3},{3,2},{4,5},{5,4},{6,7},{7,6},{8,9},{9,8},{10,11... | collective-permute-start | bytes 12296 | tf_op jit(solution)/shard_map/ppermute | solution.py:518
  34.2 0.8 %collective-permute-done.10.refs_4_ = f32[8,128]{1,0:T(8,128)S(1)} collective-permute-done((f32[8,128]{1,0:T(8,128)S(1)}, f32[8,128]{1,0:T(8,128)S(1)}, u32[]{:S(2)}, u32[]{:S(2)}) %collective-permute-start.10) | collective-permute-done | bytes 4128 | tf_op jit(solution)/shard_map/ppermute | solution.py:518
  35.0 0.0 copy-done.6
  35.0 1.2 %shard_map.107 = (f32[2,320,128]{2,1,0:T(8,128)}, f32[2,320,128]{2,1,0:T(8,128)}, f32[2,320,128]{2,1,0:T(8,128)}) custom-call(f32[1,128]{1,0:T(1,128)S(1)} %get-tuple-element.29.refs_0_, f32[1,128]{1,0:T(1,128)S(1)} %collective-permute-done.7.refs_1_, f32[2,128]{1,0:T(2,128)S(1)} %collective-permute-done.8.refs_2_, ...), custom_call_target="tpu_custom_call" | custom-call | tf_op jit(solution)/shard_map/pallas_call | solution.py:507
  (3 shorter events, 0.0 us)
Async XLA Ops:
  0.6 2.4 %copy-start = (f32[2,320,128]{2,1,0:T(8,128)S(1)}, f32[2,320,128]{2,1,0:T(8,128)}, u32[]{:S(2)}) copy-start(f32[2,320,128]{2,1,0:T(8,128)} %refs_7_.1) | copy-start | bytes 983044
  0.6 2.4 %copy-start.1 = (s32[2,320,128]{2,1,0:T(8,128)S(1)}, s32[2,320,128]{2,1,0:T(8,128)}, u32[]{:S(2)}) copy-start(s32[2,320,128]{2,1,0:T(8,128)} %refs_1_.1) | copy-start | bytes 983044
  0.7 2.4 %copy-start.2 = (f32[2,320,128]{2,1,0:T(8,128)S(1)}, f32[2,320,128]{2,1,0:T(8,128)}, u32[]{:S(2)}) copy-start(f32[2,320,128]{2,1,0:T(8,128)} %pw.5) | copy-start | bytes 983044
  0.7 2.4 %copy-start.3 = (f32[320,128]{1,0:T(8,128)S(1)}, f32[320,128]{1,0:T(8,128)}, u32[]{:S(2)}) copy-start(f32[320,128]{1,0:T(8,128)} %ek.5) | copy-start | bytes 491524
  0.7 2.4 %copy-start.4 = (f32[320,128]{1,0:T(8,128)S(1)}, f32[320,128]{1,0:T(8,128)}, u32[]{:S(2)}) copy-start(f32[320,128]{1,0:T(8,128)} %nk.5) | copy-start | bytes 491524
  1.7 1.4 %collective-permute-start = (f32[8,8,128]{2,1,0:T(8,128)S(1)}, f32[8,8,128]{2,1,0:T(8,128)S(1)}, u32[]{:S(2)}, u32[]{:S(2)}) collective-permute-start(f32[8,8,128]{2,1,0:T(8,128)S(1)} %get-tuple-element.17), channel_id=1, source_target_pairs={{0,1},{1,0},{2,3},{3,2},{4,5},{5,4},{6,7},{7,6},{8,9},{9,8},{10,11... | collective-permute-start | bytes 98312 | tf_op jit(solution)/shard_map/ppermute | solution.py:518
  2.2 0.7 %collective-permute-start.1 = (f32[56,128]{1,0:T(8,128)S(1)}, f32[56,128]{1,0:T(8,128)S(1)}, u32[]{:S(2)}, u32[]{:S(2)}) collective-permute-start(f32[56,128]{1,0:T(8,128)S(1)} %get-tuple-element.18.strip1), channel_id=1, source_target_pairs={{1,9},{3,11},{5,13},{7,15},{9,1},{11,3},{13,5},{15,7},{17,25},{19,... | collective-permute-start | bytes 86024 | tf_op jit(solution)/shard_map/ppermute | solution.py:542
  3.5 8.5 %collective-permute-start.4 = (f32[112,128]{1,0:T(8,128)S(1)}, f32[112,128]{1,0:T(8,128)S(1)}, u32[]{:S(2)}, u32[]{:S(2)}) collective-permute-start(f32[112,128]{1,0:T(8,128)S(1)} %get-tuple-element.28.refs_10_), channel_id=1, source_target_pairs={{0,16},{1,5},{2,18},{3,7},{4,20},{5,1},{6,22},{7,3},{8,24},{9,13},... | collective-permute-start | bytes 172040 | tf_op jit(solution)/shard_map/ppermute | solution.py:542
  6.4 7.1 %collective-permute-start.2 = (f32[168,128]{1,0:T(8,128)S(1)}, f32[168,128]{1,0:T(8,128)S(1)}, u32[]{:S(2)}, u32[]{:S(2)}) collective-permute-start(f32[168,128]{1,0:T(8,128)S(1)} %get-tuple-element.19), channel_id=1, source_target_pairs={{0,2},{2,0},{4,6},{6,4},{8,10},{10,8},{12,14},{14,12},{1,3},{3,1},... | collective-permute-start | bytes 258056 | tf_op jit(solution)/shard_map/ppermute | solution.py:518
  7.9 8.5 %copy-start.5 = (f32[2,320,128]{2,1,0:T(8,128)S(1)}, f32[2,320,128]{2,1,0:T(8,128)}, u32[]{:S(2)}) copy-start(f32[2,320,128]{2,1,0:T(8,128)} %refs_6_.1) | copy-start | bytes 983044
  7.9 7.3 %collective-permute-start.3 = (f32[168,128]{1,0:T(8,128)S(1)}, f32[168,128]{1,0:T(8,128)S(1)}, u32[]{:S(2)}, u32[]{:S(2)}) collective-permute-start(f32[168,128]{1,0:T(8,128)S(1)} %get-tuple-element.20), channel_id=1, source_target_pairs={{2,4},{4,2},{6,8},{8,6},{10,12},{12,10},{14,0},{0,14},{3,5},{5,3},... | collective-permute-start | bytes 258056 | tf_op jit(solution)/shard_map/ppermute | solution.py:526
  11.4 4.9 %collective-permute-start.5 = (f32[112,128]{1,0:T(8,128)S(1)}, f32[112,128]{1,0:T(8,128)S(1)}, u32[]{:S(2)}, u32[]{:S(2)}) collective-permute-start(f32[112,128]{1,0:T(8,128)S(1)} %get-tuple-element.28.refs_10_), channel_id=1, source_target_pairs={{0,16},{1,3},{2,18},{3,1},{4,20},{5,7},{6,22},{7,5},{8,24},{9,11},... | collective-permute-start | bytes 172040 | tf_op jit(solution)/shard_map/ppermute | solution.py:542
  12.0 4.4 %collective-permute-start.6 = (f32[112,128]{1,0:T(8,128)S(1)}, f32[112,128]{1,0:T(8,128)S(1)}, u32[]{:S(2)}, u32[]{:S(2)}) collective-permute-start(f32[112,128]{1,0:T(8,128)S(1)} %collective-permute-done.4.refs_11_), channel_id=1, source_target_pairs={{0,16},{1,3},{2,18},{3,1},{4,20},{5,7},{6,22},{7,5},{8,24},{9,11},... | collective-permute-start | bytes 172040 | tf_op jit(solution)/shard_map/ppermute | solution.py:542
  16.4 18.6 %copy-start.6 = (f32[2,320,128]{2,1,0:T(8,128)S(1)}, f32[2,320,128]{2,1,0:T(8,128)}, u32[]{:S(2)}) copy-start(f32[2,320,128]{2,1,0:T(8,128)} %refs_5_.1) | copy-start | bytes 983044
  21.2 3.6 %collective-permute-start.7 = (f32[1,128]{1,0:T(1,128)S(1)}, f32[1,128]{1,0:T(1,128)S(1)}, u32[]{:S(2)}, u32[]{:S(2)}) collective-permute-start(f32[1,128]{1,0:T(1,128)S(1)} %get-tuple-element.29.refs_0_), channel_id=1, source_target_pairs={{0,2},{2,0},{4,6},{6,4},{8,10},{10,8},{12,14},{14,12},{1,3},{3,1},... | collective-permute-start | bytes 1544 | tf_op jit(solution)/shard_map/ppermute | solution.py:518
  24.8 3.6 %collective-permute-start.8 = (f32[2,128]{1,0:T(2,128)S(1)}, f32[2,128]{1,0:T(2,128)S(1)}, u32[]{:S(2)}, u32[]{:S(2)}) collective-permute-start(f32[2,128]{1,0:T(2,128)S(1)} %pad_maximum_fusion.2), channel_id=1, source_target_pairs={{0,4},{2,6},{4,0},{6,2},{8,12},{10,14},{12,8},{14,10},{1,5},{3,7},... | collective-permute-start | bytes 3080 | tf_op jit(solution)/shard_map/ppermute | solution.py:518
  28.4 4.5 %collective-permute-start.9 = (f32[4,128]{1,0:T(4,128)S(1)}, f32[4,128]{1,0:T(4,128)S(1)}, u32[]{:S(2)}, u32[]{:S(2)}) collective-permute-start(f32[4,128]{1,0:T(4,128)S(1)} %pad_maximum_fusion.1), channel_id=1, source_target_pairs={{0,8},{2,10},{4,12},{6,14},{8,0},{10,2},{12,4},{14,6},{1,9},{3,11}... | collective-permute-start | bytes 6152 | tf_op jit(solution)/shard_map/ppermute | solution.py:518
  32.9 2.1 %collective-permute-start.10 = (f32[8,128]{1,0:T(8,128)S(1)}, f32[8,128]{1,0:T(8,128)S(1)}, u32[]{:S(2)}, u32[]{:S(2)}) collective-permute-start(f32[8,128]{1,0:T(8,128)S(1)} %pad_maximum_fusion), channel_id=1, source_target_pairs={{0,1},{1,0},{2,3},{3,2},{4,5},{5,4},{6,7},{7,6},{8,9},{9,8},{10,11... | collective-permute-start | bytes 12296 | tf_op jit(solution)/shard_map/ppermute | solution.py:518

commit v5 on v4

--- a/solution.py
+++ b/solution.py
@@ -12,7 +12,6 @@
 LANES = 128
 VMEM_LIMIT = 24 * 1024 * 1024
 PAY_ROWS = 168
-STEP_CHUNK = 42
 f32 = jnp.float32
 
 
@@ -134,20 +133,7 @@
 
 
 def slab_index(group, shift=0):
-    if isinstance(group, int):
-        return slice(8 + 8 * group + shift, 16 + 8 * group + shift)
-    return pl.ds(pl.multiple_of(8 * group, 8) + 8 + shift, 8)
-
-
-def over_groups(count, chunk, body):
-    def turn_of(i, carry):
-        for k in range(chunk):
-            body(i * chunk + k)
-        return carry
-
-    lax.fori_loop(0, count // chunk, turn_of, 0)
-    for group in range(count - count % chunk, count):
-        body(group)
+    return slice(8 + 8 * group + shift, 16 + 8 * group + shift)
 
 
 def east_of(x):
@@ -171,7 +157,7 @@
 
 
 def coefficient_kernel(
-    lon_axis, lat_axis, d, sea, pw, ek, nk, halo1, halo2, rows_in, field, weight, east_c, west_c, north_c, centre, ocean
+    lon_axis, lat_axis, d, sea, pw, ek, nk, halo1, halo2, rows_in, field, weight, east_c, west_c, north_c, ocean
 ):
     top = lax.axis_index(lat_axis) == 1
     even = lax.axis_index(lon_axis) % 2 == 0
@@ -244,40 +230,37 @@
             west_c[s, here, :] = oc[s] * w[s]
             north_c[s, here, :] = north_c[s, here, :] * ocean[s, at(group, 1), :]
 
-    for group in range(groups + 2):
-        for s in range(3):
-            here = at(group)
-            centre[s, here, :] = (
-                1.0 - east_c[s, here, :] - west_c[s, here, :] - north_c[s, here, :] - north_c[s, at(group, -1), :]
-            )
-
 
 def coefficients(d, sea, pw, ek, nk, halo1, halo2, rows_in):
     full = pl.BlockSpec(memory_space=pltpu.VMEM)
     extended = (3, d.shape[1] + 32, LANES)
     return pl.pallas_call(
         functools.partial(coefficient_kernel, "lon", "lat"),
-        out_shape=[jax.ShapeDtypeStruct(extended, f32)] * 6,
+        out_shape=[jax.ShapeDtypeStruct(extended, f32)] * 5,
         in_specs=[full] * 8,
-        out_specs=[full] * 6,
+        out_specs=[full] * 5,
         scratch_shapes=[pltpu.VMEM(extended, f32)],
         compiler_params=pltpu.CompilerParams(vmem_limit_bytes=VMEM_LIMIT),
     )(d, sea, pw, ek, nk, halo1, halo2, rows_in)
 
 
-def image_kernel(
-    offsets, lon_axis, lat_axis,
-    d, sea, res, first_field, weight, east_c, west_c, north_c, centre, partner, gathered_pieces,
-    image, stats,
-    blocks, folds, face_fold, field, other,
-):
+def strip_kernel(offsets, lon_axis, lat_axis, partner, gathered_pieces, beyond_out, face_out, blocks):
     lon = lax.axis_index(lon_axis)
     count = len(offsets)
+
     top = lax.axis_index(lat_axis) == 1
-    groups = d.shape[1] // 8
-    zero = jnp.zeros((8, LANES), f32)
-    at = slab_index
-
+
+    @pl.when(jnp.logical_not(top))
+    def _():
+        beyond_out[...] = jnp.zeros(beyond_out.shape, f32)
+        face_out[...] = jnp.zeros(face_out.shape, f32)
+
+    @pl.when(top)
+    def _():
+        strip_steps(lon, count, offsets, partner, gathered_pieces, beyond_out, face_out, blocks)
+
+
+def strip_steps(lon, count, offsets, partner, gathered_pieces, beyond_out, face_out, blocks):
     slot = 0
     for piece in gathered_pieces:
         for inside in range(piece.shape[0] // STRIP):
@@ -311,64 +294,92 @@
             parts.append(total)
         return parts[0] if len(parts) == 1 else jnp.concatenate(parts, axis=0)
 
-    @pl.when(top)
-    def _():
-        east_k = [strip_row(6, r) for r in range(HALO)]
-        north_k = [strip_row(7, r) for r in range(HALO)]
-        top_k = 0.5 * (north_k[-1] + across(north_k[-1]))
-        both = range(2)
-        oc = [[strip_row(2 + level, r) for r in range(HALO)] for level in both]
-        u = [[strip_row(level, r) * oc[level][r] for r in range(HALO)] for level in both]
-        oc_east = strip_shift([x for level in both for x in oc[level]], True)
-        e = [[east_k[r] * oc[level][r] * oc_east[HALO * level + r] for r in range(HALO)] for level in both]
-        w = strip_shift([x for level in both for x in e[level]], False)
-        w = [w[:HALO], w[HALO:]]
-        n = [[north_k[r] * oc[level][r] * oc[level][r + 1] for r in range(HALO - 1)] for level in both]
-        for level in both:
-            n[level].append(top_k * oc[level][-1] * across(oc[level][-1]))
-            face_fold[level] = n[level][-1]
-        c = [
-            [None] + [1.0 - e[level][r] - w[level][r] - n[level][r] - n[level][r - 1] for r in range(1, HALO)]
-            for level in both
-        ]
-        for t in range(HALO):
-            if t == STEPS:
-                for level in both:
-                    for r in range(t, HALO):
-                        u[level][r] = strip_row(4 + level, r) * oc[level][r] * u[level][r]
-            beyond = [across(u[level][-1]) for level in both]
+    block_index = lax.broadcasted_iota(jnp.int32, (count, LANES), 0)
+    to_east = lax.rem(lon + 1, count)
+    to_west = lax.rem(lon + count - 1, count)
+    one = lanes_of((1, LANES))
+    last_only = lax.broadcasted_iota(jnp.int32, (8, LANES), 0) == 7
+
+    def write_rows(out, values):
+        row = lambda level, block: jnp.sum(jnp.where(block_index == block, values[level], 0.0), axis=0, keepdims=True)
+        here = [row(level, lon) for level in range(2)]
+        east = [row(level, to_east) for level in range(2)]
+        west = [row(level, to_west) for level in range(2)]
+        turned = [turn(x, 64) for x in (here[1], east[1], west[1])]
+        beside = jnp.where(one < 32, east[0], jnp.where(one >= 96, west[0], jnp.where(one >= 64, turned[1], turned[2])))
+        for s, value in enumerate((here[0], turned[0], beside)):
+            out[8 * s : 8 * s + 8, :] = jnp.where(last_only, jnp.broadcast_to(value, (8, LANES)), 0.0)
+
+    east_k = [strip_row(6, r) for r in range(HALO)]
+    north_k = [strip_row(7, r) for r in range(HALO)]
+    top_k = 0.5 * (north_k[-1] + across(north_k[-1]))
+    both = range(2)
+    oc = [[strip_row(2 + level, r) for r in range(HALO)] for level in both]
+    u = [[strip_row(level, r) * oc[level][r] for r in range(HALO)] for level in both]
+    oc_east = strip_shift([x for level in both for x in oc[level]], True)
+    e = [[east_k[r] * oc[level][r] * oc_east[HALO * level + r] for r in range(HALO)] for level in both]
+    w = strip_shift([x for level in both for x in e[level]], False)
+    w = [w[:HALO], w[HALO:]]
+    n = [[north_k[r] * oc[level][r] * oc[level][r + 1] for r in range(HALO - 1)] for level in both]
+    for level in both:
+        n[level].append(top_k * oc[level][-1] * across(oc[level][-1]))
+    write_rows(face_out, [n[0][-1], n[1][-1]])
+    c = [
+        [None] + [1.0 - e[level][r] - w[level][r] - n[level][r] - n[level][r - 1] for r in range(1, HALO)]
+        for level in both
+    ]
+    for t in range(HALO):
+        if t == STEPS:
             for level in both:
-                folds[t, level] = beyond[level]
-            if t == HALO - 1:
-                break
-            rest = [(level, r) for level in both for r in range(t + 1, HALO)]
-            east = strip_shift([u[level][r] for level, r in rest], True)
-            west = strip_shift([u[level][r] for level, r in rest], False)
-            new = [list(u[0]), list(u[1])]
-            for (level, r), ue, uw in zip(rest, east, west):
-                north = u[level][r + 1] if r + 1 < HALO else beyond[level]
-                new[level][r] = (
-                    c[level][r] * u[level][r]
-                    + e[level][r] * ue
-                    + w[level][r] * uw
-                    + n[level][r] * north
-                    + n[level][r - 1] * u[level][r - 1]
-                )
-            u = new
-
-    def fold_rows(read):
-        to_east = lax.rem(lon + 1, count)
-        to_west = lax.rem(lon + count - 1, count)
-        one = lanes_of((1, LANES))
-        here0 = read(0, lon)
-        here1 = turn(read(1, lon), 64)
-        e0, w0 = read(0, to_east), read(0, to_west)
-        e1, w1 = turn(read(1, to_east), 64), turn(read(1, to_west), 64)
-        beside = jnp.where(one < 32, e0, jnp.where(one >= 96, w0, jnp.where(one >= 64, e1, w1)))
-        return here0, here1, beside
-
+                for r in range(t, HALO):
+                    u[level][r] = strip_row(4 + level, r) * oc[level][r] * u[level][r]
+        beyond = [across(u[level][-1]) for level in both]
+        write_rows(beyond_out.at[t], beyond)
+        if t == HALO - 1:
+            break
+        rest = [(level, r) for level in both for r in range(t + 1, HALO)]
+        east = strip_shift([u[level][r] for level, r in rest], True)
+        west = strip_shift([u[level][r] for level, r in rest], False)
+        new = [list(u[0]), list(u[1])]
+        for (level, r), ue, uw in zip(rest, east, west):
+            north = u[level][r + 1] if r + 1 < HALO else beyond[level]
+            new[level][r] = (
+                c[level][r] * u[level][r]
+                + e[level][r] * ue
+                + w[level][r] * uw
+                + n[level][r] * north
+                + n[level][r - 1] * u[level][r - 1]
+            )
+        u = new
+
+
+def strip_rows(partner, pieces, offsets):
+    count = len(offsets)
+    full = pl.BlockSpec(memory_space=pltpu.VMEM)
+    inputs = [partner, *pieces]
+
+    def kernel(partner_ref, *refs):
+        strip_kernel(offsets, "lon", "lat", partner_ref, refs[: len(pieces)], *refs[len(pieces) :])
+
+    return pl.pallas_call(
+        kernel,
+        out_shape=[jax.ShapeDtypeStruct((HALO, 24, LANES), f32), jax.ShapeDtypeStruct((24, LANES), f32)],
+        in_specs=[full] * len(inputs),
+        out_specs=[full] * 2,
+        scratch_shapes=[pltpu.VMEM((STRIP * count, LANES), f32)],
+        compiler_params=pltpu.CompilerParams(vmem_limit_bytes=VMEM_LIMIT),
+    )(*inputs)
+
+
+def image_kernel(
+    d, sea, res, first_field, weight, east_c, west_c, north_c, beyond, face, image, stats, field, other
+):
+    groups = d.shape[1] // 8
+    zero = jnp.zeros((8, LANES), f32)
+    at = slab_index
+
+    first_row = lax.broadcasted_iota(jnp.int32, (8, LANES), 0) == 0
     last = groups + 2
-    fold_at = 8 + 8 * (groups + 1)
     for s in range(3):
         for buffer in (field, other):
             buffer[s, 0:8, :] = zero
@@ -377,28 +388,26 @@
             field[s, at(group), :] = first_field[s, at(group), :]
 
     def step(t, source, target):
-        def one_group(group):
-            here, up, down = at(group), at(group, 1), at(group, -1)
+        before = [zero] * 3
+        for group in range(groups + 2):
+            here, up = at(group), at(group, 1)
             u = [source[s, here, :] for s in range(3)]
             e, w = east_of(u), west_of(u)
             for s in range(3):
+                flux = north_c[s, here, :] * (source[s, up, :] - u[s])
+                if group == groups:
+                    fold = slice(8 * s, 8 * s + 8)
+                    flux = flux + face[fold, :] * (beyond[t, fold, :] - u[s])
+                moved = turn(flux, 1, 0)
+                below = jnp.where(first_row, before[s], moved)
+                before[s] = moved
                 target[s, here, :] = (
-                    centre[s, here, :] * u[s]
-                    + east_c[s, here, :] * e[s]
-                    + west_c[s, here, :] * w[s]
-                    + north_c[s, here, :] * source[s, up, :]
-                    + north_c[s, down, :] * source[s, down, :]
+                    u[s]
+                    + east_c[s, here, :] * (e[s] - u[s])
+                    - west_c[s, here, :] * (u[s] - w[s])
+                    + flux
+                    - below
                 )
-
-        over_groups(groups + 2, STEP_CHUNK, one_group)
-
-        @pl.when(top)
-        def _():
-            face = fold_rows(lambda level, b: face_fold[level, pl.ds(b, 1), :])
-            beyond = fold_rows(lambda level, b: folds[t, level, pl.ds(b, 1), :])
-            row = slice(fold_at - 1, fold_at)
-            for s in range(3):
-                target[s, row, :] = target[s, row, :] + face[s] * (beyond[s] - source[s, row, :])
 
     def two_steps(i, carry):
         @pl.when(2 * i == STEPS)
@@ -440,27 +449,15 @@
     stats[...] = row
 
 
-def image_and_stats(d, sea, res, coeffs, partner, pieces, offsets):
-    count = len(offsets)
+def image_and_stats(d, sea, res, coeffs, beyond, face):
     full = pl.BlockSpec(memory_space=pltpu.VMEM)
-    extended = coeffs[0].shape
-    inputs = [d, sea, res, *coeffs, partner, *pieces]
-
-    def kernel(*refs):
-        image_kernel(offsets, "lon", "lat", *refs[:10], refs[10 : len(inputs)], *refs[len(inputs) :])
-
+    inputs = [d, sea, res, *coeffs, beyond, face]
     return pl.pallas_call(
-        kernel,
+        image_kernel,
         out_shape=[jax.ShapeDtypeStruct(d.shape, f32), jax.ShapeDtypeStruct((1, LANES), f32)],
         in_specs=[full] * len(inputs),
         out_specs=[full] * 2,
-        scratch_shapes=[
-            pltpu.VMEM((STRIP * count, LANES), f32),
-            pltpu.VMEM((HALO, 2, count, LANES), f32),
-            pltpu.VMEM((2, count, LANES), f32),
-            pltpu.VMEM(extended, f32),
-            pltpu.VMEM(extended, f32),
-        ],
+        scratch_shapes=[pltpu.VMEM(coeffs[0].shape, f32)] * 2,
         compiler_params=pltpu.CompilerParams(vmem_limit_bytes=VMEM_LIMIT),
     )(*inputs)
 
@@ -565,7 +562,7 @@
     pieces += [strip_swap(piece, rest[-1]) for piece in pieces]
     offsets += [o ^ rest[-1] for o in offsets]
     coeffs = coefficients(*fields, halo1, halo2, rows_in)
-    image, stats = image_and_stats(direction, land_sea, residual, coeffs, partner, pieces, offsets)
+    image, stats = image_and_stats(direction, land_sea, residual, coeffs, *strip_rows(partner, pieces, offsets))
     parts, _ = butterfly([stats], [0], lambda value, distance: swapped(value, "lon", distance), distances(count)[::-1])
     parts.append(swapped(jnp.concatenate(parts, axis=0), "lat", 1))
     return tuple(update(parts, iterate, residual, direction, image))

time: 36.4 us -> 34.5 us (0.948)
  Pallas kernels: 8.5 us -> 7.2 us
  starting transfers between devices: 13.2 us -> 12.7 us
    pallas_call x1 -> x2, Pallas kernels: 4.77 us -> 3.48 us  [the longest x1 3.46 us: image_and_stats(): pl.pallas_call(image_kernel, out_shape=[jax.ShapeDtypeStruct(d.shape, f32...]
    ppermute x6, starting transfers between devices: 4.1 us -> 3.55 us  [swapped(): lax.ppermute(value, axis, [(i, i ^ distance) for i in range(lax.axis_size...]
where the time goes in v5:
time: 34.5 us; the launch traced here: 34.4 us
  waiting for transfers between devices  13.6 us (39%)
  starting transfers between devices  12.7 us (37%)
  Pallas kernels  7.2 us (21%)
  between operations  0.8 us (2%)
    ppermute x6, waiting for transfers between devices, swapped(): lax.ppermute(value, axis, [(i, i ^ distance) for i in range(lax.axis_size...  11.9 us
    ppermute x4, starting transfers between devices, strip_swap(): lax.ppermute(value, ('member', 'lon', 'lat'), [(number(*p), other(*p)) fo...  5.58 us
    ppermute x6, starting transfers between devices, swapped(): lax.ppermute(value, axis, [(i, i ^ distance) for i in range(lax.axis_size...  3.55 us
    ppermute x1, starting transfers between devices, odd_pairs(): return lax.ppermute(value, axis, pairs)  3.54 us
    pallas_call x1, Pallas kernels, image_and_stats(): pl.pallas_call(image_kernel, out_shape=[jax.ShapeDtypeStruct(d.shape, f32...  3.46 us
    ppermute x1, waiting for transfers between devices, odd_pairs(): return lax.ppermute(value, axis, pairs)  1.71 us
    pallas_call x1, Pallas kernels, update(): pl.pallas_call(functools.partial(update_kernel, len(parts)), out_shape=[j...  1.2 us
    pallas_call x1, Pallas kernels, coefficients(): pl.pallas_call(functools.partial(coefficient_kernel, 'lon', 'lat'), out_s...  1.15 us
  transfers between devices with their start and end apart: 11, of which 6 were waited for; matrix products, arithmetic and copies ran while one was open for 0% of the time, Pallas kernels for 3%

profile of v5, /device:TPU:0, one launch (start us, length us, event | category | flops | bytes accessed | tf_op | source)
XLA Modules:
  0.0 34.4 jit_solution(6439907731931807086)
XLA Ops:
  0.6 0.0 copy-start
  0.6 0.0 copy-start.1
  0.7 0.0 copy-start.2
  0.7 0.0 copy-start.3
  0.7 0.0 copy-start.4
  0.7 1.0 %shard_map.103 = (f32[56,128]{1,0:T(8,128)S(1)}, f32[8,8,128]{2,1,0:T(8,128)S(1)}, s32[8,128]{1,0:T(8,128)S(1)}) custom-call(f32[2,320,128]{2,1,0:T(8,128)} %refs_7_.1, s32[2,320,128]{2,1,0:T(8,128)} %sea.7, f32[2,320,128]{2,1,0:T(8,128)} %pw.5, f32[320,128]{1,0:T(8,128)} %ek.5, f32[320,128]{1,0:T(8,128)} %nk.5, s32[8,128]{1,0:T(8,128)} %bitcast.1), custom_call_target="tpu_custom_call" | custom-call | tf_op jit(solution)/shard_map/pallas_call | solution.py:68
  1.7 0.5 %collective-permute-start = (f32[8,8,128]{2,1,0:T(8,128)S(1)}, f32[8,8,128]{2,1,0:T(8,128)S(1)}, u32[]{:S(2)}, u32[]{:S(2)}) collective-permute-start(f32[8,8,128]{2,1,0:T(8,128)S(1)} %get-tuple-element.18), channel_id=1, source_target_pairs={{0,1},{1,0},{2,3},{3,2},{4,5},{5,4},{6,7},{7,6},{8,9},{9,8},{10,11... | collective-permute-start | bytes 98312 | tf_op jit(solution)/shard_map/ppermute | solution.py:515
  2.2 0.7 %collective-permute-start.1 = (f32[56,128]{1,0:T(8,128)S(1)}, f32[56,128]{1,0:T(8,128)S(1)}, u32[]{:S(2)}, u32[]{:S(2)}) collective-permute-start(f32[56,128]{1,0:T(8,128)S(1)} %get-tuple-element.19.strip1), channel_id=1, source_target_pairs={{1,9},{3,11},{5,13},{7,15},{9,1},{11,3},{13,5},{15,7},{17,25},{19,... | collective-permute-start | bytes 86024 | tf_op jit(solution)/shard_map/ppermute | solution.py:539
  2.8 0.0 collective-permute-done.1.strip2
  2.9 0.2 collective-permute-done.rows_in
  3.0 0.0 copy-done
  3.0 0.0 copy-done.1
  3.0 0.0 copy-done.2
  3.1 0.0 copy-done.3
  3.1 0.0 copy-done.4
  3.1 0.4 %shard_map.104 = (f32[168,128]{1,0:T(8,128)S(1)}, f32[168,128]{1,0:T(8,128)S(1)}, f32[112,128]{1,0:T(8,128)S(1)}) custom-call(f32[2,320,128]{2,1,0:T(8,128)S(1)} %copy-done, s32[2,320,128]{2,1,0:T(8,128)S(1)} %copy-done.1, f32[2,320,128]{2,1,0:T(8,128)S(1)} %copy-done.2, f32[320,128]{1,0:T(8,128)S(1)} %copy-done.3, f32[320,128]{1,0:T(8,128)S(1)} %copy-done.4, ...), custom_call_target="tpu_custom_call" | custom-call | tf_op jit(solution)/shard_map/pallas_call | solution.py:126
  3.5 2.9 %collective-permute-start.4 = (f32[112,128]{1,0:T(8,128)S(1)}, f32[112,128]{1,0:T(8,128)S(1)}, u32[]{:S(2)}, u32[]{:S(2)}) collective-permute-start(f32[112,128]{1,0:T(8,128)S(1)} %get-tuple-element.28.refs_0_), channel_id=1, source_target_pairs={{0,16},{1,5},{2,18},{3,7},{4,20},{5,1},{6,22},{7,3},{8,24},{9,13},... | collective-permute-start | bytes 172040 | tf_op jit(solution)/shard_map/ppermute | solution.py:539
  6.4 1.5 %collective-permute-start.2 = (f32[168,128]{1,0:T(8,128)S(1)}, f32[168,128]{1,0:T(8,128)S(1)}, u32[]{:S(2)}, u32[]{:S(2)}) collective-permute-start(f32[168,128]{1,0:T(8,128)S(1)} %get-tuple-element.20), channel_id=1, source_target_pairs={{0,2},{2,0},{4,6},{6,4},{8,10},{10,8},{12,14},{14,12},{1,3},{3,1},... | collective-permute-start | bytes 258056 | tf_op jit(solution)/shard_map/ppermute | solution.py:515
  7.9 3.5 %collective-permute-start.3 = (f32[168,128]{1,0:T(8,128)S(1)}, f32[168,128]{1,0:T(8,128)S(1)}, u32[]{:S(2)}, u32[]{:S(2)}) collective-permute-start(f32[168,128]{1,0:T(8,128)S(1)} %get-tuple-element.21), channel_id=1, source_target_pairs={{2,4},{4,2},{6,8},{8,6},{10,12},{12,10},{14,0},{0,14},{3,5},{5,3},... | collective-permute-start | bytes 258056 | tf_op jit(solution)/shard_map/ppermute | solution.py:523
  11.4 0.5 %collective-permute-start.5 = (f32[112,128]{1,0:T(8,128)S(1)}, f32[112,128]{1,0:T(8,128)S(1)}, u32[]{:S(2)}, u32[]{:S(2)}) collective-permute-start(f32[112,128]{1,0:T(8,128)S(1)} %get-tuple-element.28.refs_0_), channel_id=1, source_target_pairs={{0,16},{1,3},{2,18},{3,1},{4,20},{5,7},{6,22},{7,5},{8,24},{9,11},... | collective-permute-start | bytes 172040 | tf_op jit(solution)/shard_map/ppermute | solution.py:539
  12.0 0.0 collective-permute-done.4.refs_1_
  12.0 1.5 %collective-permute-start.6 = (f32[112,128]{1,0:T(8,128)S(1)}, f32[112,128]{1,0:T(8,128)S(1)}, u32[]{:S(2)}, u32[]{:S(2)}) collective-permute-start(f32[112,128]{1,0:T(8,128)S(1)} %collective-permute-done.4.refs_1_), channel_id=1, source_target_pairs={{0,16},{1,3},{2,18},{3,1},{4,20},{5,7},{6,22},{7,5},{8,24},{9,11},... | collective-permute-start | bytes 172040 | tf_op jit(solution)/shard_map/ppermute | solution.py:539
  13.5 0.0 collective-permute-done.2.halo1
  13.5 1.7 %collective-permute-done.3.halo2 = f32[168,128]{1,0:T(8,128)S(1)} collective-permute-done((f32[168,128]{1,0:T(8,128)S(1)}, f32[168,128]{1,0:T(8,128)S(1)}, u32[]{:S(2)}, u32[]{:S(2)}) %collective-permute-start.3) | collective-permute-done | bytes 86048 | tf_op jit(solution)/shard_map/ppermute | solution.py:523
  15.2 0.0 copy-start.5
  15.2 1.2 %shard_map.105 = (f32[3,352,128]{2,1,0:T(8,128)S(1)}, f32[3,352,128]{2,1,0:T(8,128)S(1)}, f32[3,352,128]{2,1,0:T(8,128)S(1)}, f32[3,352,128]{2,1,0:T(8,128)S(1)}, f32[3,352,128]{2,1,0:T(8,128)S(1)}) custom-call(f32[2,320,128]{2,1,0:T(8,128)S(1)} %copy-done, s32[2,320,128]{2,1,0:T(8,128)S(1)} %copy-done.1, f32[2,320,128]{2,1,0:T(8,128)S(1)} %copy-done.2, ...), custom_call_target="tpu_custom_call" | custom-call | tf_op jit(solution)/shard_map/pallas_call | solution.py:237
  16.3 0.0 collective-permute-done.5.refs_2_
  16.4 0.0 collective-permute-done.6.refs_3_
  16.4 0.0 copy-done.5
  16.4 0.0 copy-start.6
  16.4 3.5 %shard_map.107 = (f32[2,320,128]{2,1,0:T(8,128)S(1)}, f32[1,128]{1,0:T(1,128)S(1)}) custom-call(f32[2,320,128]{2,1,0:T(8,128)S(1)} %copy-done, s32[2,320,128]{2,1,0:T(8,128)S(1)} %copy-done.1, f32[2,320,128]{2,1,0:T(8,128)S(1)} %copy-done.5, f32[3,352,128]{2,1,0:T(8,128)S(1)} %get-tuple-element.22.first_field, f32[3,352,128]{2,1,0:T(8,128)S(1)} %get-tuple-element.23.weight, ...), custom_call_target="tpu_custom_call" | custom-call | tf_op jit(solution)/shard_map/pallas_call | solution.py:455
  19.9 0.1 collective-permute-start.7
  20.0 3.5 %collective-permute-done.7.refs_1_ = f32[1,128]{1,0:T(1,128)S(1)} collective-permute-done((f32[1,128]{1,0:T(1,128)S(1)}, f32[1,128]{1,0:T(1,128)S(1)}, u32[]{:S(2)}, u32[]{:S(2)}) %collective-permute-start.7) | collective-permute-done | bytes 544 | tf_op jit(solution)/shard_map/ppermute | solution.py:515
  23.5 0.0 collective-permute-start.8
  23.5 3.6 %collective-permute-done.8.refs_2_ = f32[2,128]{1,0:T(2,128)S(1)} collective-permute-done((f32[2,128]{1,0:T(2,128)S(1)}, f32[2,128]{1,0:T(2,128)S(1)}, u32[]{:S(2)}, u32[]{:S(2)}) %collective-permute-start.8) | collective-permute-done | bytes 1056 | tf_op jit(solution)/shard_map/ppermute | solution.py:515
  27.1 0.7 %collective-permute-start.9 = (f32[4,128]{1,0:T(4,128)S(1)}, f32[4,128]{1,0:T(4,128)S(1)}, u32[]{:S(2)}, u32[]{:S(2)}) collective-permute-start(f32[4,128]{1,0:T(4,128)S(1)} %pad_maximum_fusion.1), channel_id=1, source_target_pairs={{0,8},{2,10},{4,12},{6,14},{8,0},{10,2},{12,4},{14,6},{1,9},{3,11}... | collective-permute-start | bytes 6152 | tf_op jit(solution)/shard_map/ppermute | solution.py:515
  27.8 3.8 %collective-permute-done.9.refs_3_ = f32[4,128]{1,0:T(4,128)S(1)} collective-permute-done((f32[4,128]{1,0:T(4,128)S(1)}, f32[4,128]{1,0:T(4,128)S(1)}, u32[]{:S(2)}, u32[]{:S(2)}) %collective-permute-start.9) | collective-permute-done | bytes 2080 | tf_op jit(solution)/shard_map/ppermute | solution.py:515
  31.6 0.7 %collective-permute-start.10 = (f32[8,128]{1,0:T(8,128)S(1)}, f32[8,128]{1,0:T(8,128)S(1)}, u32[]{:S(2)}, u32[]{:S(2)}) collective-permute-start(f32[8,128]{1,0:T(8,128)S(1)} %pad_maximum_fusion), channel_id=1, source_target_pairs={{0,1},{1,0},{2,3},{3,2},{4,5},{5,4},{6,7},{7,6},{8,9},{9,8},{10,11... | collective-permute-start | bytes 12296 | tf_op jit(solution)/shard_map/ppermute | solution.py:515
  32.3 0.8 %collective-permute-done.10.refs_4_ = f32[8,128]{1,0:T(8,128)S(1)} collective-permute-done((f32[8,128]{1,0:T(8,128)S(1)}, f32[8,128]{1,0:T(8,128)S(1)}, u32[]{:S(2)}, u32[]{:S(2)}) %collective-permute-start.10) | collective-permute-done | bytes 4128 | tf_op jit(solution)/shard_map/ppermute | solution.py:515
  33.2 0.0 copy-done.6
  33.2 1.2 %shard_map.108 = (f32[2,320,128]{2,1,0:T(8,128)}, f32[2,320,128]{2,1,0:T(8,128)}, f32[2,320,128]{2,1,0:T(8,128)}) custom-call(f32[1,128]{1,0:T(1,128)S(1)} %get-tuple-element.31.refs_0_, f32[1,128]{1,0:T(1,128)S(1)} %collective-permute-done.7.refs_1_, f32[2,128]{1,0:T(2,128)S(1)} %collective-permute-done.8.refs_2_, ...), custom_call_target="tpu_custom_call" | custom-call | tf_op jit(solution)/shard_map/pallas_call | solution.py:504
  (4 shorter events, 0.1 us)
Async XLA Ops:
  0.6 2.4 %copy-start = (f32[2,320,128]{2,1,0:T(8,128)S(1)}, f32[2,320,128]{2,1,0:T(8,128)}, u32[]{:S(2)}) copy-start(f32[2,320,128]{2,1,0:T(8,128)} %refs_7_.1) | copy-start | bytes 983044
  0.6 2.4 %copy-start.1 = (s32[2,320,128]{2,1,0:T(8,128)S(1)}, s32[2,320,128]{2,1,0:T(8,128)}, u32[]{:S(2)}) copy-start(s32[2,320,128]{2,1,0:T(8,128)} %sea.7) | copy-start | bytes 983044
  0.7 2.4 %copy-start.2 = (f32[2,320,128]{2,1,0:T(8,128)S(1)}, f32[2,320,128]{2,1,0:T(8,128)}, u32[]{:S(2)}) copy-start(f32[2,320,128]{2,1,0:T(8,128)} %pw.5) | copy-start | bytes 983044
  0.7 2.4 %copy-start.3 = (f32[320,128]{1,0:T(8,128)S(1)}, f32[320,128]{1,0:T(8,128)}, u32[]{:S(2)}) copy-start(f32[320,128]{1,0:T(8,128)} %ek.5) | copy-start | bytes 491524
  0.7 2.4 %copy-start.4 = (f32[320,128]{1,0:T(8,128)S(1)}, f32[320,128]{1,0:T(8,128)}, u32[]{:S(2)}) copy-start(f32[320,128]{1,0:T(8,128)} %nk.5) | copy-start | bytes 491524
  1.7 1.4 %collective-permute-start = (f32[8,8,128]{2,1,0:T(8,128)S(1)}, f32[8,8,128]{2,1,0:T(8,128)S(1)}, u32[]{:S(2)}, u32[]{:S(2)}) collective-permute-start(f32[8,8,128]{2,1,0:T(8,128)S(1)} %get-tuple-element.18), channel_id=1, source_target_pairs={{0,1},{1,0},{2,3},{3,2},{4,5},{5,4},{6,7},{7,6},{8,9},{9,8},{10,11... | collective-permute-start | bytes 98312 | tf_op jit(solution)/shard_map/ppermute | solution.py:515
  2.2 0.7 %collective-permute-start.1 = (f32[56,128]{1,0:T(8,128)S(1)}, f32[56,128]{1,0:T(8,128)S(1)}, u32[]{:S(2)}, u32[]{:S(2)}) collective-permute-start(f32[56,128]{1,0:T(8,128)S(1)} %get-tuple-element.19.strip1), channel_id=1, source_target_pairs={{1,9},{3,11},{5,13},{7,15},{9,1},{11,3},{13,5},{15,7},{17,25},{19,... | collective-permute-start | bytes 86024 | tf_op jit(solution)/shard_map/ppermute | solution.py:539
  3.5 8.5 %collective-permute-start.4 = (f32[112,128]{1,0:T(8,128)S(1)}, f32[112,128]{1,0:T(8,128)S(1)}, u32[]{:S(2)}, u32[]{:S(2)}) collective-permute-start(f32[112,128]{1,0:T(8,128)S(1)} %get-tuple-element.28.refs_0_), channel_id=1, source_target_pairs={{0,16},{1,5},{2,18},{3,7},{4,20},{5,1},{6,22},{7,3},{8,24},{9,13},... | collective-permute-start | bytes 172040 | tf_op jit(solution)/shard_map/ppermute | solution.py:539
  6.4 7.1 %collective-permute-start.2 = (f32[168,128]{1,0:T(8,128)S(1)}, f32[168,128]{1,0:T(8,128)S(1)}, u32[]{:S(2)}, u32[]{:S(2)}) collective-permute-start(f32[168,128]{1,0:T(8,128)S(1)} %get-tuple-element.20), channel_id=1, source_target_pairs={{0,2},{2,0},{4,6},{6,4},{8,10},{10,8},{12,14},{14,12},{1,3},{3,1},... | collective-permute-start | bytes 258056 | tf_op jit(solution)/shard_map/ppermute | solution.py:515
  7.9 7.3 %collective-permute-start.3 = (f32[168,128]{1,0:T(8,128)S(1)}, f32[168,128]{1,0:T(8,128)S(1)}, u32[]{:S(2)}, u32[]{:S(2)}) collective-permute-start(f32[168,128]{1,0:T(8,128)S(1)} %get-tuple-element.21), channel_id=1, source_target_pairs={{2,4},{4,2},{6,8},{8,6},{10,12},{12,10},{14,0},{0,14},{3,5},{5,3},... | collective-permute-start | bytes 258056 | tf_op jit(solution)/shard_map/ppermute | solution.py:523
  11.4 4.9 %collective-permute-start.5 = (f32[112,128]{1,0:T(8,128)S(1)}, f32[112,128]{1,0:T(8,128)S(1)}, u32[]{:S(2)}, u32[]{:S(2)}) collective-permute-start(f32[112,128]{1,0:T(8,128)S(1)} %get-tuple-element.28.refs_0_), channel_id=1, source_target_pairs={{0,16},{1,3},{2,18},{3,1},{4,20},{5,7},{6,22},{7,5},{8,24},{9,11},... | collective-permute-start | bytes 172040 | tf_op jit(solution)/shard_map/ppermute | solution.py:539
  12.0 4.4 %collective-permute-start.6 = (f32[112,128]{1,0:T(8,128)S(1)}, f32[112,128]{1,0:T(8,128)S(1)}, u32[]{:S(2)}, u32[]{:S(2)}) collective-permute-start(f32[112,128]{1,0:T(8,128)S(1)} %collective-permute-done.4.refs_1_), channel_id=1, source_target_pairs={{0,16},{1,3},{2,18},{3,1},{4,20},{5,7},{6,22},{7,5},{8,24},{9,11},... | collective-permute-start | bytes 172040 | tf_op jit(solution)/shard_map/ppermute | solution.py:539
  15.2 1.2 %copy-start.5 = (f32[2,320,128]{2,1,0:T(8,128)S(1)}, f32[2,320,128]{2,1,0:T(8,128)}, u32[]{:S(2)}) copy-start(f32[2,320,128]{2,1,0:T(8,128)} %refs_6_.1) | copy-start | bytes 983044
  16.4 16.7 %copy-start.6 = (f32[2,320,128]{2,1,0:T(8,128)S(1)}, f32[2,320,128]{2,1,0:T(8,128)}, u32[]{:S(2)}) copy-start(f32[2,320,128]{2,1,0:T(8,128)} %refs_5_.1) | copy-start | bytes 983044
  19.9 3.6 %collective-permute-start.7 = (f32[1,128]{1,0:T(1,128)S(1)}, f32[1,128]{1,0:T(1,128)S(1)}, u32[]{:S(2)}, u32[]{:S(2)}) collective-permute-start(f32[1,128]{1,0:T(1,128)S(1)} %get-tuple-element.31.refs_0_), channel_id=1, source_target_pairs={{0,2},{2,0},{4,6},{6,4},{8,10},{10,8},{12,14},{14,12},{1,3},{3,1},... | collective-permute-start | bytes 1544 | tf_op jit(solution)/shard_map/ppermute | solution.py:515
  23.5 3.6 %collective-permute-start.8 = (f32[2,128]{1,0:T(2,128)S(1)}, f32[2,128]{1,0:T(2,128)S(1)}, u32[]{:S(2)}, u32[]{:S(2)}) collective-permute-start(f32[2,128]{1,0:T(2,128)S(1)} %pad_maximum_fusion.2), channel_id=1, source_target_pairs={{0,4},{2,6},{4,0},{6,2},{8,12},{10,14},{12,8},{14,10},{1,5},{3,7},... | collective-permute-start | bytes 3080 | tf_op jit(solution)/shard_map/ppermute | solution.py:515
  27.1 4.5 %collective-permute-start.9 = (f32[4,128]{1,0:T(4,128)S(1)}, f32[4,128]{1,0:T(4,128)S(1)}, u32[]{:S(2)}, u32[]{:S(2)}) collective-permute-start(f32[4,128]{1,0:T(4,128)S(1)} %pad_maximum_fusion.1), channel_id=1, source_target_pairs={{0,8},{2,10},{4,12},{6,14},{8,0},{10,2},{12,4},{14,6},{1,9},{3,11}... | collective-permute-start | bytes 6152 | tf_op jit(solution)/shard_map/ppermute | solution.py:515
  31.6 1.5 %collective-permute-start.10 = (f32[8,128]{1,0:T(8,128)S(1)}, f32[8,128]{1,0:T(8,128)S(1)}, u32[]{:S(2)}, u32[]{:S(2)}) collective-permute-start(f32[8,128]{1,0:T(8,128)S(1)} %pad_maximum_fusion), channel_id=1, source_target_pairs={{0,1},{1,0},{2,3},{3,2},{4,5},{5,4},{6,7},{7,6},{8,9},{9,8},{10,11... | collective-permute-start | bytes 12296 | tf_op jit(solution)/shard_map/ppermute | solution.py:515

commit v6 on v5

--- a/solution.py
+++ b/solution.py
@@ -11,7 +11,6 @@
 HALO = 2 * STEPS
 LANES = 128
 VMEM_LIMIT = 24 * 1024 * 1024
-PAY_ROWS = 168
 f32 = jnp.float32
 
 
@@ -84,9 +83,14 @@
     )(*inputs)
 
 
-def pack_kernel(lon_axis, d, sea, pw, ek, nk, rows_in, strip1, strip2, pay1, pay2, strips):
-    strips[:STRIP, :] = strip1[...]
-    strips[STRIP:, :] = strip2[...]
+def pack_kernel(lon_axis, d, sea, pw, ek, nk, rows_in, *refs):
+    *pieces, pay1, pay2, strips = refs
+    first = d.shape[1] // 2 + 8
+    for target, at in ((strips, 0), (pay1, first), (pay2, first)):
+        for piece in pieces:
+            size = piece.shape[0]
+            target[at : at + size, :] = piece[...]
+            at += size
     rows = d.shape[1]
     groups = rows // 8
     half_groups = groups // 2
@@ -120,16 +124,18 @@
         pay2[8 * line : 8 * line + 8, :] = jnp.where(even, west, east)
 
 
-def columns_to_send(d, sea, pw, ek, nk, rows_in, strip1, strip2):
-    size = PAY_ROWS
+def columns_to_send(d, sea, pw, ek, nk, rows_in, pieces):
+    strips = sum(piece.shape[0] for piece in pieces)
+    size = d.shape[1] // 2 + 8 + strips
     full = pl.BlockSpec(memory_space=pltpu.VMEM)
+    inputs = (d, sea, pw, ek, nk, rows_in, *pieces)
     return pl.pallas_call(
         functools.partial(pack_kernel, "lon"),
-        out_shape=[jax.ShapeDtypeStruct((size, LANES), f32) for size in (size, size, 2 * STRIP)],
-        in_specs=[full] * 8,
+        out_shape=[jax.ShapeDtypeStruct((n, LANES), f32) for n in (size, size, strips)],
+        in_specs=[full] * len(inputs),
         out_specs=[full] * 3,
         compiler_params=pltpu.CompilerParams(vmem_limit_bytes=VMEM_LIMIT),
-    )(d, sea, pw, ek, nk, rows_in, strip1, strip2)
+    )(*inputs)
 
 
 def slab_index(group, shift=0):
@@ -157,7 +163,8 @@
 
 
 def coefficient_kernel(
-    lon_axis, lat_axis, d, sea, pw, ek, nk, halo1, halo2, rows_in, field, weight, east_c, west_c, north_c, ocean
+    lon_axis, lat_axis, d, sea, pw, ek, nk, res, halo1, halo2, rows_in, face_in,
+    field, weight, east_c, west_c, north_c, squares, face, ocean,
 ):
     top = lax.axis_index(lat_axis) == 1
     even = lax.axis_index(lon_axis) % 2 == 0
@@ -220,6 +227,14 @@
         masked_side[1] = jnp.where(used, side[1], 0.0)
         set_group(group, masked, masked_side)
 
+    total = zero
+    for level in range(2):
+        for group in range(groups):
+            r = res[level, 8 * group : 8 * group + 8, :]
+            total = total + r * r
+    squares[...] = total
+    face[...] = face_in[...]
+
     for group in range(groups + 2):
         here = at(group)
         oc = [ocean[s, here, :] for s in range(3)]
@@ -231,22 +246,22 @@
             north_c[s, here, :] = north_c[s, here, :] * ocean[s, at(group, 1), :]
 
 
-def coefficients(d, sea, pw, ek, nk, halo1, halo2, rows_in):
+def coefficients(d, sea, pw, ek, nk, res, halo1, halo2, rows_in, face):
     full = pl.BlockSpec(memory_space=pltpu.VMEM)
     extended = (3, d.shape[1] + 32, LANES)
     return pl.pallas_call(
         functools.partial(coefficient_kernel, "lon", "lat"),
-        out_shape=[jax.ShapeDtypeStruct(extended, f32)] * 5,
-        in_specs=[full] * 8,
-        out_specs=[full] * 5,
+        out_shape=[jax.ShapeDtypeStruct(extended, f32)] * 5
+        + [jax.ShapeDtypeStruct((8, LANES), f32), jax.ShapeDtypeStruct(face.shape, f32)],
+        in_specs=[full] * 10,
+        out_specs=[full] * 7,
         scratch_shapes=[pltpu.VMEM(extended, f32)],
         compiler_params=pltpu.CompilerParams(vmem_limit_bytes=VMEM_LIMIT),
-    )(d, sea, pw, ek, nk, halo1, halo2, rows_in)
-
-
-def strip_kernel(offsets, lon_axis, lat_axis, partner, gathered_pieces, beyond_out, face_out, blocks):
+    )(d, sea, pw, ek, nk, res, halo1, halo2, rows_in, face)
+
+
+def strip_kernel(count, offsets, lon_axis, lat_axis, partner, gathered_pieces, beyond_out, face_out, blocks):
     lon = lax.axis_index(lon_axis)
-    count = len(offsets)
 
     top = lax.axis_index(lat_axis) == 1
 
@@ -261,12 +276,15 @@
 
 
 def strip_steps(lon, count, offsets, partner, gathered_pieces, beyond_out, face_out, blocks):
-    slot = 0
-    for piece in gathered_pieces:
-        for inside in range(piece.shape[0] // STRIP):
-            block = lax.bitwise_xor(lon, offsets[slot])
-            blocks[pl.ds(pl.multiple_of(block * STRIP, 8), STRIP), :] = piece[STRIP * inside : STRIP * (inside + 1), :]
-            slot += 1
+    odd = lon % 2
+    neighbour = lax.rem(lon + 2 * odd + count - 1, count)
+    owners = (lon, lax.bitwise_xor(lon, 2), lax.bitwise_xor(lon, 1), neighbour)
+    for piece, owner in zip(gathered_pieces, owners):
+        first = piece.shape[0] - STRIP * len(offsets)
+        for slot, offset in enumerate(offsets):
+            block = lax.bitwise_xor(owner, offset)
+            row = first + STRIP * slot
+            blocks[pl.ds(pl.multiple_of(block * STRIP, 8), STRIP), :] = piece[row : row + STRIP, :]
     wide = lanes_of((count, LANES))
 
     def strip_row(index, row):
@@ -354,12 +372,12 @@
 
 
 def strip_rows(partner, pieces, offsets):
-    count = len(offsets)
+    count = partner.shape[0]
     full = pl.BlockSpec(memory_space=pltpu.VMEM)
     inputs = [partner, *pieces]
 
     def kernel(partner_ref, *refs):
-        strip_kernel(offsets, "lon", "lat", partner_ref, refs[: len(pieces)], *refs[len(pieces) :])
+        strip_kernel(count, offsets, "lon", "lat", partner_ref, refs[: len(pieces)], *refs[len(pieces) :])
 
     return pl.pallas_call(
         kernel,
@@ -372,7 +390,7 @@
 
 
 def image_kernel(
-    d, sea, res, first_field, weight, east_c, west_c, north_c, beyond, face, image, stats, field, other
+    d, sea, res, squares, first_field, weight, east_c, west_c, north_c, beyond, face, image, stats, field, other
 ):
     groups = d.shape[1] // 8
     zero = jnp.zeros((8, LANES), f32)
@@ -422,7 +440,7 @@
 
     lax.fori_loop(0, STEPS, two_steps, 0)
 
-    rr = rq = dq = qq = zero
+    rr, rq, dq, qq = squares[...], zero, zero, zero
     for group in range(groups):
         here = slice(8 * group, 8 * group + 8)
         for level in range(2):
@@ -431,7 +449,7 @@
             dv, rv = d[level, here, :], res[level, here, :]
             q = dv + o * u
             image[level, here, :] = q
-            rr, rq, dq, qq = rr + rv * rv, rq + rv * q, dq + dv * q, qq + q * q
+            rq, dq, qq = rq + rv * q, dq + dv * q, qq + q * q
     rr, rq, dq, qq = (jnp.sum(x) for x in (rr, rq, dq, qq))
     a0 = jnp.where(qq > 0.0, rq / jnp.where(qq > 0.0, qq, 1.0), 0.0)
     ss = sq = zero
@@ -449,9 +467,9 @@
     stats[...] = row
 
 
-def image_and_stats(d, sea, res, coeffs, beyond, face):
+def image_and_stats(d, sea, res, squares, coeffs, beyond, face):
     full = pl.BlockSpec(memory_space=pltpu.VMEM)
-    inputs = [d, sea, res, *coeffs, beyond, face]
+    inputs = [d, sea, res, squares, *coeffs, beyond, face]
     return pl.pallas_call(
         image_kernel,
         out_shape=[jax.ShapeDtypeStruct(d.shape, f32), jax.ShapeDtypeStruct((1, LANES), f32)],
@@ -553,16 +571,15 @@
     fields = (direction, land_sea, precision_weight, east_kappa, north_kappa)
     strip, edge, partner = rows_to_send(*fields, fold_partner.reshape(count, LANES))
     rows_in = swapped(edge, "lat", 1)
-    strip2 = strip_swap(strip, count // 2, True)
-    pay1, pay2, strips = columns_to_send(*fields, rows_in, strip, strip2)
+    far, *rest = distances(count)[:-2]
+    pieces, offsets = butterfly([strip, strip_swap(strip, far, True)], [0, far], strip_swap, rest)
+    pay1, pay2, strips = columns_to_send(*fields, rows_in, pieces)
+    halo1 = swapped(pay1, "lon", 1)
     halo2 = odd_pairs(pay2, "lon")
-    halo1 = swapped(pay1, "lon", 1)
-    rest = distances(count)[1:]
-    pieces, offsets = butterfly([strips], [0, count // 2], strip_swap, rest[:-1])
-    pieces += [strip_swap(piece, rest[-1]) for piece in pieces]
-    offsets += [o ^ rest[-1] for o in offsets]
-    coeffs = coefficients(*fields, halo1, halo2, rows_in)
-    image, stats = image_and_stats(direction, land_sea, residual, coeffs, *strip_rows(partner, pieces, offsets))
+    across_two = strip_swap(strips, 2)
+    beyond, face = strip_rows(partner, [strips, across_two, halo1, halo2], offsets)
+    *coeffs, squares, face = coefficients(*fields, residual, halo1, halo2, rows_in, face)
+    image, stats = image_and_stats(direction, land_sea, residual, squares, coeffs, beyond, face)
     parts, _ = butterfly([stats], [0], lambda value, distance: swapped(value, "lon", distance), distances(count)[::-1])
     parts.append(swapped(jnp.concatenate(parts, axis=0), "lat", 1))
     return tuple(update(parts, iterate, residual, direction, image))

time: 34.5 us -> 33.9 us (0.983)
  starting transfers between devices: 12.7 us -> 10.8 us
  waiting for transfers between devices: 13.6 us -> 14.8 us
    ppermute x4 -> x2, starting transfers between devices: 5.58 us -> 2.14 us  [strip_swap(): lax.ppermute(value, ('member', 'lon', 'lat'), [(number(*p), other(*p)) fo...]
    ppermute x4 -> x2, waiting for transfers between devices: 0.01 us -> 2.69 us  [strip_swap(): lax.ppermute(value, ('member', 'lon', 'lat'), [(number(*p), other(*p)) fo...]
    ppermute x6, starting transfers between devices: 3.55 us -> 5.13 us  [swapped(): lax.ppermute(value, axis, [(i, i ^ distance) for i in range(lax.axis_size...]
    ppermute x1, waiting for transfers between devices: 1.71 us -> 0.18 us  [odd_pairs(): return lax.ppermute(value, axis, pairs)]
  transfers between devices with their start and end apart: 11 -> 9, of which waited for: 6 -> 7; matrix products, arithmetic and copies ran while one was open for 0% -> 0% of each run, Pallas kernels for 3% -> 0%
where the time goes in v6:
time: 33.9 us; the launch traced here: 33.7 us
  waiting for transfers between devices  14.8 us (44%)
  starting transfers between devices  10.8 us (32%)
  Pallas kernels  7.3 us (22%)
  between operations  0.79 us (2%)
    ppermute x6, waiting for transfers between devices, swapped(): lax.ppermute(value, axis, [(i, i ^ distance) for i in range(lax.axis_size...  11.9 us
    ppermute x6, starting transfers between devices, swapped(): lax.ppermute(value, axis, [(i, i ^ distance) for i in range(lax.axis_size...  5.13 us
    pallas_call x1, Pallas kernels, image_and_stats(): pl.pallas_call(image_kernel, out_shape=[jax.ShapeDtypeStruct(d.shape, f32...  3.55 us
    ppermute x1, starting transfers between devices, odd_pairs(): return lax.ppermute(value, axis, pairs)  3.54 us
    ppermute x2, waiting for transfers between devices, strip_swap(): lax.ppermute(value, ('member', 'lon', 'lat'), [(number(*p), other(*p)) fo...  2.69 us
    ppermute x2, starting transfers between devices, strip_swap(): lax.ppermute(value, ('member', 'lon', 'lat'), [(number(*p), other(*p)) fo...  2.14 us
    pallas_call x1, Pallas kernels, update(): pl.pallas_call(functools.partial(update_kernel, len(parts)), out_shape=[j...  1.19 us
    pallas_call x1, Pallas kernels, coefficients(): pl.pallas_call(functools.partial(coefficient_kernel, 'lon', 'lat'), out_s...  1.17 us
  transfers between devices with their start and end apart: 9, of which 7 were waited for; matrix products, arithmetic and copies ran while one was open for 0% of the time, Pallas kernels for 0%

profile of v6, /device:TPU:0, one launch (start us, length us, event | category | flops | bytes accessed | tf_op | source)
XLA Modules:
  0.0 33.7 jit_solution(9014949381839086295)
XLA Ops:
  0.6 0.0 copy-start
  0.6 0.0 copy-start.1
  0.7 0.0 copy-start.2
  0.7 0.0 copy-start.4
  0.7 0.0 copy-start.5
  0.7 1.0 %shard_map.103 = (f32[56,128]{1,0:T(8,128)S(1)}, f32[8,8,128]{2,1,0:T(8,128)S(1)}, s32[8,128]{1,0:T(8,128)S(1)}) custom-call(f32[2,320,128]{2,1,0:T(8,128)} %refs_7_.1, s32[2,320,128]{2,1,0:T(8,128)} %sea.7, f32[2,320,128]{2,1,0:T(8,128)} %pw.5, f32[320,128]{1,0:T(8,128)} %ek.5, f32[320,128]{1,0:T(8,128)} %nk.5, s32[8,128]{1,0:T(8,128)} %bitcast.1), custom_call_target="tpu_custom_call" | custom-call | tf_op jit(solution)/shard_map/pallas_call | solution.py:67
  1.7 0.5 %collective-permute-start = (f32[8,8,128]{2,1,0:T(8,128)S(1)}, f32[8,8,128]{2,1,0:T(8,128)S(1)}, u32[]{:S(2)}, u32[]{:S(2)}) collective-permute-start(f32[8,8,128]{2,1,0:T(8,128)S(1)} %get-tuple-element.20), channel_id=1, source_target_pairs={{0,1},{1,0},{2,3},{3,2},{4,5},{5,4},{6,7},{7,6},{8,9},{9,8},{10,11... | collective-permute-start | bytes 98312 | tf_op jit(solution)/shard_map/ppermute | solution.py:533
  2.2 0.7 %collective-permute-start.1 = (f32[56,128]{1,0:T(8,128)S(1)}, f32[56,128]{1,0:T(8,128)S(1)}, u32[]{:S(2)}, u32[]{:S(2)}) collective-permute-start(f32[56,128]{1,0:T(8,128)S(1)} %get-tuple-element.21.refs_0_), channel_id=1, source_target_pairs={{1,9},{3,11},{5,13},{7,15},{9,1},{11,3},{13,5},{15,7},{17,25},{19,... | collective-permute-start | bytes 86024 | tf_op jit(solution)/shard_map/ppermute | solution.py:557
  2.8 0.0 collective-permute-done.1.refs_1_
  2.9 0.2 collective-permute-done.rows_in
  3.0 0.0 copy-done
  3.0 0.0 copy-done.1
  3.0 0.0 copy-done.2
  3.1 0.0 copy-done.4
  3.1 0.0 copy-done.5
  3.1 0.4 %shard_map.104 = (f32[280,128]{1,0:T(8,128)S(1)}, f32[280,128]{1,0:T(8,128)S(1)}, f32[112,128]{1,0:T(8,128)S(1)}) custom-call(f32[2,320,128]{2,1,0:T(8,128)S(1)} %copy-done, s32[2,320,128]{2,1,0:T(8,128)S(1)} %copy-done.1, f32[2,320,128]{2,1,0:T(8,128)S(1)} %copy-done.2, f32[320,128]{1,0:T(8,128)S(1)} %copy-done.4, f32[320,128]{1,0:T(8,128)S(1)} %copy-done.5, ...), custom_call_target="tpu_custom_call" | custom-call | tf_op jit(solution)/shard_map/pallas_call | solution.py:132
  3.5 0.0 copy-start.3
  3.5 2.9 %collective-permute-start.2 = (f32[280,128]{1,0:T(8,128)S(1)}, f32[280,128]{1,0:T(8,128)S(1)}, u32[]{:S(2)}, u32[]{:S(2)}) collective-permute-start(f32[280,128]{1,0:T(8,128)S(1)} %get-tuple-element.22), channel_id=1, source_target_pairs={{0,2},{2,0},{4,6},{6,4},{8,10},{10,8},{12,14},{14,12},{1,3},{3,1},... | collective-permute-start | bytes 430088 | tf_op jit(solution)/shard_map/ppermute | solution.py:533
  6.4 3.5 %collective-permute-start.3 = (f32[280,128]{1,0:T(8,128)S(1)}, f32[280,128]{1,0:T(8,128)S(1)}, u32[]{:S(2)}, u32[]{:S(2)}) collective-permute-start(f32[280,128]{1,0:T(8,128)S(1)} %get-tuple-element.23), channel_id=1, source_target_pairs={{2,4},{4,2},{6,8},{8,6},{10,12},{12,10},{14,0},{0,14},{3,5},{5,3},... | collective-permute-start | bytes 430088 | tf_op jit(solution)/shard_map/ppermute | solution.py:541
  10.0 1.5 %collective-permute-start.4 = (f32[112,128]{1,0:T(8,128)S(1)}, f32[112,128]{1,0:T(8,128)S(1)}, u32[]{:S(2)}, u32[]{:S(2)}) collective-permute-start(f32[112,128]{1,0:T(8,128)S(1)} %get-tuple-element.25.refs_0_), channel_id=1, source_target_pairs={{0,16},{1,5},{2,18},{3,7},{4,20},{5,1},{6,22},{7,3},{8,24},{9,13},... | collective-permute-start | bytes 172040 | tf_op jit(solution)/shard_map/ppermute | solution.py:557
  11.5 2.7 %collective-permute-done.4.refs_1_ = f32[112,128]{1,0:T(8,128)S(1)} collective-permute-done((f32[112,128]{1,0:T(8,128)S(1)}, f32[112,128]{1,0:T(8,128)S(1)}, u32[]{:S(2)}, u32[]{:S(2)}) %collective-permute-start.4) | collective-permute-done | bytes 57376 | tf_op jit(solution)/shard_map/ppermute | solution.py:557
  14.1 0.0 collective-permute-done.2.refs_2_.halo1
  14.2 0.2 collective-permute-done.3.refs_3_.halo2
  14.3 0.0 copy-done.3
  14.4 1.2 %shard_map.106 = (f32[3,352,128]{2,1,0:T(8,128)S(1)}, f32[3,352,128]{2,1,0:T(8,128)S(1)}, f32[3,352,128]{2,1,0:T(8,128)S(1)}, f32[3,352,128]{2,1,0:T(8,128)S(1)}...) custom-call(f32[2,320,128]{2,1,0:T(8,128)S(1)} %copy-done, ...), custom_call_target="tpu_custom_call" | custom-call | tf_op jit(solution)/shard_map/pallas_call | solution.py:252
  15.5 0.0 copy-start.6
  15.5 3.6 %shard_map.107 = (f32[2,320,128]{2,1,0:T(8,128)S(1)}, f32[1,128]{1,0:T(1,128)S(1)}) custom-call(f32[2,320,128]{2,1,0:T(8,128)S(1)} %copy-done, s32[2,320,128]{2,1,0:T(8,128)S(1)} %copy-done.1, f32[2,320,128]{2,1,0:T(8,128)S(1)} %copy-done.3, f32[8,128]{1,0:T(8,128)S(1)} %get-tuple-element.27.squares, f32[3,352,128]{2,1,0:T(8,128)S(1)} %get-tuple-element.28.first_field, ...), custom_call_target="tpu_custom_call" | custom-call | tf_op jit(solution)/shard_map/pallas_call | solution.py:473
  19.1 0.1 collective-permute-start.5
  19.2 3.5 %collective-permute-done.5.refs_1_ = f32[1,128]{1,0:T(1,128)S(1)} collective-permute-done((f32[1,128]{1,0:T(1,128)S(1)}, f32[1,128]{1,0:T(1,128)S(1)}, u32[]{:S(2)}, u32[]{:S(2)}) %collective-permute-start.5) | collective-permute-done | bytes 544 | tf_op jit(solution)/shard_map/ppermute | solution.py:533
  22.7 0.0 collective-permute-start.6
  22.7 3.6 %collective-permute-done.6.refs_2_ = f32[2,128]{1,0:T(2,128)S(1)} collective-permute-done((f32[2,128]{1,0:T(2,128)S(1)}, f32[2,128]{1,0:T(2,128)S(1)}, u32[]{:S(2)}, u32[]{:S(2)}) %collective-permute-start.6) | collective-permute-done | bytes 1056 | tf_op jit(solution)/shard_map/ppermute | solution.py:533
  26.3 0.8 %collective-permute-start.7 = (f32[4,128]{1,0:T(4,128)S(1)}, f32[4,128]{1,0:T(4,128)S(1)}, u32[]{:S(2)}, u32[]{:S(2)}) collective-permute-start(f32[4,128]{1,0:T(4,128)S(1)} %pad_maximum_fusion.1), channel_id=1, source_target_pairs={{0,8},{2,10},{4,12},{6,14},{8,0},{10,2},{12,4},{14,6},{1,9},{3,11}... | collective-permute-start | bytes 6152 | tf_op jit(solution)/shard_map/ppermute | solution.py:533
  27.1 3.8 %collective-permute-done.7.refs_3_ = f32[4,128]{1,0:T(4,128)S(1)} collective-permute-done((f32[4,128]{1,0:T(4,128)S(1)}, f32[4,128]{1,0:T(4,128)S(1)}, u32[]{:S(2)}, u32[]{:S(2)}) %collective-permute-start.7) | collective-permute-done | bytes 2080 | tf_op jit(solution)/shard_map/ppermute | solution.py:533
  30.9 0.9 %collective-permute-start.8 = (f32[8,128]{1,0:T(8,128)S(1)}, f32[8,128]{1,0:T(8,128)S(1)}, u32[]{:S(2)}, u32[]{:S(2)}) collective-permute-start(f32[8,128]{1,0:T(8,128)S(1)} %pad_maximum_fusion), channel_id=1, source_target_pairs={{0,1},{1,0},{2,3},{3,2},{4,5},{5,4},{6,7},{7,6},{8,9},{9,8},{10,11... | collective-permute-start | bytes 12296 | tf_op jit(solution)/shard_map/ppermute | solution.py:533
  31.7 0.8 %collective-permute-done.8.refs_4_ = f32[8,128]{1,0:T(8,128)S(1)} collective-permute-done((f32[8,128]{1,0:T(8,128)S(1)}, f32[8,128]{1,0:T(8,128)S(1)}, u32[]{:S(2)}, u32[]{:S(2)}) %collective-permute-start.8) | collective-permute-done | bytes 4128 | tf_op jit(solution)/shard_map/ppermute | solution.py:533
  32.5 0.0 copy-done.6
  32.5 1.2 %shard_map.108 = (f32[2,320,128]{2,1,0:T(8,128)}, f32[2,320,128]{2,1,0:T(8,128)}, f32[2,320,128]{2,1,0:T(8,128)}) custom-call(f32[1,128]{1,0:T(1,128)S(1)} %get-tuple-element.35.refs_0_, f32[1,128]{1,0:T(1,128)S(1)} %collective-permute-done.5.refs_1_, f32[2,128]{1,0:T(2,128)S(1)} %collective-permute-done.6.refs_2_, ...), custom_call_target="tpu_custom_call" | custom-call | tf_op jit(solution)/shard_map/pallas_call | solution.py:522
  (4 shorter events, 0.0 us)
Async XLA Ops:
  0.6 2.4 %copy-start = (f32[2,320,128]{2,1,0:T(8,128)S(1)}, f32[2,320,128]{2,1,0:T(8,128)}, u32[]{:S(2)}) copy-start(f32[2,320,128]{2,1,0:T(8,128)} %refs_7_.1) | copy-start | bytes 983044
  0.6 2.4 %copy-start.1 = (s32[2,320,128]{2,1,0:T(8,128)S(1)}, s32[2,320,128]{2,1,0:T(8,128)}, u32[]{:S(2)}) copy-start(s32[2,320,128]{2,1,0:T(8,128)} %sea.7) | copy-start | bytes 983044
  0.7 2.4 %copy-start.2 = (f32[2,320,128]{2,1,0:T(8,128)S(1)}, f32[2,320,128]{2,1,0:T(8,128)}, u32[]{:S(2)}) copy-start(f32[2,320,128]{2,1,0:T(8,128)} %pw.5) | copy-start | bytes 983044
  0.7 2.4 %copy-start.4 = (f32[320,128]{1,0:T(8,128)S(1)}, f32[320,128]{1,0:T(8,128)}, u32[]{:S(2)}) copy-start(f32[320,128]{1,0:T(8,128)} %ek.5) | copy-start | bytes 491524
  0.7 2.4 %copy-start.5 = (f32[320,128]{1,0:T(8,128)S(1)}, f32[320,128]{1,0:T(8,128)}, u32[]{:S(2)}) copy-start(f32[320,128]{1,0:T(8,128)} %nk.5) | copy-start | bytes 491524
  1.7 1.4 %collective-permute-start = (f32[8,8,128]{2,1,0:T(8,128)S(1)}, f32[8,8,128]{2,1,0:T(8,128)S(1)}, u32[]{:S(2)}, u32[]{:S(2)}) collective-permute-start(f32[8,8,128]{2,1,0:T(8,128)S(1)} %get-tuple-element.20), channel_id=1, source_target_pairs={{0,1},{1,0},{2,3},{3,2},{4,5},{5,4},{6,7},{7,6},{8,9},{9,8},{10,11... | collective-permute-start | bytes 98312 | tf_op jit(solution)/shard_map/ppermute | solution.py:533
  2.2 0.7 %collective-permute-start.1 = (f32[56,128]{1,0:T(8,128)S(1)}, f32[56,128]{1,0:T(8,128)S(1)}, u32[]{:S(2)}, u32[]{:S(2)}) collective-permute-start(f32[56,128]{1,0:T(8,128)S(1)} %get-tuple-element.21.refs_0_), channel_id=1, source_target_pairs={{1,9},{3,11},{5,13},{7,15},{9,1},{11,3},{13,5},{15,7},{17,25},{19,... | collective-permute-start | bytes 86024 | tf_op jit(solution)/shard_map/ppermute | solution.py:557
  3.5 10.9 %copy-start.3 = (f32[2,320,128]{2,1,0:T(8,128)S(1)}, f32[2,320,128]{2,1,0:T(8,128)}, u32[]{:S(2)}) copy-start(f32[2,320,128]{2,1,0:T(8,128)} %refs_6_.1) | copy-start | bytes 983044
  3.5 10.7 %collective-permute-start.2 = (f32[280,128]{1,0:T(8,128)S(1)}, f32[280,128]{1,0:T(8,128)S(1)}, u32[]{:S(2)}, u32[]{:S(2)}) collective-permute-start(f32[280,128]{1,0:T(8,128)S(1)} %get-tuple-element.22), channel_id=1, source_target_pairs={{0,2},{2,0},{4,6},{6,4},{8,10},{10,8},{12,14},{14,12},{1,3},{3,1},... | collective-permute-start | bytes 430088 | tf_op jit(solution)/shard_map/ppermute | solution.py:533
  6.4 7.9 %collective-permute-start.3 = (f32[280,128]{1,0:T(8,128)S(1)}, f32[280,128]{1,0:T(8,128)S(1)}, u32[]{:S(2)}, u32[]{:S(2)}) collective-permute-start(f32[280,128]{1,0:T(8,128)S(1)} %get-tuple-element.23), channel_id=1, source_target_pairs={{2,4},{4,2},{6,8},{8,6},{10,12},{12,10},{14,0},{0,14},{3,5},{5,3},... | collective-permute-start | bytes 430088 | tf_op jit(solution)/shard_map/ppermute | solution.py:541
  10.0 4.2 %collective-permute-start.4 = (f32[112,128]{1,0:T(8,128)S(1)}, f32[112,128]{1,0:T(8,128)S(1)}, u32[]{:S(2)}, u32[]{:S(2)}) collective-permute-start(f32[112,128]{1,0:T(8,128)S(1)} %get-tuple-element.25.refs_0_), channel_id=1, source_target_pairs={{0,16},{1,5},{2,18},{3,7},{4,20},{5,1},{6,22},{7,3},{8,24},{9,13},... | collective-permute-start | bytes 172040 | tf_op jit(solution)/shard_map/ppermute | solution.py:557
  15.5 17.0 %copy-start.6 = (f32[2,320,128]{2,1,0:T(8,128)S(1)}, f32[2,320,128]{2,1,0:T(8,128)}, u32[]{:S(2)}) copy-start(f32[2,320,128]{2,1,0:T(8,128)} %refs_5_.1) | copy-start | bytes 983044
  19.1 3.6 %collective-permute-start.5 = (f32[1,128]{1,0:T(1,128)S(1)}, f32[1,128]{1,0:T(1,128)S(1)}, u32[]{:S(2)}, u32[]{:S(2)}) collective-permute-start(f32[1,128]{1,0:T(1,128)S(1)} %get-tuple-element.35.refs_0_), channel_id=1, source_target_pairs={{0,2},{2,0},{4,6},{6,4},{8,10},{10,8},{12,14},{14,12},{1,3},{3,1},... | collective-permute-start | bytes 1544 | tf_op jit(solution)/shard_map/ppermute | solution.py:533
  22.7 3.6 %collective-permute-start.6 = (f32[2,128]{1,0:T(2,128)S(1)}, f32[2,128]{1,0:T(2,128)S(1)}, u32[]{:S(2)}, u32[]{:S(2)}) collective-permute-start(f32[2,128]{1,0:T(2,128)S(1)} %pad_maximum_fusion.2), channel_id=1, source_target_pairs={{0,4},{2,6},{4,0},{6,2},{8,12},{10,14},{12,8},{14,10},{1,5},{3,7},... | collective-permute-start | bytes 3080 | tf_op jit(solution)/shard_map/ppermute | solution.py:533
  26.3 4.5 %collective-permute-start.7 = (f32[4,128]{1,0:T(4,128)S(1)}, f32[4,128]{1,0:T(4,128)S(1)}, u32[]{:S(2)}, u32[]{:S(2)}) collective-permute-start(f32[4,128]{1,0:T(4,128)S(1)} %pad_maximum_fusion.1), channel_id=1, source_target_pairs={{0,8},{2,10},{4,12},{6,14},{8,0},{10,2},{12,4},{14,6},{1,9},{3,11}... | collective-permute-start | bytes 6152 | tf_op jit(solution)/shard_map/ppermute | solution.py:533
  30.9 1.7 %collective-permute-start.8 = (f32[8,128]{1,0:T(8,128)S(1)}, f32[8,128]{1,0:T(8,128)S(1)}, u32[]{:S(2)}, u32[]{:S(2)}) collective-permute-start(f32[8,128]{1,0:T(8,128)S(1)} %pad_maximum_fusion), channel_id=1, source_target_pairs={{0,1},{1,0},{2,3},{3,2},{4,5},{5,4},{6,7},{7,6},{8,9},{9,8},{10,11... | collective-permute-start | bytes 12296 | tf_op jit(solution)/shard_map/ppermute | solution.py:533

commit v7 on v6

--- a/solution.py
+++ b/solution.py
@@ -248,7 +248,7 @@
 
 def coefficients(d, sea, pw, ek, nk, res, halo1, halo2, rows_in, face):
     full = pl.BlockSpec(memory_space=pltpu.VMEM)
-    extended = (3, d.shape[1] + 32, LANES)
+    extended = (3, d.shape[1] + 40, LANES)
     return pl.pallas_call(
         functools.partial(coefficient_kernel, "lon", "lat"),
         out_shape=[jax.ShapeDtypeStruct(extended, f32)] * 5
@@ -499,20 +499,26 @@
     alpha = jnp.broadcast_to(alpha, (8, LANES))
     beta = jnp.broadcast_to(beta, (8, LANES))
     copies = []
-    for level in range(2):
-        for piece in range(pieces):
-            first, size = piece * (rows // pieces), rows // pieces
-            for row in range(first, first + size, 8):
-                here = slice(row, row + 8)
-                dv = d[level, here, :]
-                rv = res[level, here, :] - alpha * image[level, here, :]
-                new_iterate[level, here, :] = iterate[level, here, :] + alpha * dv
-                new_res[level, here, :] = rv
-                new_d[level, here, :] = rv + beta * dv
-            for index, (a, b) in enumerate(((new_iterate, iterate_hbm), (new_res, res_hbm), (new_d, d_hbm))):
-                part = (level, pl.ds(first, size), slice(None))
-                copies.append(pltpu.make_async_copy(a.at[part], b.at[part], sent.at[len(copies)]))
-                copies[-1].start()
+
+    def send(source, target, part):
+        copies.append(pltpu.make_async_copy(source.at[part], target.at[part], sent.at[len(copies)]))
+        copies[-1].start()
+
+    size = rows // pieces
+    parts_of = [(level, first) for level in range(2) for first in range(0, rows, size)]
+    for level, first in parts_of:
+        for row in range(first, first + size, 8):
+            here = slice(row, row + 8)
+            new_iterate[level, here, :] = iterate[level, here, :] + alpha * d[level, here, :]
+            new_res[level, here, :] = res[level, here, :] - alpha * image[level, here, :]
+        part = (level, pl.ds(first, size), slice(None))
+        send(new_iterate, iterate_hbm, part)
+        send(new_res, res_hbm, part)
+    for level, first in parts_of:
+        for row in range(first, first + size, 8):
+            here = slice(row, row + 8)
+            new_d[level, here, :] = new_res[level, here, :] + beta * d[level, here, :]
+        send(new_d, d_hbm, (level, pl.ds(first, size), slice(None)))
     for copy in copies:
         copy.wait()
 

time: 33.9 us -> 33.7 us (level)
  no operation moved by 1% of the time
where the time goes in v7:
time: 33.7 us; the launch traced here: 33.5 us
  waiting for transfers between devices  14.8 us (44%)
  starting transfers between devices  10.8 us (32%)
  Pallas kernels  7.06 us (21%)
  between operations  0.79 us (2%)
    ppermute x6, waiting for transfers between devices, swapped(): lax.ppermute(value, axis, [(i, i ^ distance) for i in range(lax.axis_size...  11.9 us
    ppermute x6, starting transfers between devices, swapped(): lax.ppermute(value, axis, [(i, i ^ distance) for i in range(lax.axis_size...  5.13 us
    ppermute x1, starting transfers between devices, odd_pairs(): return lax.ppermute(value, axis, pairs)  3.54 us
    pallas_call x1, Pallas kernels, image_and_stats(): pl.pallas_call(image_kernel, out_shape=[jax.ShapeDtypeStruct(d.shape, f32...  3.36 us
    ppermute x2, waiting for transfers between devices, strip_swap(): lax.ppermute(value, ('member', 'lon', 'lat'), [(number(*p), other(*p)) fo...  2.69 us
    ppermute x2, starting transfers between devices, strip_swap(): lax.ppermute(value, ('member', 'lon', 'lat'), [(number(*p), other(*p)) fo...  2.14 us
    pallas_call x1, Pallas kernels, coefficients(): pl.pallas_call(functools.partial(coefficient_kernel, 'lon', 'lat'), out_s...  1.17 us
    pallas_call x1, Pallas kernels, update(): pl.pallas_call(functools.partial(update_kernel, len(parts)), out_shape=[j...  1.14 us
  transfers between devices with their start and end apart: 9, of which 7 were waited for; matrix products, arithmetic and copies ran while one was open for 0% of the time, Pallas kernels for 0%

profile of v7, /device:TPU:0, one launch (start us, length us, event | category | flops | bytes accessed | tf_op | source)
XLA Modules:
  0.0 33.5 jit_solution(2694826517930949846)
XLA Ops:
  0.6 0.0 copy-start
  0.6 0.0 copy-start.1
  0.7 0.0 copy-start.3
  0.7 0.0 copy-start.4
  0.7 0.0 copy-start.5
  0.7 1.0 %shard_map.103 = (f32[56,128]{1,0:T(8,128)S(1)}, f32[8,8,128]{2,1,0:T(8,128)S(1)}, s32[8,128]{1,0:T(8,128)S(1)}) custom-call(f32[2,320,128]{2,1,0:T(8,128)} %refs_7_.1, s32[2,320,128]{2,1,0:T(8,128)} %sea.7, f32[2,320,128]{2,1,0:T(8,128)} %pw.5, f32[320,128]{1,0:T(8,128)} %ek.5, f32[320,128]{1,0:T(8,128)} %nk.5, s32[8,128]{1,0:T(8,128)} %bitcast.1), custom_call_target="tpu_custom_call" | custom-call | tf_op jit(solution)/shard_map/pallas_call | solution.py:67
  1.7 0.5 %collective-permute-start = (f32[8,8,128]{2,1,0:T(8,128)S(1)}, f32[8,8,128]{2,1,0:T(8,128)S(1)}, u32[]{:S(2)}, u32[]{:S(2)}) collective-permute-start(f32[8,8,128]{2,1,0:T(8,128)S(1)} %get-tuple-element.20), channel_id=1, source_target_pairs={{0,1},{1,0},{2,3},{3,2},{4,5},{5,4},{6,7},{7,6},{8,9},{9,8},{10,11... | collective-permute-start | bytes 98312 | tf_op jit(solution)/shard_map/ppermute | solution.py:539
  2.2 0.7 %collective-permute-start.1 = (f32[56,128]{1,0:T(8,128)S(1)}, f32[56,128]{1,0:T(8,128)S(1)}, u32[]{:S(2)}, u32[]{:S(2)}) collective-permute-start(f32[56,128]{1,0:T(8,128)S(1)} %get-tuple-element.21.refs_0_), channel_id=1, source_target_pairs={{1,9},{3,11},{5,13},{7,15},{9,1},{11,3},{13,5},{15,7},{17,25},{19,... | collective-permute-start | bytes 86024 | tf_op jit(solution)/shard_map/ppermute | solution.py:563
  2.8 0.0 collective-permute-done.1.refs_1_
  2.9 0.2 collective-permute-done.rows_in
  3.0 0.0 copy-done
  3.0 0.0 copy-done.1
  3.0 0.0 copy-done.3
  3.1 0.0 copy-done.4
  3.1 0.0 copy-done.5
  3.1 0.4 %shard_map.104 = (f32[280,128]{1,0:T(8,128)S(1)}, f32[280,128]{1,0:T(8,128)S(1)}, f32[112,128]{1,0:T(8,128)S(1)}) custom-call(f32[2,320,128]{2,1,0:T(8,128)S(1)} %copy-done, s32[2,320,128]{2,1,0:T(8,128)S(1)} %copy-done.1, f32[2,320,128]{2,1,0:T(8,128)S(1)} %copy-done.3, f32[320,128]{1,0:T(8,128)S(1)} %copy-done.4, f32[320,128]{1,0:T(8,128)S(1)} %copy-done.5, ...), custom_call_target="tpu_custom_call" | custom-call | tf_op jit(solution)/shard_map/pallas_call | solution.py:132
  3.5 0.0 copy-start.2
  3.5 2.9 %collective-permute-start.2 = (f32[280,128]{1,0:T(8,128)S(1)}, f32[280,128]{1,0:T(8,128)S(1)}, u32[]{:S(2)}, u32[]{:S(2)}) collective-permute-start(f32[280,128]{1,0:T(8,128)S(1)} %get-tuple-element.22), channel_id=1, source_target_pairs={{0,2},{2,0},{4,6},{6,4},{8,10},{10,8},{12,14},{14,12},{1,3},{3,1},... | collective-permute-start | bytes 430088 | tf_op jit(solution)/shard_map/ppermute | solution.py:539
  6.4 3.5 %collective-permute-start.3 = (f32[280,128]{1,0:T(8,128)S(1)}, f32[280,128]{1,0:T(8,128)S(1)}, u32[]{:S(2)}, u32[]{:S(2)}) collective-permute-start(f32[280,128]{1,0:T(8,128)S(1)} %get-tuple-element.23), channel_id=1, source_target_pairs={{2,4},{4,2},{6,8},{8,6},{10,12},{12,10},{14,0},{0,14},{3,5},{5,3},... | collective-permute-start | bytes 430088 | tf_op jit(solution)/shard_map/ppermute | solution.py:547
  10.0 1.5 %collective-permute-start.4 = (f32[112,128]{1,0:T(8,128)S(1)}, f32[112,128]{1,0:T(8,128)S(1)}, u32[]{:S(2)}, u32[]{:S(2)}) collective-permute-start(f32[112,128]{1,0:T(8,128)S(1)} %get-tuple-element.25.refs_0_), channel_id=1, source_target_pairs={{0,16},{1,5},{2,18},{3,7},{4,20},{5,1},{6,22},{7,3},{8,24},{9,13},... | collective-permute-start | bytes 172040 | tf_op jit(solution)/shard_map/ppermute | solution.py:563
  11.5 2.7 %collective-permute-done.4.refs_1_ = f32[112,128]{1,0:T(8,128)S(1)} collective-permute-done((f32[112,128]{1,0:T(8,128)S(1)}, f32[112,128]{1,0:T(8,128)S(1)}, u32[]{:S(2)}, u32[]{:S(2)}) %collective-permute-start.4) | collective-permute-done | bytes 57376 | tf_op jit(solution)/shard_map/ppermute | solution.py:563
  14.1 0.0 collective-permute-done.2.refs_2_.halo1
  14.1 0.2 collective-permute-done.3.refs_3_.halo2
  14.3 0.0 copy-done.2
  14.3 1.2 %shard_map.106 = (f32[3,360,128]{2,1,0:T(8,128)S(1)}, f32[3,360,128]{2,1,0:T(8,128)S(1)}, f32[3,360,128]{2,1,0:T(8,128)S(1)}, f32[3,360,128]{2,1,0:T(8,128)S(1)}...) custom-call(f32[2,320,128]{2,1,0:T(8,128)S(1)} %copy-done, ...), custom_call_target="tpu_custom_call" | custom-call | tf_op jit(solution)/shard_map/pallas_call | solution.py:252
  15.5 0.0 copy-start.6
  15.5 3.4 %shard_map.107 = (f32[2,320,128]{2,1,0:T(8,128)S(1)}, f32[1,128]{1,0:T(1,128)S(1)}) custom-call(f32[2,320,128]{2,1,0:T(8,128)S(1)} %copy-done, s32[2,320,128]{2,1,0:T(8,128)S(1)} %copy-done.1, f32[2,320,128]{2,1,0:T(8,128)S(1)} %copy-done.2, f32[8,128]{1,0:T(8,128)S(1)} %get-tuple-element.27.squares, f32[3,360,128]{2,1,0:T(8,128)S(1)} %get-tuple-element.28.first_field, ...), custom_call_target="tpu_custom_call" | custom-call | tf_op jit(solution)/shard_map/pallas_call | solution.py:473
  18.9 0.1 collective-permute-start.5
  19.0 3.5 %collective-permute-done.5.refs_1_ = f32[1,128]{1,0:T(1,128)S(1)} collective-permute-done((f32[1,128]{1,0:T(1,128)S(1)}, f32[1,128]{1,0:T(1,128)S(1)}, u32[]{:S(2)}, u32[]{:S(2)}) %collective-permute-start.5) | collective-permute-done | bytes 544 | tf_op jit(solution)/shard_map/ppermute | solution.py:539
  22.5 0.0 collective-permute-start.6
  22.5 3.6 %collective-permute-done.6.refs_2_ = f32[2,128]{1,0:T(2,128)S(1)} collective-permute-done((f32[2,128]{1,0:T(2,128)S(1)}, f32[2,128]{1,0:T(2,128)S(1)}, u32[]{:S(2)}, u32[]{:S(2)}) %collective-permute-start.6) | collective-permute-done | bytes 1056 | tf_op jit(solution)/shard_map/ppermute | solution.py:539
  26.1 0.8 %collective-permute-start.7 = (f32[4,128]{1,0:T(4,128)S(1)}, f32[4,128]{1,0:T(4,128)S(1)}, u32[]{:S(2)}, u32[]{:S(2)}) collective-permute-start(f32[4,128]{1,0:T(4,128)S(1)} %pad_maximum_fusion.1), channel_id=1, source_target_pairs={{0,8},{2,10},{4,12},{6,14},{8,0},{10,2},{12,4},{14,6},{1,9},{3,11}... | collective-permute-start | bytes 6152 | tf_op jit(solution)/shard_map/ppermute | solution.py:539
  26.9 3.8 %collective-permute-done.7.refs_3_ = f32[4,128]{1,0:T(4,128)S(1)} collective-permute-done((f32[4,128]{1,0:T(4,128)S(1)}, f32[4,128]{1,0:T(4,128)S(1)}, u32[]{:S(2)}, u32[]{:S(2)}) %collective-permute-start.7) | collective-permute-done | bytes 2080 | tf_op jit(solution)/shard_map/ppermute | solution.py:539
  30.7 0.9 %collective-permute-start.8 = (f32[8,128]{1,0:T(8,128)S(1)}, f32[8,128]{1,0:T(8,128)S(1)}, u32[]{:S(2)}, u32[]{:S(2)}) collective-permute-start(f32[8,128]{1,0:T(8,128)S(1)} %pad_maximum_fusion), channel_id=1, source_target_pairs={{0,1},{1,0},{2,3},{3,2},{4,5},{5,4},{6,7},{7,6},{8,9},{9,8},{10,11... | collective-permute-start | bytes 12296 | tf_op jit(solution)/shard_map/ppermute | solution.py:539
  31.5 0.8 %collective-permute-done.8.refs_4_ = f32[8,128]{1,0:T(8,128)S(1)} collective-permute-done((f32[8,128]{1,0:T(8,128)S(1)}, f32[8,128]{1,0:T(8,128)S(1)}, u32[]{:S(2)}, u32[]{:S(2)}) %collective-permute-start.8) | collective-permute-done | bytes 4128 | tf_op jit(solution)/shard_map/ppermute | solution.py:539
  32.3 0.0 copy-done.6
  32.3 1.1 %shard_map.108 = (f32[2,320,128]{2,1,0:T(8,128)}, f32[2,320,128]{2,1,0:T(8,128)}, f32[2,320,128]{2,1,0:T(8,128)}) custom-call(f32[1,128]{1,0:T(1,128)S(1)} %get-tuple-element.35.refs_0_, f32[1,128]{1,0:T(1,128)S(1)} %collective-permute-done.5.refs_1_, f32[2,128]{1,0:T(2,128)S(1)} %collective-permute-done.6.refs_2_, ...), custom_call_target="tpu_custom_call" | custom-call | tf_op jit(solution)/shard_map/pallas_call | solution.py:528
  (4 shorter events, 0.0 us)
Async XLA Ops:
  0.6 2.4 %copy-start = (f32[2,320,128]{2,1,0:T(8,128)S(1)}, f32[2,320,128]{2,1,0:T(8,128)}, u32[]{:S(2)}) copy-start(f32[2,320,128]{2,1,0:T(8,128)} %refs_7_.1) | copy-start | bytes 983044
  0.6 2.4 %copy-start.1 = (s32[2,320,128]{2,1,0:T(8,128)S(1)}, s32[2,320,128]{2,1,0:T(8,128)}, u32[]{:S(2)}) copy-start(s32[2,320,128]{2,1,0:T(8,128)} %sea.7) | copy-start | bytes 983044
  0.7 2.4 %copy-start.3 = (f32[2,320,128]{2,1,0:T(8,128)S(1)}, f32[2,320,128]{2,1,0:T(8,128)}, u32[]{:S(2)}) copy-start(f32[2,320,128]{2,1,0:T(8,128)} %pw.5) | copy-start | bytes 983044
  0.7 2.4 %copy-start.4 = (f32[320,128]{1,0:T(8,128)S(1)}, f32[320,128]{1,0:T(8,128)}, u32[]{:S(2)}) copy-start(f32[320,128]{1,0:T(8,128)} %ek.5) | copy-start | bytes 491524
  0.7 2.4 %copy-start.5 = (f32[320,128]{1,0:T(8,128)S(1)}, f32[320,128]{1,0:T(8,128)}, u32[]{:S(2)}) copy-start(f32[320,128]{1,0:T(8,128)} %nk.5) | copy-start | bytes 491524
  1.7 1.4 %collective-permute-start = (f32[8,8,128]{2,1,0:T(8,128)S(1)}, f32[8,8,128]{2,1,0:T(8,128)S(1)}, u32[]{:S(2)}, u32[]{:S(2)}) collective-permute-start(f32[8,8,128]{2,1,0:T(8,128)S(1)} %get-tuple-element.20), channel_id=1, source_target_pairs={{0,1},{1,0},{2,3},{3,2},{4,5},{5,4},{6,7},{7,6},{8,9},{9,8},{10,11... | collective-permute-start | bytes 98312 | tf_op jit(solution)/shard_map/ppermute | solution.py:539
  2.2 0.7 %collective-permute-start.1 = (f32[56,128]{1,0:T(8,128)S(1)}, f32[56,128]{1,0:T(8,128)S(1)}, u32[]{:S(2)}, u32[]{:S(2)}) collective-permute-start(f32[56,128]{1,0:T(8,128)S(1)} %get-tuple-element.21.refs_0_), channel_id=1, source_target_pairs={{1,9},{3,11},{5,13},{7,15},{9,1},{11,3},{13,5},{15,7},{17,25},{19,... | collective-permute-start | bytes 86024 | tf_op jit(solution)/shard_map/ppermute | solution.py:563
  3.5 10.9 %copy-start.2 = (f32[2,320,128]{2,1,0:T(8,128)S(1)}, f32[2,320,128]{2,1,0:T(8,128)}, u32[]{:S(2)}) copy-start(f32[2,320,128]{2,1,0:T(8,128)} %refs_6_.1) | copy-start | bytes 983044
  3.5 10.7 %collective-permute-start.2 = (f32[280,128]{1,0:T(8,128)S(1)}, f32[280,128]{1,0:T(8,128)S(1)}, u32[]{:S(2)}, u32[]{:S(2)}) collective-permute-start(f32[280,128]{1,0:T(8,128)S(1)} %get-tuple-element.22), channel_id=1, source_target_pairs={{0,2},{2,0},{4,6},{6,4},{8,10},{10,8},{12,14},{14,12},{1,3},{3,1},... | collective-permute-start | bytes 430088 | tf_op jit(solution)/shard_map/ppermute | solution.py:539
  6.4 7.9 %collective-permute-start.3 = (f32[280,128]{1,0:T(8,128)S(1)}, f32[280,128]{1,0:T(8,128)S(1)}, u32[]{:S(2)}, u32[]{:S(2)}) collective-permute-start(f32[280,128]{1,0:T(8,128)S(1)} %get-tuple-element.23), channel_id=1, source_target_pairs={{2,4},{4,2},{6,8},{8,6},{10,12},{12,10},{14,0},{0,14},{3,5},{5,3},... | collective-permute-start | bytes 430088 | tf_op jit(solution)/shard_map/ppermute | solution.py:547
  10.0 4.2 %collective-permute-start.4 = (f32[112,128]{1,0:T(8,128)S(1)}, f32[112,128]{1,0:T(8,128)S(1)}, u32[]{:S(2)}, u32[]{:S(2)}) collective-permute-start(f32[112,128]{1,0:T(8,128)S(1)} %get-tuple-element.25.refs_0_), channel_id=1, source_target_pairs={{0,16},{1,5},{2,18},{3,7},{4,20},{5,1},{6,22},{7,3},{8,24},{9,13},... | collective-permute-start | bytes 172040 | tf_op jit(solution)/shard_map/ppermute | solution.py:563
  15.5 16.8 %copy-start.6 = (f32[2,320,128]{2,1,0:T(8,128)S(1)}, f32[2,320,128]{2,1,0:T(8,128)}, u32[]{:S(2)}) copy-start(f32[2,320,128]{2,1,0:T(8,128)} %refs_5_.1) | copy-start | bytes 983044
  18.9 3.6 %collective-permute-start.5 = (f32[1,128]{1,0:T(1,128)S(1)}, f32[1,128]{1,0:T(1,128)S(1)}, u32[]{:S(2)}, u32[]{:S(2)}) collective-permute-start(f32[1,128]{1,0:T(1,128)S(1)} %get-tuple-element.35.refs_0_), channel_id=1, source_target_pairs={{0,2},{2,0},{4,6},{6,4},{8,10},{10,8},{12,14},{14,12},{1,3},{3,1},... | collective-permute-start | bytes 1544 | tf_op jit(solution)/shard_map/ppermute | solution.py:539
  22.5 3.6 %collective-permute-start.6 = (f32[2,128]{1,0:T(2,128)S(1)}, f32[2,128]{1,0:T(2,128)S(1)}, u32[]{:S(2)}, u32[]{:S(2)}) collective-permute-start(f32[2,128]{1,0:T(2,128)S(1)} %pad_maximum_fusion.2), channel_id=1, source_target_pairs={{0,4},{2,6},{4,0},{6,2},{8,12},{10,14},{12,8},{14,10},{1,5},{3,7},... | collective-permute-start | bytes 3080 | tf_op jit(solution)/shard_map/ppermute | solution.py:539
  26.1 4.5 %collective-permute-start.7 = (f32[4,128]{1,0:T(4,128)S(1)}, f32[4,128]{1,0:T(4,128)S(1)}, u32[]{:S(2)}, u32[]{:S(2)}) collective-permute-start(f32[4,128]{1,0:T(4,128)S(1)} %pad_maximum_fusion.1), channel_id=1, source_target_pairs={{0,8},{2,10},{4,12},{6,14},{8,0},{10,2},{12,4},{14,6},{1,9},{3,11}... | collective-permute-start | bytes 6152 | tf_op jit(solution)/shard_map/ppermute | solution.py:539
  30.7 1.7 %collective-permute-start.8 = (f32[8,128]{1,0:T(8,128)S(1)}, f32[8,128]{1,0:T(8,128)S(1)}, u32[]{:S(2)}, u32[]{:S(2)}) collective-permute-start(f32[8,128]{1,0:T(8,128)S(1)} %pad_maximum_fusion), channel_id=1, source_target_pairs={{0,1},{1,0},{2,3},{3,2},{4,5},{5,4},{6,7},{7,6},{8,9},{9,8},{10,11... | collective-permute-start | bytes 12296 | tf_op jit(solution)/shard_map/ppermute | solution.py:539

commit v8 on v7

--- a/solution.py
+++ b/solution.py
@@ -24,7 +24,7 @@
 
 
 def place(kind, level, half):
-    return 8 * kind + 32 * half + 64 * level
+    return 16 * kind + 8 * half + 64 * level
 
 
 STRIP = 56
@@ -172,17 +172,13 @@
     half_groups = groups // 2
     lane = lanes_of((8, LANES))
     zero = jnp.zeros((8, LANES), f32)
-    right = (lane & 63) < 32
     low = (lane < 32) | (lane >= 96)
     near = ((lane & 63) < 8) | ((lane & 63) >= 56)
     at = slab_index
 
     def beside_slabs(from_east, from_west, half):
-        out = []
-        for kind, extra in ((0, 0), (1, 0), (2, 0), (3, 0), (3, 64)):
-            r = turn(from_east, extra - (place(kind, 0, half) + 8))
-            w = turn(from_west, extra + 120 - place(kind, 0, half))
-            out.append(jnp.where(right, r, w))
+        both = jnp.where((lane & 8) == 8 * half, from_west, from_east)
+        out = [turn(both, extra + 120 - place(kind, 0, half)) for kind, extra in ((0, 0), (1, 0), (2, 0), (3, 0), (3, 64))]
         pair, pair_turned = out[3:]
         out[3:] = [jnp.where(low, pair, pair_turned), jnp.where(low, pair_turned, pair)]
         out[1] = jnp.where(near, out[1], 0.0)

time: 33.7 us -> 33.5 us (level)
  no operation moved by 1% of the time
where the time goes in v8:
time: 33.5 us; the launch traced here: 33.3 us
  waiting for transfers between devices  14.8 us (44%)
  starting transfers between devices  10.8 us (32%)
  Pallas kernels  6.85 us (20%)
  between operations  0.79 us (2%)
    ppermute x6, waiting for transfers between devices, swapped(): lax.ppermute(value, axis, [(i, i ^ distance) for i in range(lax.axis_size...  11.9 us
    ppermute x6, starting transfers between devices, swapped(): lax.ppermute(value, axis, [(i, i ^ distance) for i in range(lax.axis_size...  5.13 us
    ppermute x1, starting transfers between devices, odd_pairs(): return lax.ppermute(value, axis, pairs)  3.54 us
    pallas_call x1, Pallas kernels, image_and_stats(): pl.pallas_call(image_kernel, out_shape=[jax.ShapeDtypeStruct(d.shape, f32...  3.36 us
    ppermute x2, waiting for transfers between devices, strip_swap(): lax.ppermute(value, ('member', 'lon', 'lat'), [(number(*p), other(*p)) fo...  2.69 us
    ppermute x2, starting transfers between devices, strip_swap(): lax.ppermute(value, ('member', 'lon', 'lat'), [(number(*p), other(*p)) fo...  2.14 us
    pallas_call x1, Pallas kernels, update(): pl.pallas_call(functools.partial(update_kernel, len(parts)), out_shape=[j...  1.14 us
    pallas_call x1, Pallas kernels, rows_to_send(): pl.pallas_call(functools.partial(rows_kernel, 'lat'), out_shape=[jax.Shap...  0.98 us
  transfers between devices with their start and end apart: 9, of which 7 were waited for; matrix products, arithmetic and copies ran while one was open for 0% of the time, Pallas kernels for 0%

profile of v8, /device:TPU:0, one launch (start us, length us, event | category | flops | bytes accessed | tf_op | source)
XLA Modules:
  0.0 33.3 jit_solution(285975399632406720)
XLA Ops:
  0.6 0.0 copy-start
  0.6 0.0 copy-start.1
  0.7 0.0 copy-start.3
  0.7 0.0 copy-start.4
  0.7 0.0 copy-start.5
  0.7 1.0 %shard_map.103 = (f32[56,128]{1,0:T(8,128)S(1)}, f32[8,8,128]{2,1,0:T(8,128)S(1)}, s32[8,128]{1,0:T(8,128)S(1)}) custom-call(f32[2,320,128]{2,1,0:T(8,128)} %refs_7_.1, s32[2,320,128]{2,1,0:T(8,128)} %sea.7, f32[2,320,128]{2,1,0:T(8,128)} %pw.5, f32[320,128]{1,0:T(8,128)} %ek.5, f32[320,128]{1,0:T(8,128)} %nk.5, s32[8,128]{1,0:T(8,128)} %bitcast.1), custom_call_target="tpu_custom_call" | custom-call | tf_op jit(solution)/shard_map/pallas_call | solution.py:67
  1.7 0.5 %collective-permute-start = (f32[8,8,128]{2,1,0:T(8,128)S(1)}, f32[8,8,128]{2,1,0:T(8,128)S(1)}, u32[]{:S(2)}, u32[]{:S(2)}) collective-permute-start(f32[8,8,128]{2,1,0:T(8,128)S(1)} %get-tuple-element.20), channel_id=1, source_target_pairs={{0,1},{1,0},{2,3},{3,2},{4,5},{5,4},{6,7},{7,6},{8,9},{9,8},{10,11... | collective-permute-start | bytes 98312 | tf_op jit(solution)/shard_map/ppermute | solution.py:535
  2.2 0.7 %collective-permute-start.1 = (f32[56,128]{1,0:T(8,128)S(1)}, f32[56,128]{1,0:T(8,128)S(1)}, u32[]{:S(2)}, u32[]{:S(2)}) collective-permute-start(f32[56,128]{1,0:T(8,128)S(1)} %get-tuple-element.21.refs_0_), channel_id=1, source_target_pairs={{1,9},{3,11},{5,13},{7,15},{9,1},{11,3},{13,5},{15,7},{17,25},{19,... | collective-permute-start | bytes 86024 | tf_op jit(solution)/shard_map/ppermute | solution.py:559
  2.8 0.0 collective-permute-done.1.refs_1_
  2.9 0.2 collective-permute-done.rows_in
  3.0 0.0 copy-done
  3.0 0.0 copy-done.1
  3.0 0.0 copy-done.3
  3.1 0.0 copy-done.4
  3.1 0.0 copy-done.5
  3.1 0.4 %shard_map.104 = (f32[280,128]{1,0:T(8,128)S(1)}, f32[280,128]{1,0:T(8,128)S(1)}, f32[112,128]{1,0:T(8,128)S(1)}) custom-call(f32[2,320,128]{2,1,0:T(8,128)S(1)} %copy-done, s32[2,320,128]{2,1,0:T(8,128)S(1)} %copy-done.1, f32[2,320,128]{2,1,0:T(8,128)S(1)} %copy-done.3, f32[320,128]{1,0:T(8,128)S(1)} %copy-done.4, f32[320,128]{1,0:T(8,128)S(1)} %copy-done.5, ...), custom_call_target="tpu_custom_call" | custom-call | tf_op jit(solution)/shard_map/pallas_call | solution.py:132
  3.5 0.0 copy-start.2
  3.5 2.9 %collective-permute-start.2 = (f32[280,128]{1,0:T(8,128)S(1)}, f32[280,128]{1,0:T(8,128)S(1)}, u32[]{:S(2)}, u32[]{:S(2)}) collective-permute-start(f32[280,128]{1,0:T(8,128)S(1)} %get-tuple-element.22), channel_id=1, source_target_pairs={{0,2},{2,0},{4,6},{6,4},{8,10},{10,8},{12,14},{14,12},{1,3},{3,1},... | collective-permute-start | bytes 430088 | tf_op jit(solution)/shard_map/ppermute | solution.py:535
  6.4 3.5 %collective-permute-start.3 = (f32[280,128]{1,0:T(8,128)S(1)}, f32[280,128]{1,0:T(8,128)S(1)}, u32[]{:S(2)}, u32[]{:S(2)}) collective-permute-start(f32[280,128]{1,0:T(8,128)S(1)} %get-tuple-element.23), channel_id=1, source_target_pairs={{2,4},{4,2},{6,8},{8,6},{10,12},{12,10},{14,0},{0,14},{3,5},{5,3},... | collective-permute-start | bytes 430088 | tf_op jit(solution)/shard_map/ppermute | solution.py:543
  10.0 1.5 %collective-permute-start.4 = (f32[112,128]{1,0:T(8,128)S(1)}, f32[112,128]{1,0:T(8,128)S(1)}, u32[]{:S(2)}, u32[]{:S(2)}) collective-permute-start(f32[112,128]{1,0:T(8,128)S(1)} %get-tuple-element.25.refs_0_), channel_id=1, source_target_pairs={{0,16},{1,5},{2,18},{3,7},{4,20},{5,1},{6,22},{7,3},{8,24},{9,13},... | collective-permute-start | bytes 172040 | tf_op jit(solution)/shard_map/ppermute | solution.py:559
  11.5 2.7 %collective-permute-done.4.refs_1_ = f32[112,128]{1,0:T(8,128)S(1)} collective-permute-done((f32[112,128]{1,0:T(8,128)S(1)}, f32[112,128]{1,0:T(8,128)S(1)}, u32[]{:S(2)}, u32[]{:S(2)}) %collective-permute-start.4) | collective-permute-done | bytes 57376 | tf_op jit(solution)/shard_map/ppermute | solution.py:559
  14.1 0.0 collective-permute-done.2.refs_2_.halo1
  14.1 0.2 collective-permute-done.3.refs_3_.halo2
  14.3 0.0 copy-done.2
  14.3 1.0 %shard_map.106 = (f32[3,360,128]{2,1,0:T(8,128)S(1)}, f32[3,360,128]{2,1,0:T(8,128)S(1)}, f32[3,360,128]{2,1,0:T(8,128)S(1)}, f32[3,360,128]{2,1,0:T(8,128)S(1)}...) custom-call(f32[2,320,128]{2,1,0:T(8,128)S(1)} %copy-done, ...), custom_call_target="tpu_custom_call" | custom-call | tf_op jit(solution)/shard_map/pallas_call | solution.py:248
  15.3 0.0 copy-start.6
  15.3 3.4 %shard_map.107 = (f32[2,320,128]{2,1,0:T(8,128)S(1)}, f32[1,128]{1,0:T(1,128)S(1)}) custom-call(f32[2,320,128]{2,1,0:T(8,128)S(1)} %copy-done, s32[2,320,128]{2,1,0:T(8,128)S(1)} %copy-done.1, f32[2,320,128]{2,1,0:T(8,128)S(1)} %copy-done.2, f32[8,128]{1,0:T(8,128)S(1)} %get-tuple-element.27.squares, f32[3,360,128]{2,1,0:T(8,128)S(1)} %get-tuple-element.28.first_field, ...), custom_call_target="tpu_custom_call" | custom-call | tf_op jit(solution)/shard_map/pallas_call | solution.py:469
  18.7 0.1 collective-permute-start.5
  18.8 3.5 %collective-permute-done.5.refs_1_ = f32[1,128]{1,0:T(1,128)S(1)} collective-permute-done((f32[1,128]{1,0:T(1,128)S(1)}, f32[1,128]{1,0:T(1,128)S(1)}, u32[]{:S(2)}, u32[]{:S(2)}) %collective-permute-start.5) | collective-permute-done | bytes 544 | tf_op jit(solution)/shard_map/ppermute | solution.py:535
  22.3 0.0 collective-permute-start.6
  22.3 3.6 %collective-permute-done.6.refs_2_ = f32[2,128]{1,0:T(2,128)S(1)} collective-permute-done((f32[2,128]{1,0:T(2,128)S(1)}, f32[2,128]{1,0:T(2,128)S(1)}, u32[]{:S(2)}, u32[]{:S(2)}) %collective-permute-start.6) | collective-permute-done | bytes 1056 | tf_op jit(solution)/shard_map/ppermute | solution.py:535
  25.9 0.8 %collective-permute-start.7 = (f32[4,128]{1,0:T(4,128)S(1)}, f32[4,128]{1,0:T(4,128)S(1)}, u32[]{:S(2)}, u32[]{:S(2)}) collective-permute-start(f32[4,128]{1,0:T(4,128)S(1)} %pad_maximum_fusion.1), channel_id=1, source_target_pairs={{0,8},{2,10},{4,12},{6,14},{8,0},{10,2},{12,4},{14,6},{1,9},{3,11}... | collective-permute-start | bytes 6152 | tf_op jit(solution)/shard_map/ppermute | solution.py:535
  26.7 3.8 %collective-permute-done.7.refs_3_ = f32[4,128]{1,0:T(4,128)S(1)} collective-permute-done((f32[4,128]{1,0:T(4,128)S(1)}, f32[4,128]{1,0:T(4,128)S(1)}, u32[]{:S(2)}, u32[]{:S(2)}) %collective-permute-start.7) | collective-permute-done | bytes 2080 | tf_op jit(solution)/shard_map/ppermute | solution.py:535
  30.5 0.9 %collective-permute-start.8 = (f32[8,128]{1,0:T(8,128)S(1)}, f32[8,128]{1,0:T(8,128)S(1)}, u32[]{:S(2)}, u32[]{:S(2)}) collective-permute-start(f32[8,128]{1,0:T(8,128)S(1)} %pad_maximum_fusion), channel_id=1, source_target_pairs={{0,1},{1,0},{2,3},{3,2},{4,5},{5,4},{6,7},{7,6},{8,9},{9,8},{10,11... | collective-permute-start | bytes 12296 | tf_op jit(solution)/shard_map/ppermute | solution.py:535
  31.3 0.8 %collective-permute-done.8.refs_4_ = f32[8,128]{1,0:T(8,128)S(1)} collective-permute-done((f32[8,128]{1,0:T(8,128)S(1)}, f32[8,128]{1,0:T(8,128)S(1)}, u32[]{:S(2)}, u32[]{:S(2)}) %collective-permute-start.8) | collective-permute-done | bytes 4128 | tf_op jit(solution)/shard_map/ppermute | solution.py:535
  32.1 0.0 copy-done.6
  32.1 1.1 %shard_map.108 = (f32[2,320,128]{2,1,0:T(8,128)}, f32[2,320,128]{2,1,0:T(8,128)}, f32[2,320,128]{2,1,0:T(8,128)}) custom-call(f32[1,128]{1,0:T(1,128)S(1)} %get-tuple-element.35.refs_0_, f32[1,128]{1,0:T(1,128)S(1)} %collective-permute-done.5.refs_1_, f32[2,128]{1,0:T(2,128)S(1)} %collective-permute-done.6.refs_2_, ...), custom_call_target="tpu_custom_call" | custom-call | tf_op jit(solution)/shard_map/pallas_call | solution.py:524
  (4 shorter events, 0.0 us)
Async XLA Ops:
  0.6 2.4 %copy-start = (f32[2,320,128]{2,1,0:T(8,128)S(1)}, f32[2,320,128]{2,1,0:T(8,128)}, u32[]{:S(2)}) copy-start(f32[2,320,128]{2,1,0:T(8,128)} %refs_7_.1) | copy-start | bytes 983044
  0.6 2.4 %copy-start.1 = (s32[2,320,128]{2,1,0:T(8,128)S(1)}, s32[2,320,128]{2,1,0:T(8,128)}, u32[]{:S(2)}) copy-start(s32[2,320,128]{2,1,0:T(8,128)} %sea.7) | copy-start | bytes 983044
  0.7 2.4 %copy-start.3 = (f32[2,320,128]{2,1,0:T(8,128)S(1)}, f32[2,320,128]{2,1,0:T(8,128)}, u32[]{:S(2)}) copy-start(f32[2,320,128]{2,1,0:T(8,128)} %pw.5) | copy-start | bytes 983044
  0.7 2.4 %copy-start.4 = (f32[320,128]{1,0:T(8,128)S(1)}, f32[320,128]{1,0:T(8,128)}, u32[]{:S(2)}) copy-start(f32[320,128]{1,0:T(8,128)} %ek.5) | copy-start | bytes 491524
  0.7 2.4 %copy-start.5 = (f32[320,128]{1,0:T(8,128)S(1)}, f32[320,128]{1,0:T(8,128)}, u32[]{:S(2)}) copy-start(f32[320,128]{1,0:T(8,128)} %nk.5) | copy-start | bytes 491524
  1.7 1.4 %collective-permute-start = (f32[8,8,128]{2,1,0:T(8,128)S(1)}, f32[8,8,128]{2,1,0:T(8,128)S(1)}, u32[]{:S(2)}, u32[]{:S(2)}) collective-permute-start(f32[8,8,128]{2,1,0:T(8,128)S(1)} %get-tuple-element.20), channel_id=1, source_target_pairs={{0,1},{1,0},{2,3},{3,2},{4,5},{5,4},{6,7},{7,6},{8,9},{9,8},{10,11... | collective-permute-start | bytes 98312 | tf_op jit(solution)/shard_map/ppermute | solution.py:535
  2.2 0.7 %collective-permute-start.1 = (f32[56,128]{1,0:T(8,128)S(1)}, f32[56,128]{1,0:T(8,128)S(1)}, u32[]{:S(2)}, u32[]{:S(2)}) collective-permute-start(f32[56,128]{1,0:T(8,128)S(1)} %get-tuple-element.21.refs_0_), channel_id=1, source_target_pairs={{1,9},{3,11},{5,13},{7,15},{9,1},{11,3},{13,5},{15,7},{17,25},{19,... | collective-permute-start | bytes 86024 | tf_op jit(solution)/shard_map/ppermute | solution.py:559
  3.5 10.9 %copy-start.2 = (f32[2,320,128]{2,1,0:T(8,128)S(1)}, f32[2,320,128]{2,1,0:T(8,128)}, u32[]{:S(2)}) copy-start(f32[2,320,128]{2,1,0:T(8,128)} %refs_6_.1) | copy-start | bytes 983044
  3.5 10.7 %collective-permute-start.2 = (f32[280,128]{1,0:T(8,128)S(1)}, f32[280,128]{1,0:T(8,128)S(1)}, u32[]{:S(2)}, u32[]{:S(2)}) collective-permute-start(f32[280,128]{1,0:T(8,128)S(1)} %get-tuple-element.22), channel_id=1, source_target_pairs={{0,2},{2,0},{4,6},{6,4},{8,10},{10,8},{12,14},{14,12},{1,3},{3,1},... | collective-permute-start | bytes 430088 | tf_op jit(solution)/shard_map/ppermute | solution.py:535
  6.4 7.9 %collective-permute-start.3 = (f32[280,128]{1,0:T(8,128)S(1)}, f32[280,128]{1,0:T(8,128)S(1)}, u32[]{:S(2)}, u32[]{:S(2)}) collective-permute-start(f32[280,128]{1,0:T(8,128)S(1)} %get-tuple-element.23), channel_id=1, source_target_pairs={{2,4},{4,2},{6,8},{8,6},{10,12},{12,10},{14,0},{0,14},{3,5},{5,3},... | collective-permute-start | bytes 430088 | tf_op jit(solution)/shard_map/ppermute | solution.py:543
  10.0 4.2 %collective-permute-start.4 = (f32[112,128]{1,0:T(8,128)S(1)}, f32[112,128]{1,0:T(8,128)S(1)}, u32[]{:S(2)}, u32[]{:S(2)}) collective-permute-start(f32[112,128]{1,0:T(8,128)S(1)} %get-tuple-element.25.refs_0_), channel_id=1, source_target_pairs={{0,16},{1,5},{2,18},{3,7},{4,20},{5,1},{6,22},{7,3},{8,24},{9,13},... | collective-permute-start | bytes 172040 | tf_op jit(solution)/shard_map/ppermute | solution.py:559
  15.3 16.8 %copy-start.6 = (f32[2,320,128]{2,1,0:T(8,128)S(1)}, f32[2,320,128]{2,1,0:T(8,128)}, u32[]{:S(2)}) copy-start(f32[2,320,128]{2,1,0:T(8,128)} %refs_5_.1) | copy-start | bytes 983044
  18.7 3.6 %collective-permute-start.5 = (f32[1,128]{1,0:T(1,128)S(1)}, f32[1,128]{1,0:T(1,128)S(1)}, u32[]{:S(2)}, u32[]{:S(2)}) collective-permute-start(f32[1,128]{1,0:T(1,128)S(1)} %get-tuple-element.35.refs_0_), channel_id=1, source_target_pairs={{0,2},{2,0},{4,6},{6,4},{8,10},{10,8},{12,14},{14,12},{1,3},{3,1},... | collective-permute-start | bytes 1544 | tf_op jit(solution)/shard_map/ppermute | solution.py:535
  22.3 3.6 %collective-permute-start.6 = (f32[2,128]{1,0:T(2,128)S(1)}, f32[2,128]{1,0:T(2,128)S(1)}, u32[]{:S(2)}, u32[]{:S(2)}) collective-permute-start(f32[2,128]{1,0:T(2,128)S(1)} %pad_maximum_fusion.2), channel_id=1, source_target_pairs={{0,4},{2,6},{4,0},{6,2},{8,12},{10,14},{12,8},{14,10},{1,5},{3,7},... | collective-permute-start | bytes 3080 | tf_op jit(solution)/shard_map/ppermute | solution.py:535
  25.9 4.5 %collective-permute-start.7 = (f32[4,128]{1,0:T(4,128)S(1)}, f32[4,128]{1,0:T(4,128)S(1)}, u32[]{:S(2)}, u32[]{:S(2)}) collective-permute-start(f32[4,128]{1,0:T(4,128)S(1)} %pad_maximum_fusion.1), channel_id=1, source_target_pairs={{0,8},{2,10},{4,12},{6,14},{8,0},{10,2},{12,4},{14,6},{1,9},{3,11}... | collective-permute-start | bytes 6152 | tf_op jit(solution)/shard_map/ppermute | solution.py:535
  30.5 1.7 %collective-permute-start.8 = (f32[8,128]{1,0:T(8,128)S(1)}, f32[8,128]{1,0:T(8,128)S(1)}, u32[]{:S(2)}, u32[]{:S(2)}) collective-permute-start(f32[8,128]{1,0:T(8,128)S(1)} %pad_maximum_fusion), channel_id=1, source_target_pairs={{0,1},{1,0},{2,3},{3,2},{4,5},{5,4},{6,7},{7,6},{8,9},{9,8},{10,11... | collective-permute-start | bytes 12296 | tf_op jit(solution)/shard_map/ppermute | solution.py:535

commit v9 on v8

--- a/solution.py
+++ b/solution.py
@@ -162,66 +162,39 @@
     )
 
 
-def coefficient_kernel(
-    lon_axis, lat_axis, d, sea, pw, ek, nk, res, halo1, halo2, rows_in, face_in,
-    field, weight, east_c, west_c, north_c, squares, face, ocean,
+def own_kernel(
+    lat_axis, d, sea, pw, ek, nk, res, rows_in,
+    field, weight, east_c, west_c, north_c, oc_edge, ek_edge, squares, ocean,
 ):
     top = lax.axis_index(lat_axis) == 1
-    even = lax.axis_index(lon_axis) % 2 == 0
     groups = d.shape[1] // 8
-    half_groups = groups // 2
     lane = lanes_of((8, LANES))
     zero = jnp.zeros((8, LANES), f32)
-    low = (lane < 32) | (lane >= 96)
-    near = ((lane & 63) < 8) | ((lane & 63) >= 56)
     at = slab_index
 
-    def beside_slabs(from_east, from_west, half):
-        both = jnp.where((lane & 8) == 8 * half, from_west, from_east)
-        out = [turn(both, extra + 120 - place(kind, 0, half)) for kind, extra in ((0, 0), (1, 0), (2, 0), (3, 0), (3, 64))]
-        pair, pair_turned = out[3:]
-        out[3:] = [jnp.where(low, pair, pair_turned), jnp.where(low, pair_turned, pair)]
-        out[1] = jnp.where(near, out[1], 0.0)
-        return out
-
-    def set_group(group, planes, side):
-        ek_here, nk_here = planes[6], planes[7]
-        d_s = (planes[0], turn(planes[1], 64), side[0])
-        oc_s = (planes[2], turn(planes[3], 64), side[1])
-        pw_s = (planes[4], turn(planes[5], 64), side[2])
-        ek_s = (ek_here, turn(ek_here, 64), side[3])
-        nk_s = (nk_here, turn(nk_here, 64), side[4])
-        for s in range(3):
-            ocean[s, at(group), :] = oc_s[s]
-            field[s, at(group), :] = d_s[s] * oc_s[s]
-            weight[s, at(group), :] = pw_s[s] * oc_s[s]
-            east_c[s, at(group), :] = ek_s[s] * oc_s[s]
-            north_c[s, at(group), :] = nk_s[s] * oc_s[s]
-
-    last = groups + 2
-    for s in range(3):
-        for buffer in (ocean, north_c):
-            buffer[s, 0:8, :] = zero
-            buffer[s, 8 + 8 * last : 16 + 8 * last, :] = zero
+    def set_group(group, planes):
+        d0, d1, oc0, oc1, pw0, pw1, ek_here, nk_here = planes
+        turned = [turn(x, 64) for x in (d1, oc1, pw1, ek_here, nk_here)]
+        for s, (dv, oc, weights, east, north) in enumerate(((d0, oc0, pw0, ek_here, nk_here), turned)):
+            ocean[s, at(group), :] = oc
+            field[s, at(group), :] = dv * oc
+            weight[s, at(group), :] = weights * oc
+            east_c[s, at(group), :] = east * oc
+            north_c[s, at(group), :] = north * oc
+
+    for s in range(2):
+        ocean[s, at(groups + 2), :] = zero
     for group in range(groups):
         here = slice(8 * group, 8 * group + 8)
-        half, inside = divmod(group, half_groups)
-        there = slice(8 * inside, 8 * inside + 8)
-        a, b = halo1[there, :], halo2[there, :]
-        side = beside_slabs(jnp.where(even, a, b), jnp.where(even, b, a), half)
-        planes = [d[0, here, :], d[1, here, :], sea[0, here, :].astype(f32), sea[1, here, :].astype(f32),
-                  pw[0, here, :], pw[1, here, :], ek[here, :], nk[here, :]]
-        set_group(group + 1, planes, side)
-    planes = [rows_in[i] for i in range(8)]
-    corner = slice(8 * half_groups, 8 * half_groups + 8)
-    a, b = halo1[corner, :], halo2[corner, :]
-    side = beside_slabs(jnp.where(even, a, b), jnp.where(even, b, a), 0)
+        set_group(
+            group + 1,
+            [d[0, here, :], d[1, here, :], sea[0, here, :].astype(f32), sea[1, here, :].astype(f32),
+             pw[0, here, :], pw[1, here, :], ek[here, :], nk[here, :]],
+        )
     for group, used in ((0, top), (groups + 1, jnp.logical_not(top))):
-        masked, masked_side = list(planes), list(side)
-        masked[2] = jnp.where(used, planes[2], 0.0)
-        masked[3] = jnp.where(used, planes[3], 0.0)
-        masked_side[1] = jnp.where(used, side[1], 0.0)
-        set_group(group, masked, masked_side)
+        planes = [rows_in[i] for i in range(8)]
+        planes[2:4] = [jnp.where(used, x, 0.0) for x in planes[2:4]]
+        set_group(group, planes)
 
     total = zero
     for level in range(2):
@@ -229,31 +202,94 @@
             r = res[level, 8 * group : 8 * group + 8, :]
             total = total + r * r
     squares[...] = total
-    face[...] = face_in[...]
 
     for group in range(groups + 2):
         here = at(group)
-        oc = [ocean[s, here, :] for s in range(3)]
-        half_face = [east_c[s, here, :] for s in range(3)]
-        e, w = east_of(oc), west_of(half_face)
-        for s in range(3):
-            east_c[s, here, :] = half_face[s] * e[s]
-            west_c[s, here, :] = oc[s] * w[s]
+        oc = [ocean[s, here, :] for s in range(2)]
+        half_face = [east_c[s, here, :] for s in range(2)]
+        e = [turn(x, -1) for x in oc]
+        w = [turn(x, 1) for x in half_face]
+        for s in range(2):
+            east_c[s, here, :] = jnp.where(lane == 127 - 64 * s, half_face[s], half_face[s] * e[s])
+            west_c[s, here, :] = jnp.where(lane == 64 * s, oc[s], oc[s] * w[s])
             north_c[s, here, :] = north_c[s, here, :] * ocean[s, at(group, 1), :]
-
-
-def coefficients(d, sea, pw, ek, nk, res, halo1, halo2, rows_in, face):
+        oc_edge[here, :] = jnp.where(lane == 63, e[1], e[0])
+        ek_edge[here, :] = jnp.where(lane == 64, w[1], w[0])
+
+
+def own_coefficients(d, sea, pw, ek, nk, res, rows_in):
     full = pl.BlockSpec(memory_space=pltpu.VMEM)
-    extended = (3, d.shape[1] + 40, LANES)
+    rows = d.shape[1] + 40
     return pl.pallas_call(
-        functools.partial(coefficient_kernel, "lon", "lat"),
-        out_shape=[jax.ShapeDtypeStruct(extended, f32)] * 5
-        + [jax.ShapeDtypeStruct((8, LANES), f32), jax.ShapeDtypeStruct(face.shape, f32)],
-        in_specs=[full] * 10,
-        out_specs=[full] * 7,
-        scratch_shapes=[pltpu.VMEM(extended, f32)],
+        functools.partial(own_kernel, "lat"),
+        out_shape=[jax.ShapeDtypeStruct((3, rows, LANES), f32)] * 5
+        + [jax.ShapeDtypeStruct((n, LANES), f32) for n in (rows, rows, 8)],
+        in_specs=[full] * 7,
+        out_specs=[full] * 8,
+        scratch_shapes=[pltpu.VMEM((2, rows, LANES), f32)],
         compiler_params=pltpu.CompilerParams(vmem_limit_bytes=VMEM_LIMIT),
-    )(d, sea, pw, ek, nk, res, halo1, halo2, rows_in, face)
+    )(d, sea, pw, ek, nk, res, rows_in)
+
+
+def beside_kernel(
+    lon_axis, lat_axis, groups, oc_edge, ek_edge, halo1, halo2, face_in, field_in, weight_in, east_in, west_in, north_in,
+    field, weight, east_c, west_c, north_c, face, ocean,
+):
+    top = lax.axis_index(lat_axis) == 1
+    even = lax.axis_index(lon_axis) % 2 == 0
+    half_groups = groups // 2
+    lane = lanes_of((8, LANES))
+    low = (lane < 32) | (lane >= 96)
+    near = ((lane & 63) < 8) | ((lane & 63) >= 56)
+    at = slab_index
+
+    def set_group(group, line, half, used=None):
+        there = slice(8 * line, 8 * line + 8)
+        a, b = halo1[there, :], halo2[there, :]
+        from_east, from_west = jnp.where(even, a, b), jnp.where(even, b, a)
+        both = jnp.where((lane & 8) == 8 * half, from_west, from_east)
+        dv, oc, weights, pair, pair_turned = (
+            turn(both, extra + 120 - place(kind, 0, half)) for kind, extra in ((0, 0), (1, 0), (2, 0), (3, 0), (3, 64))
+        )
+        oc = jnp.where(near if used is None else near & used, oc, 0.0)
+        ocean[at(group), :] = oc
+        field[2, at(group), :] = dv * oc
+        weight[2, at(group), :] = weights * oc
+        east_c[2, at(group), :] = jnp.where(low, pair, pair_turned) * oc
+        north_c[2, at(group), :] = jnp.where(low, pair_turned, pair) * oc
+
+    ocean[at(groups + 2), :] = jnp.zeros((8, LANES), f32)
+    for group in range(groups):
+        set_group(group + 1, group % half_groups, group // half_groups)
+    set_group(0, half_groups, 0, top)
+    set_group(groups + 1, half_groups, 0, jnp.logical_not(top))
+    face[...] = face_in[...]
+
+    for group in range(groups + 2):
+        here = at(group)
+        oc, half_face = ocean[here, :], east_c[2, here, :]
+        e, w = turn(oc, -1), turn(half_face, 1)
+        east_c[2, here, :] = half_face * jnp.where((lane & 63) == 63, oc_edge[here, :], e)
+        west_c[2, here, :] = oc * jnp.where((lane & 63) == 0, ek_edge[here, :], w)
+        north_c[2, here, :] = north_c[2, here, :] * ocean[at(group, 1), :]
+        for s in range(2):
+            east, west = east_in[s, here, :], west_in[s, here, :]
+            east_c[s, here, :] = jnp.where(lane == 127 - 64 * s, east * e, east)
+            west_c[s, here, :] = jnp.where(lane == 64 * s, west * w, west)
+
+
+def with_columns_beside(groups, own, edges, halo1, halo2, face):
+    full = pl.BlockSpec(memory_space=pltpu.VMEM)
+    inputs = [*edges, halo1, halo2, face, *own]
+    return pl.pallas_call(
+        functools.partial(beside_kernel, "lon", "lat", groups),
+        out_shape=[jax.ShapeDtypeStruct(x.shape, f32) for x in (*own, face)],
+        in_specs=[full] * len(inputs),
+        out_specs=[full] * 6,
+        scratch_shapes=[pltpu.VMEM(edges[0].shape, f32)],
+        input_output_aliases={5 + i: i for i in range(5)},
+        compiler_params=pltpu.CompilerParams(vmem_limit_bytes=VMEM_LIMIT),
+    )(*inputs)
 
 
 def strip_kernel(count, offsets, lon_axis, lat_axis, partner, gathered_pieces, beyond_out, face_out, blocks):
@@ -580,7 +616,9 @@
     halo2 = odd_pairs(pay2, "lon")
     across_two = strip_swap(strips, 2)
     beyond, face = strip_rows(partner, [strips, across_two, halo1, halo2], offsets)
-    *coeffs, squares, face = coefficients(*fields, residual, halo1, halo2, rows_in, face)
+    *own, oc_edge, ek_edge, squares = own_coefficients(*fields, residual, rows_in)
+    groups = direction.shape[1] // 8
+    *coeffs, face = with_columns_beside(groups, own, (oc_edge, ek_edge), halo1, halo2, face)
     image, stats = image_and_stats(direction, land_sea, residual, squares, coeffs, beyond, face)
     parts, _ = butterfly([stats], [0], lambda value, distance: swapped(value, "lon", distance), distances(count)[::-1])
     parts.append(swapped(jnp.concatenate(parts, axis=0), "lat", 1))

time: 33.5 us -> 33.2 us (level)
  waiting for transfers between devices: 14.8 us -> 14 us
  starting transfers between devices: 10.8 us -> 11.3 us
    ppermute x2, waiting for transfers between devices: 2.69 us -> 2.08 us  [strip_swap(): lax.ppermute(value, ('member', 'lon', 'lat'), [(number(*p), other(*p)) fo...]
    pallas_call x1 -> x2, Pallas kernels: 0.97 us -> 1.16 us  [the longest x1 0.6 us: own_coefficients(): pl.pallas_call(functools.partial(own_kernel, 'lat'), out_shape=[jax.Shape...]
  transfers between devices with their start and end apart: 9 -> 9, of which waited for: 7 -> 7; matrix products, arithmetic and copies ran while one was open for 0% -> 0% of each run, Pallas kernels for 0% -> 2%
where the time goes in v9:
time: 33.2 us; the launch traced here: 33 us
  waiting for transfers between devices  14 us (42%)
  starting transfers between devices  11.3 us (34%)
  Pallas kernels  6.91 us (21%)
  between operations  0.78 us (2%)
    ppermute x6, waiting for transfers between devices, swapped(): lax.ppermute(value, axis, [(i, i ^ distance) for i in range(lax.axis_size...  11.8 us
    ppermute x6, starting transfers between devices, swapped(): lax.ppermute(value, axis, [(i, i ^ distance) for i in range(lax.axis_size...  5.45 us
    ppermute x1, starting transfers between devices, odd_pairs(): return lax.ppermute(value, axis, pairs)  3.54 us
    pallas_call x1, Pallas kernels, image_and_stats(): pl.pallas_call(image_kernel, out_shape=[jax.ShapeDtypeStruct(d.shape, f32...  3.23 us
    ppermute x2, starting transfers between devices, strip_swap(): lax.ppermute(value, ('member', 'lon', 'lat'), [(number(*p), other(*p)) fo...  2.27 us
    ppermute x2, waiting for transfers between devices, strip_swap(): lax.ppermute(value, ('member', 'lon', 'lat'), [(number(*p), other(*p)) fo...  2.08 us
    pallas_call x1, Pallas kernels, update(): pl.pallas_call(functools.partial(update_kernel, len(parts)), out_shape=[j...  1.14 us
    pallas_call x1, Pallas kernels, rows_to_send(): pl.pallas_call(functools.partial(rows_kernel, 'lat'), out_shape=[jax.Shap...  0.98 us
  transfers between devices with their start and end apart: 9, of which 7 were waited for; matrix products, arithmetic and copies ran while one was open for 0% of the time, Pallas kernels for 2%

profile of v9, /device:TPU:0, one launch (start us, length us, event | category | flops | bytes accessed | tf_op | source)
XLA Modules:
  0.0 33.0 jit_solution(3280521007381563104)
XLA Ops:
  0.6 0.0 copy-start
  0.6 0.0 copy-start.1
  0.7 0.0 copy-start.3
  0.7 0.0 copy-start.4
  0.7 0.0 copy-start.5
  0.7 1.0 %shard_map.103 = (f32[56,128]{1,0:T(8,128)S(1)}, f32[8,8,128]{2,1,0:T(8,128)S(1)}, s32[8,128]{1,0:T(8,128)S(1)}) custom-call(f32[2,320,128]{2,1,0:T(8,128)} %refs_7_.1, s32[2,320,128]{2,1,0:T(8,128)} %sea.7, f32[2,320,128]{2,1,0:T(8,128)} %pw.5, f32[320,128]{1,0:T(8,128)} %ek.5, f32[320,128]{1,0:T(8,128)} %nk.5, s32[8,128]{1,0:T(8,128)} %bitcast.1), custom_call_target="tpu_custom_call" | custom-call | tf_op jit(solution)/shard_map/pallas_call | solution.py:67
  1.7 0.5 %collective-permute-start = (f32[8,8,128]{2,1,0:T(8,128)S(1)}, f32[8,8,128]{2,1,0:T(8,128)S(1)}, u32[]{:S(2)}, u32[]{:S(2)}) collective-permute-start(f32[8,8,128]{2,1,0:T(8,128)S(1)} %get-tuple-element.27), channel_id=1, source_target_pairs={{0,1},{1,0},{2,3},{3,2},{4,5},{5,4},{6,7},{7,6},{8,9},{9,8},{10,11... | collective-permute-start | bytes 98312 | tf_op jit(solution)/shard_map/ppermute | solution.py:571
  2.2 0.0 copy-start.2
  2.2 0.8 %collective-permute-start.1 = (f32[56,128]{1,0:T(8,128)S(1)}, f32[56,128]{1,0:T(8,128)S(1)}, u32[]{:S(2)}, u32[]{:S(2)}) collective-permute-start(f32[56,128]{1,0:T(8,128)S(1)} %get-tuple-element.31.refs_0_), channel_id=1, source_target_pairs={{1,9},{3,11},{5,13},{7,15},{9,1},{11,3},{13,5},{15,7},{17,25},{19,... | collective-permute-start | bytes 86024 | tf_op jit(solution)/shard_map/ppermute | solution.py:595
  3.0 0.0 collective-permute-done.1.refs_1_
  3.0 0.1 collective-permute-done.rows_in
  3.0 0.0 copy-done
  3.0 0.0 copy-done.1
  3.0 0.0 copy-done.3
  3.1 0.0 copy-done.4
  3.1 0.0 copy-done.5
  3.1 0.4 %shard_map.105 = (f32[280,128]{1,0:T(8,128)S(1)}, f32[280,128]{1,0:T(8,128)S(1)}, f32[112,128]{1,0:T(8,128)S(1)}) custom-call(f32[2,320,128]{2,1,0:T(8,128)S(1)} %copy-done, s32[2,320,128]{2,1,0:T(8,128)S(1)} %copy-done.1, f32[2,320,128]{2,1,0:T(8,128)S(1)} %copy-done.3, f32[320,128]{1,0:T(8,128)S(1)} %copy-done.4, f32[320,128]{1,0:T(8,128)S(1)} %copy-done.5, ...), custom_call_target="tpu_custom_call" | custom-call | tf_op jit(solution)/shard_map/pallas_call | solution.py:132
  3.5 2.9 %collective-permute-start.2 = (f32[280,128]{1,0:T(8,128)S(1)}, f32[280,128]{1,0:T(8,128)S(1)}, u32[]{:S(2)}, u32[]{:S(2)}) collective-permute-start(f32[280,128]{1,0:T(8,128)S(1)} %get-tuple-element.32), channel_id=1, source_target_pairs={{0,2},{2,0},{4,6},{6,4},{8,10},{10,8},{12,14},{14,12},{1,3},{3,1},... | collective-permute-start | bytes 430088 | tf_op jit(solution)/shard_map/ppermute | solution.py:571
  6.4 3.5 %collective-permute-start.3 = (f32[280,128]{1,0:T(8,128)S(1)}, f32[280,128]{1,0:T(8,128)S(1)}, u32[]{:S(2)}, u32[]{:S(2)}) collective-permute-start(f32[280,128]{1,0:T(8,128)S(1)} %get-tuple-element.33), channel_id=1, source_target_pairs={{2,4},{4,2},{6,8},{8,6},{10,12},{12,10},{14,0},{0,14},{3,5},{5,3},... | collective-permute-start | bytes 430088 | tf_op jit(solution)/shard_map/ppermute | solution.py:579
  10.0 1.5 %collective-permute-start.4 = (f32[112,128]{1,0:T(8,128)S(1)}, f32[112,128]{1,0:T(8,128)S(1)}, u32[]{:S(2)}, u32[]{:S(2)}) collective-permute-start(f32[112,128]{1,0:T(8,128)S(1)} %get-tuple-element.35.refs_0_), channel_id=1, source_target_pairs={{0,16},{1,5},{2,18},{3,7},{4,20},{5,1},{6,22},{7,3},{8,24},{9,13},... | collective-permute-start | bytes 172040 | tf_op jit(solution)/shard_map/ppermute | solution.py:595
  11.4 0.0 copy-done.2
  11.4 0.6 %shard_map.104 = (f32[3,360,128]{2,1,0:T(8,128)S(1)}, f32[3,360,128]{2,1,0:T(8,128)S(1)}, f32[3,360,128]{2,1,0:T(8,128)S(1)}, f32[3,360,128]{2,1,0:T(8,128)S(1)}...) custom-call(f32[2,320,128]{2,1,0:T(8,128)S(1)} %copy-done, ...), custom_call_target="tpu_custom_call" | custom-call | tf_op jit(solution)/shard_map/pallas_call | solution.py:223
  12.1 2.1 %collective-permute-done.4.refs_1_ = f32[112,128]{1,0:T(8,128)S(1)} collective-permute-done((f32[112,128]{1,0:T(8,128)S(1)}, f32[112,128]{1,0:T(8,128)S(1)}, u32[]{:S(2)}, u32[]{:S(2)}) %collective-permute-start.4) | collective-permute-done | bytes 57376 | tf_op jit(solution)/shard_map/ppermute | solution.py:595
  14.1 0.0 collective-permute-done.2.refs_2_.halo1
  14.1 0.2 collective-permute-done.3.refs_3_.halo2
  14.3 0.6 %shard_map.107 = (f32[3,360,128]{2,1,0:T(8,128)S(1)}, f32[3,360,128]{2,1,0:T(8,128)S(1)}, f32[3,360,128]{2,1,0:T(8,128)S(1)}, f32[3,360,128]{2,1,0:T(8,128)S(1)}...) custom-call(f32[360,128]{1,0:T(8,128)S(1)} %get-tuple-element.29.oc_, ...), custom_call_target="tpu_custom_call", output_to_operand_aliasing={{0}: (5, {}), {1}: (6, {}), {2}: (7, {}), {3}: (8, {}), {4}... | custom-call | tf_op jit(solution)/shard_map/pallas_call | solution.py:284
  14.9 0.0 copy-start.6
  14.9 3.2 %shard_map.108 = (f32[2,320,128]{2,1,0:T(8,128)S(1)}, f32[1,128]{1,0:T(1,128)S(1)}) custom-call(f32[2,320,128]{2,1,0:T(8,128)S(1)} %copy-done, s32[2,320,128]{2,1,0:T(8,128)S(1)} %copy-done.1, f32[2,320,128]{2,1,0:T(8,128)S(1)} %copy-done.2, f32[8,128]{1,0:T(8,128)S(1)} %get-tuple-element.28.squares, f32[3,360,128]{2,1,0:T(8,128)S(1)} %get-tuple-element.42.first_field, ...), custom_call_target="tpu_custom_call" | custom-call | tf_op jit(solution)/shard_map/pallas_call | solution.py:505
  18.1 0.1 collective-permute-start.5
  18.2 3.5 %collective-permute-done.5.refs_1_ = f32[1,128]{1,0:T(1,128)S(1)} collective-permute-done((f32[1,128]{1,0:T(1,128)S(1)}, f32[1,128]{1,0:T(1,128)S(1)}, u32[]{:S(2)}, u32[]{:S(2)}) %collective-permute-start.5) | collective-permute-done | bytes 544 | tf_op jit(solution)/shard_map/ppermute | solution.py:571
  21.8 0.0 collective-permute-start.6
  21.8 3.6 %collective-permute-done.6.refs_2_ = f32[2,128]{1,0:T(2,128)S(1)} collective-permute-done((f32[2,128]{1,0:T(2,128)S(1)}, f32[2,128]{1,0:T(2,128)S(1)}, u32[]{:S(2)}, u32[]{:S(2)}) %collective-permute-start.6) | collective-permute-done | bytes 1056 | tf_op jit(solution)/shard_map/ppermute | solution.py:571
  25.3 0.8 %collective-permute-start.7 = (f32[4,128]{1,0:T(4,128)S(1)}, f32[4,128]{1,0:T(4,128)S(1)}, u32[]{:S(2)}, u32[]{:S(2)}) collective-permute-start(f32[4,128]{1,0:T(4,128)S(1)} %pad_maximum_fusion.1), channel_id=1, source_target_pairs={{0,8},{2,10},{4,12},{6,14},{8,0},{10,2},{12,4},{14,6},{1,9},{3,11}... | collective-permute-start | bytes 6152 | tf_op jit(solution)/shard_map/ppermute | solution.py:571
  26.1 3.8 %collective-permute-done.7.refs_3_ = f32[4,128]{1,0:T(4,128)S(1)} collective-permute-done((f32[4,128]{1,0:T(4,128)S(1)}, f32[4,128]{1,0:T(4,128)S(1)}, u32[]{:S(2)}, u32[]{:S(2)}) %collective-permute-start.7) | collective-permute-done | bytes 2080 | tf_op jit(solution)/shard_map/ppermute | solution.py:571
  29.9 1.2 %collective-permute-start.8 = (f32[8,128]{1,0:T(8,128)S(1)}, f32[8,128]{1,0:T(8,128)S(1)}, u32[]{:S(2)}, u32[]{:S(2)}) collective-permute-start(f32[8,128]{1,0:T(8,128)S(1)} %pad_maximum_fusion), channel_id=1, source_target_pairs={{0,1},{1,0},{2,3},{3,2},{4,5},{5,4},{6,7},{7,6},{8,9},{9,8},{10,11... | collective-permute-start | bytes 12296 | tf_op jit(solution)/shard_map/ppermute | solution.py:571
  31.1 0.8 %collective-permute-done.8.refs_4_ = f32[8,128]{1,0:T(8,128)S(1)} collective-permute-done((f32[8,128]{1,0:T(8,128)S(1)}, f32[8,128]{1,0:T(8,128)S(1)}, u32[]{:S(2)}, u32[]{:S(2)}) %collective-permute-start.8) | collective-permute-done | bytes 4128 | tf_op jit(solution)/shard_map/ppermute | solution.py:571
  31.9 0.0 copy-done.6
  31.9 1.1 %shard_map.109 = (f32[2,320,128]{2,1,0:T(8,128)}, f32[2,320,128]{2,1,0:T(8,128)}, f32[2,320,128]{2,1,0:T(8,128)}) custom-call(f32[1,128]{1,0:T(1,128)S(1)} %get-tuple-element.49.refs_0_, f32[1,128]{1,0:T(1,128)S(1)} %collective-permute-done.5.refs_1_, f32[2,128]{1,0:T(2,128)S(1)} %collective-permute-done.6.refs_2_, ...), custom_call_target="tpu_custom_call" | custom-call | tf_op jit(solution)/shard_map/pallas_call | solution.py:560
  (4 shorter events, 0.0 us)
Async XLA Ops:
  0.6 2.4 %copy-start = (f32[2,320,128]{2,1,0:T(8,128)S(1)}, f32[2,320,128]{2,1,0:T(8,128)}, u32[]{:S(2)}) copy-start(f32[2,320,128]{2,1,0:T(8,128)} %refs_7_.1) | copy-start | bytes 983044
  0.6 2.4 %copy-start.1 = (s32[2,320,128]{2,1,0:T(8,128)S(1)}, s32[2,320,128]{2,1,0:T(8,128)}, u32[]{:S(2)}) copy-start(s32[2,320,128]{2,1,0:T(8,128)} %sea.7) | copy-start | bytes 983044
  0.7 2.4 %copy-start.3 = (f32[2,320,128]{2,1,0:T(8,128)S(1)}, f32[2,320,128]{2,1,0:T(8,128)}, u32[]{:S(2)}) copy-start(f32[2,320,128]{2,1,0:T(8,128)} %pw.5) | copy-start | bytes 983044
  0.7 2.4 %copy-start.4 = (f32[320,128]{1,0:T(8,128)S(1)}, f32[320,128]{1,0:T(8,128)}, u32[]{:S(2)}) copy-start(f32[320,128]{1,0:T(8,128)} %ek.5) | copy-start | bytes 491524
  0.7 2.4 %copy-start.5 = (f32[320,128]{1,0:T(8,128)S(1)}, f32[320,128]{1,0:T(8,128)}, u32[]{:S(2)}) copy-start(f32[320,128]{1,0:T(8,128)} %nk.5) | copy-start | bytes 491524
  1.7 1.4 %collective-permute-start = (f32[8,8,128]{2,1,0:T(8,128)S(1)}, f32[8,8,128]{2,1,0:T(8,128)S(1)}, u32[]{:S(2)}, u32[]{:S(2)}) collective-permute-start(f32[8,8,128]{2,1,0:T(8,128)S(1)} %get-tuple-element.27), channel_id=1, source_target_pairs={{0,1},{1,0},{2,3},{3,2},{4,5},{5,4},{6,7},{7,6},{8,9},{9,8},{10,11... | collective-permute-start | bytes 98312 | tf_op jit(solution)/shard_map/ppermute | solution.py:571
  2.2 9.3 %copy-start.2 = (f32[2,320,128]{2,1,0:T(8,128)S(1)}, f32[2,320,128]{2,1,0:T(8,128)}, u32[]{:S(2)}) copy-start(f32[2,320,128]{2,1,0:T(8,128)} %refs_6_.1) | copy-start | bytes 983044
  2.2 0.8 %collective-permute-start.1 = (f32[56,128]{1,0:T(8,128)S(1)}, f32[56,128]{1,0:T(8,128)S(1)}, u32[]{:S(2)}, u32[]{:S(2)}) collective-permute-start(f32[56,128]{1,0:T(8,128)S(1)} %get-tuple-element.31.refs_0_), channel_id=1, source_target_pairs={{1,9},{3,11},{5,13},{7,15},{9,1},{11,3},{13,5},{15,7},{17,25},{19,... | collective-permute-start | bytes 86024 | tf_op jit(solution)/shard_map/ppermute | solution.py:595
  3.5 10.7 %collective-permute-start.2 = (f32[280,128]{1,0:T(8,128)S(1)}, f32[280,128]{1,0:T(8,128)S(1)}, u32[]{:S(2)}, u32[]{:S(2)}) collective-permute-start(f32[280,128]{1,0:T(8,128)S(1)} %get-tuple-element.32), channel_id=1, source_target_pairs={{0,2},{2,0},{4,6},{6,4},{8,10},{10,8},{12,14},{14,12},{1,3},{3,1},... | collective-permute-start | bytes 430088 | tf_op jit(solution)/shard_map/ppermute | solution.py:571
  6.4 7.9 %collective-permute-start.3 = (f32[280,128]{1,0:T(8,128)S(1)}, f32[280,128]{1,0:T(8,128)S(1)}, u32[]{:S(2)}, u32[]{:S(2)}) collective-permute-start(f32[280,128]{1,0:T(8,128)S(1)} %get-tuple-element.33), channel_id=1, source_target_pairs={{2,4},{4,2},{6,8},{8,6},{10,12},{12,10},{14,0},{0,14},{3,5},{5,3},... | collective-permute-start | bytes 430088 | tf_op jit(solution)/shard_map/ppermute | solution.py:579
  10.0 4.2 %collective-permute-start.4 = (f32[112,128]{1,0:T(8,128)S(1)}, f32[112,128]{1,0:T(8,128)S(1)}, u32[]{:S(2)}, u32[]{:S(2)}) collective-permute-start(f32[112,128]{1,0:T(8,128)S(1)} %get-tuple-element.35.refs_0_), channel_id=1, source_target_pairs={{0,16},{1,5},{2,18},{3,7},{4,20},{5,1},{6,22},{7,3},{8,24},{9,13},... | collective-permute-start | bytes 172040 | tf_op jit(solution)/shard_map/ppermute | solution.py:595
  14.9 17.0 %copy-start.6 = (f32[2,320,128]{2,1,0:T(8,128)S(1)}, f32[2,320,128]{2,1,0:T(8,128)}, u32[]{:S(2)}) copy-start(f32[2,320,128]{2,1,0:T(8,128)} %refs_5_.1) | copy-start | bytes 983044
  18.1 3.6 %collective-permute-start.5 = (f32[1,128]{1,0:T(1,128)S(1)}, f32[1,128]{1,0:T(1,128)S(1)}, u32[]{:S(2)}, u32[]{:S(2)}) collective-permute-start(f32[1,128]{1,0:T(1,128)S(1)} %get-tuple-element.49.refs_0_), channel_id=1, source_target_pairs={{0,2},{2,0},{4,6},{6,4},{8,10},{10,8},{12,14},{14,12},{1,3},{3,1},... | collective-permute-start | bytes 1544 | tf_op jit(solution)/shard_map/ppermute | solution.py:571
  21.8 3.6 %collective-permute-start.6 = (f32[2,128]{1,0:T(2,128)S(1)}, f32[2,128]{1,0:T(2,128)S(1)}, u32[]{:S(2)}, u32[]{:S(2)}) collective-permute-start(f32[2,128]{1,0:T(2,128)S(1)} %pad_maximum_fusion.2), channel_id=1, source_target_pairs={{0,4},{2,6},{4,0},{6,2},{8,12},{10,14},{12,8},{14,10},{1,5},{3,7},... | collective-permute-start | bytes 3080 | tf_op jit(solution)/shard_map/ppermute | solution.py:571
  25.3 4.5 %collective-permute-start.7 = (f32[4,128]{1,0:T(4,128)S(1)}, f32[4,128]{1,0:T(4,128)S(1)}, u32[]{:S(2)}, u32[]{:S(2)}) collective-permute-start(f32[4,128]{1,0:T(4,128)S(1)} %pad_maximum_fusion.1), channel_id=1, source_target_pairs={{0,8},{2,10},{4,12},{6,14},{8,0},{10,2},{12,4},{14,6},{1,9},{3,11}... | collective-permute-start | bytes 6152 | tf_op jit(solution)/shard_map/ppermute | solution.py:571
  29.9 2.0 %collective-permute-start.8 = (f32[8,128]{1,0:T(8,128)S(1)}, f32[8,128]{1,0:T(8,128)S(1)}, u32[]{:S(2)}, u32[]{:S(2)}) collective-permute-start(f32[8,128]{1,0:T(8,128)S(1)} %pad_maximum_fusion), channel_id=1, source_target_pairs={{0,1},{1,0},{2,3},{3,2},{4,5},{5,4},{6,7},{7,6},{8,9},{9,8},{10,11... | collective-permute-start | bytes 12296 | tf_op jit(solution)/shard_map/ppermute | solution.py:571

commit v10 on v9

--- a/solution.py
+++ b/solution.py
@@ -184,6 +184,7 @@
 
     for s in range(2):
         ocean[s, at(groups + 2), :] = zero
+        field[s, at(groups + 2), :] = zero
     for group in range(groups):
         here = slice(8 * group, 8 * group + 8)
         set_group(
@@ -259,6 +260,7 @@
         north_c[2, at(group), :] = jnp.where(low, pair_turned, pair) * oc
 
     ocean[at(groups + 2), :] = jnp.zeros((8, LANES), f32)
+    field[2, at(groups + 2), :] = jnp.zeros((8, LANES), f32)
     for group in range(groups):
         set_group(group + 1, group % half_groups, group // half_groups)
     set_group(0, half_groups, 0, top)
@@ -422,7 +424,7 @@
 
 
 def image_kernel(
-    d, sea, res, squares, first_field, weight, east_c, west_c, north_c, beyond, face, image, stats, field, other
+    d, sea, res, squares, _, weight, east_c, west_c, north_c, beyond, face, image, stats, field, other
 ):
     groups = d.shape[1] // 8
     zero = jnp.zeros((8, LANES), f32)
@@ -431,11 +433,7 @@
     first_row = lax.broadcasted_iota(jnp.int32, (8, LANES), 0) == 0
     last = groups + 2
     for s in range(3):
-        for buffer in (field, other):
-            buffer[s, 0:8, :] = zero
-            buffer[s, 8 + 8 * last : 16 + 8 * last, :] = zero
-        for group in range(groups + 2):
-            field[s, at(group), :] = first_field[s, at(group), :]
+        other[s, at(last), :] = zero
 
     def step(t, source, target):
         before = [zero] * 3
@@ -482,16 +480,20 @@
             q = dv + o * u
             image[level, here, :] = q
             rq, dq, qq = rq + rv * q, dq + dv * q, qq + q * q
-    rr, rq, dq, qq = (jnp.sum(x) for x in (rr, rq, dq, qq))
-    a0 = jnp.where(qq > 0.0, rq / jnp.where(qq > 0.0, qq, 1.0), 0.0)
+    own = jnp.where(qq > 0.0, rq / jnp.where(qq > 0.0, qq, 1.0), 0.0)
     ss = sq = zero
     for group in range(groups):
         here = slice(8 * group, 8 * group + 8)
         for level in range(2):
             q = image[level, here, :]
-            s = res[level, here, :] - a0 * q
+            s = res[level, here, :] - own * q
             ss, sq = ss + s * s, sq + s * q
-    ss, sq = jnp.sum(ss), jnp.sum(sq)
+    rr, rq, dq, qq_all = (jnp.sum(x) for x in (rr, rq, dq, qq))
+    a0 = jnp.where(qq_all > 0.0, rq / jnp.where(qq_all > 0.0, qq_all, 1.0), 0.0)
+    t = a0 - own
+    ss = jnp.sum(ss + t * (t * qq - 2.0 * sq))
+    sq = jnp.sum(sq - t * qq)
+    qq = qq_all
     one = lanes_of((1, LANES))
     row = jnp.zeros((1, LANES), f32)
     for index, value in enumerate((rr, dq, ss, sq, qq, a0)):
@@ -502,14 +504,16 @@
 def image_and_stats(d, sea, res, squares, coeffs, beyond, face):
     full = pl.BlockSpec(memory_space=pltpu.VMEM)
     inputs = [d, sea, res, squares, *coeffs, beyond, face]
-    return pl.pallas_call(
+    image, stats, _ = pl.pallas_call(
         image_kernel,
-        out_shape=[jax.ShapeDtypeStruct(d.shape, f32), jax.ShapeDtypeStruct((1, LANES), f32)],
+        out_shape=[jax.ShapeDtypeStruct(x, f32) for x in (d.shape, (1, LANES), coeffs[0].shape)],
         in_specs=[full] * len(inputs),
-        out_specs=[full] * 2,
-        scratch_shapes=[pltpu.VMEM(coeffs[0].shape, f32)] * 2,
+        out_specs=[full] * 3,
+        scratch_shapes=[pltpu.VMEM(coeffs[0].shape, f32)],
+        input_output_aliases={4: 2},
         compiler_params=pltpu.CompilerParams(vmem_limit_bytes=VMEM_LIMIT),
     )(*inputs)
+    return image, stats
 
 
 def update_kernel(count, *refs):
@@ -527,7 +531,7 @@
     new_norm = pick(jnp.sum(norms, axis=0, keepdims=True), 2)
     beta = new_norm / old_norm
     rows = d.shape[1]
-    pieces = 2
+    pieces = 1
     alpha = jnp.broadcast_to(alpha, (8, LANES))
     beta = jnp.broadcast_to(beta, (8, LANES))
     copies = []

time: 33.2 us -> 33.2 us (level)
  no operation moved by 1% of the time
where the time goes in v10:
time: 33.2 us; the launch traced here: 33 us
  waiting for transfers between devices  14 us (42%)
  starting transfers between devices  11.3 us (34%)
  Pallas kernels  6.89 us (21%)
  between operations  0.78 us (2%)
    ppermute x6, waiting for transfers between devices, swapped(): lax.ppermute(value, axis, [(i, i ^ distance) for i in range(lax.axis_size...  11.8 us
    ppermute x6, starting transfers between devices, swapped(): lax.ppermute(value, axis, [(i, i ^ distance) for i in range(lax.axis_size...  5.45 us
    ppermute x1, starting transfers between devices, odd_pairs(): return lax.ppermute(value, axis, pairs)  3.54 us
    pallas_call x1, Pallas kernels, image_and_stats(): pl.pallas_call(image_kernel, out_shape=[jax.ShapeDtypeStruct(x, f32) for...  3.19 us
    ppermute x2, starting transfers between devices, strip_swap(): lax.ppermute(value, ('member', 'lon', 'lat'), [(number(*p), other(*p)) fo...  2.27 us
    ppermute x2, waiting for transfers between devices, strip_swap(): lax.ppermute(value, ('member', 'lon', 'lat'), [(number(*p), other(*p)) fo...  2.08 us
    pallas_call x1, Pallas kernels, update(): pl.pallas_call(functools.partial(update_kernel, len(parts)), out_shape=[j...  1.16 us
    pallas_call x1, Pallas kernels, rows_to_send(): pl.pallas_call(functools.partial(rows_kernel, 'lat'), out_shape=[jax.Shap...  0.98 us
  transfers between devices with their start and end apart: 9, of which 7 were waited for; matrix products, arithmetic and copies ran while one was open for 0% of the time, Pallas kernels for 2%

profile of v10, /device:TPU:0, one launch (start us, length us, event | category | flops | bytes accessed | tf_op | source)
XLA Modules:
  0.0 33.0 jit_solution(12777862872584777231)
XLA Ops:
  0.6 0.0 copy-start
  0.6 0.0 copy-start.1
  0.7 0.0 copy-start.3
  0.7 0.0 copy-start.4
  0.7 0.0 copy-start.5
  0.7 1.0 %shard_map.103 = (f32[56,128]{1,0:T(8,128)S(1)}, f32[8,8,128]{2,1,0:T(8,128)S(1)}, s32[8,128]{1,0:T(8,128)S(1)}) custom-call(f32[2,320,128]{2,1,0:T(8,128)} %refs_7_.1, s32[2,320,128]{2,1,0:T(8,128)} %sea.7, f32[2,320,128]{2,1,0:T(8,128)} %pw.5, f32[320,128]{1,0:T(8,128)} %ek.5, f32[320,128]{1,0:T(8,128)} %nk.5, s32[8,128]{1,0:T(8,128)} %bitcast.1), custom_call_target="tpu_custom_call" | custom-call | tf_op jit(solution)/shard_map/pallas_call | solution.py:67
  1.7 0.5 %collective-permute-start = (f32[8,8,128]{2,1,0:T(8,128)S(1)}, f32[8,8,128]{2,1,0:T(8,128)S(1)}, u32[]{:S(2)}, u32[]{:S(2)}) collective-permute-start(f32[8,8,128]{2,1,0:T(8,128)S(1)} %get-tuple-element.27), channel_id=1, source_target_pairs={{0,1},{1,0},{2,3},{3,2},{4,5},{5,4},{6,7},{7,6},{8,9},{9,8},{10,11... | collective-permute-start | bytes 98312 | tf_op jit(solution)/shard_map/ppermute | solution.py:575
  2.2 0.0 copy-start.2
  2.2 0.8 %collective-permute-start.1 = (f32[56,128]{1,0:T(8,128)S(1)}, f32[56,128]{1,0:T(8,128)S(1)}, u32[]{:S(2)}, u32[]{:S(2)}) collective-permute-start(f32[56,128]{1,0:T(8,128)S(1)} %get-tuple-element.31.refs_0_), channel_id=1, source_target_pairs={{1,9},{3,11},{5,13},{7,15},{9,1},{11,3},{13,5},{15,7},{17,25},{19,... | collective-permute-start | bytes 86024 | tf_op jit(solution)/shard_map/ppermute | solution.py:599
  3.0 0.0 collective-permute-done.1.refs_1_
  3.0 0.1 collective-permute-done.rows_in
  3.0 0.0 copy-done
  3.0 0.0 copy-done.1
  3.0 0.0 copy-done.3
  3.1 0.0 copy-done.4
  3.1 0.0 copy-done.5
  3.1 0.4 %shard_map.105 = (f32[280,128]{1,0:T(8,128)S(1)}, f32[280,128]{1,0:T(8,128)S(1)}, f32[112,128]{1,0:T(8,128)S(1)}) custom-call(f32[2,320,128]{2,1,0:T(8,128)S(1)} %copy-done, s32[2,320,128]{2,1,0:T(8,128)S(1)} %copy-done.1, f32[2,320,128]{2,1,0:T(8,128)S(1)} %copy-done.3, f32[320,128]{1,0:T(8,128)S(1)} %copy-done.4, f32[320,128]{1,0:T(8,128)S(1)} %copy-done.5, ...), custom_call_target="tpu_custom_call" | custom-call | tf_op jit(solution)/shard_map/pallas_call | solution.py:132
  3.5 2.9 %collective-permute-start.2 = (f32[280,128]{1,0:T(8,128)S(1)}, f32[280,128]{1,0:T(8,128)S(1)}, u32[]{:S(2)}, u32[]{:S(2)}) collective-permute-start(f32[280,128]{1,0:T(8,128)S(1)} %get-tuple-element.32), channel_id=1, source_target_pairs={{0,2},{2,0},{4,6},{6,4},{8,10},{10,8},{12,14},{14,12},{1,3},{3,1},... | collective-permute-start | bytes 430088 | tf_op jit(solution)/shard_map/ppermute | solution.py:575
  6.4 3.5 %collective-permute-start.3 = (f32[280,128]{1,0:T(8,128)S(1)}, f32[280,128]{1,0:T(8,128)S(1)}, u32[]{:S(2)}, u32[]{:S(2)}) collective-permute-start(f32[280,128]{1,0:T(8,128)S(1)} %get-tuple-element.33), channel_id=1, source_target_pairs={{2,4},{4,2},{6,8},{8,6},{10,12},{12,10},{14,0},{0,14},{3,5},{5,3},... | collective-permute-start | bytes 430088 | tf_op jit(solution)/shard_map/ppermute | solution.py:583
  10.0 1.5 %collective-permute-start.4 = (f32[112,128]{1,0:T(8,128)S(1)}, f32[112,128]{1,0:T(8,128)S(1)}, u32[]{:S(2)}, u32[]{:S(2)}) collective-permute-start(f32[112,128]{1,0:T(8,128)S(1)} %get-tuple-element.35.refs_0_), channel_id=1, source_target_pairs={{0,16},{1,5},{2,18},{3,7},{4,20},{5,1},{6,22},{7,3},{8,24},{9,13},... | collective-permute-start | bytes 172040 | tf_op jit(solution)/shard_map/ppermute | solution.py:599
  11.4 0.0 copy-done.2
  11.4 0.6 %shard_map.104 = (f32[3,360,128]{2,1,0:T(8,128)S(1)}, f32[3,360,128]{2,1,0:T(8,128)S(1)}, f32[3,360,128]{2,1,0:T(8,128)S(1)}, f32[3,360,128]{2,1,0:T(8,128)S(1)}...) custom-call(f32[2,320,128]{2,1,0:T(8,128)S(1)} %copy-done, ...), custom_call_target="tpu_custom_call" | custom-call | tf_op jit(solution)/shard_map/pallas_call | solution.py:224
  12.1 2.1 %collective-permute-done.4.refs_1_ = f32[112,128]{1,0:T(8,128)S(1)} collective-permute-done((f32[112,128]{1,0:T(8,128)S(1)}, f32[112,128]{1,0:T(8,128)S(1)}, u32[]{:S(2)}, u32[]{:S(2)}) %collective-permute-start.4) | collective-permute-done | bytes 57376 | tf_op jit(solution)/shard_map/ppermute | solution.py:599
  14.1 0.0 collective-permute-done.2.refs_2_.halo1
  14.1 0.2 collective-permute-done.3.refs_3_.halo2
  14.3 0.6 %shard_map.107 = (f32[3,360,128]{2,1,0:T(8,128)S(1)}, f32[3,360,128]{2,1,0:T(8,128)S(1)}, f32[3,360,128]{2,1,0:T(8,128)S(1)}, f32[3,360,128]{2,1,0:T(8,128)S(1)}...) custom-call(f32[360,128]{1,0:T(8,128)S(1)} %get-tuple-element.29.oc_, ...), custom_call_target="tpu_custom_call", output_to_operand_aliasing={{0}: (5, {}), {1}: (6, {}), {2}: (7, {}), {3}: (8, {}), {4}... | custom-call | tf_op jit(solution)/shard_map/pallas_call | solution.py:286
  14.9 0.0 copy-start.6
  14.9 3.2 %shard_map.108 = (f32[2,320,128]{2,1,0:T(8,128)S(1)}, f32[1,128]{1,0:T(1,128)S(1)}, f32[3,360,128]{2,1,0:T(8,128)S(1)}) custom-call(f32[2,320,128]{2,1,0:T(8,128)S(1)} %copy-done, s32[2,320,128]{2,1,0:T(8,128)S(1)} %copy-done.1, f32[2,320,128]{2,1,0:T(8,128)S(1)} %copy-done.2, ...), custom_call_target="tpu_custom_call", output_to_operand_aliasing={{2}: (4, {})} | custom-call | tf_op jit(solution)/shard_map/pallas_call | solution.py:507
  18.1 0.1 collective-permute-start.5
  18.2 3.5 %collective-permute-done.5.refs_1_ = f32[1,128]{1,0:T(1,128)S(1)} collective-permute-done((f32[1,128]{1,0:T(1,128)S(1)}, f32[1,128]{1,0:T(1,128)S(1)}, u32[]{:S(2)}, u32[]{:S(2)}) %collective-permute-start.5) | collective-permute-done | bytes 544 | tf_op jit(solution)/shard_map/ppermute | solution.py:575
  21.7 0.0 collective-permute-start.6
  21.7 3.6 %collective-permute-done.6.refs_2_ = f32[2,128]{1,0:T(2,128)S(1)} collective-permute-done((f32[2,128]{1,0:T(2,128)S(1)}, f32[2,128]{1,0:T(2,128)S(1)}, u32[]{:S(2)}, u32[]{:S(2)}) %collective-permute-start.6) | collective-permute-done | bytes 1056 | tf_op jit(solution)/shard_map/ppermute | solution.py:575
  25.3 0.8 %collective-permute-start.7 = (f32[4,128]{1,0:T(4,128)S(1)}, f32[4,128]{1,0:T(4,128)S(1)}, u32[]{:S(2)}, u32[]{:S(2)}) collective-permute-start(f32[4,128]{1,0:T(4,128)S(1)} %pad_maximum_fusion.1), channel_id=1, source_target_pairs={{0,8},{2,10},{4,12},{6,14},{8,0},{10,2},{12,4},{14,6},{1,9},{3,11}... | collective-permute-start | bytes 6152 | tf_op jit(solution)/shard_map/ppermute | solution.py:575
  26.1 3.8 %collective-permute-done.7.refs_3_ = f32[4,128]{1,0:T(4,128)S(1)} collective-permute-done((f32[4,128]{1,0:T(4,128)S(1)}, f32[4,128]{1,0:T(4,128)S(1)}, u32[]{:S(2)}, u32[]{:S(2)}) %collective-permute-start.7) | collective-permute-done | bytes 2080 | tf_op jit(solution)/shard_map/ppermute | solution.py:575
  29.9 1.2 %collective-permute-start.8 = (f32[8,128]{1,0:T(8,128)S(1)}, f32[8,128]{1,0:T(8,128)S(1)}, u32[]{:S(2)}, u32[]{:S(2)}) collective-permute-start(f32[8,128]{1,0:T(8,128)S(1)} %pad_maximum_fusion), channel_id=1, source_target_pairs={{0,1},{1,0},{2,3},{3,2},{4,5},{5,4},{6,7},{7,6},{8,9},{9,8},{10,11... | collective-permute-start | bytes 12296 | tf_op jit(solution)/shard_map/ppermute | solution.py:575
  31.0 0.8 %collective-permute-done.8.refs_4_ = f32[8,128]{1,0:T(8,128)S(1)} collective-permute-done((f32[8,128]{1,0:T(8,128)S(1)}, f32[8,128]{1,0:T(8,128)S(1)}, u32[]{:S(2)}, u32[]{:S(2)}) %collective-permute-start.8) | collective-permute-done | bytes 4128 | tf_op jit(solution)/shard_map/ppermute | solution.py:575
  31.9 0.0 copy-done.6
  31.9 1.2 %shard_map.109 = (f32[2,320,128]{2,1,0:T(8,128)}, f32[2,320,128]{2,1,0:T(8,128)}, f32[2,320,128]{2,1,0:T(8,128)}) custom-call(f32[1,128]{1,0:T(1,128)S(1)} %get-tuple-element.49.refs_0_, f32[1,128]{1,0:T(1,128)S(1)} %collective-permute-done.5.refs_1_, f32[2,128]{1,0:T(2,128)S(1)} %collective-permute-done.6.refs_2_, ...), custom_call_target="tpu_custom_call" | custom-call | tf_op jit(solution)/shard_map/pallas_call | solution.py:564
  (4 shorter events, 0.0 us)
Async XLA Ops:
  0.6 2.4 %copy-start = (f32[2,320,128]{2,1,0:T(8,128)S(1)}, f32[2,320,128]{2,1,0:T(8,128)}, u32[]{:S(2)}) copy-start(f32[2,320,128]{2,1,0:T(8,128)} %refs_7_.1) | copy-start | bytes 983044
  0.6 2.4 %copy-start.1 = (s32[2,320,128]{2,1,0:T(8,128)S(1)}, s32[2,320,128]{2,1,0:T(8,128)}, u32[]{:S(2)}) copy-start(s32[2,320,128]{2,1,0:T(8,128)} %sea.7) | copy-start | bytes 983044
  0.7 2.4 %copy-start.3 = (f32[2,320,128]{2,1,0:T(8,128)S(1)}, f32[2,320,128]{2,1,0:T(8,128)}, u32[]{:S(2)}) copy-start(f32[2,320,128]{2,1,0:T(8,128)} %pw.5) | copy-start | bytes 983044
  0.7 2.4 %copy-start.4 = (f32[320,128]{1,0:T(8,128)S(1)}, f32[320,128]{1,0:T(8,128)}, u32[]{:S(2)}) copy-start(f32[320,128]{1,0:T(8,128)} %ek.5) | copy-start | bytes 491524
  0.7 2.4 %copy-start.5 = (f32[320,128]{1,0:T(8,128)S(1)}, f32[320,128]{1,0:T(8,128)}, u32[]{:S(2)}) copy-start(f32[320,128]{1,0:T(8,128)} %nk.5) | copy-start | bytes 491524
  1.7 1.4 %collective-permute-start = (f32[8,8,128]{2,1,0:T(8,128)S(1)}, f32[8,8,128]{2,1,0:T(8,128)S(1)}, u32[]{:S(2)}, u32[]{:S(2)}) collective-permute-start(f32[8,8,128]{2,1,0:T(8,128)S(1)} %get-tuple-element.27), channel_id=1, source_target_pairs={{0,1},{1,0},{2,3},{3,2},{4,5},{5,4},{6,7},{7,6},{8,9},{9,8},{10,11... | collective-permute-start | bytes 98312 | tf_op jit(solution)/shard_map/ppermute | solution.py:575
  2.2 9.3 %copy-start.2 = (f32[2,320,128]{2,1,0:T(8,128)S(1)}, f32[2,320,128]{2,1,0:T(8,128)}, u32[]{:S(2)}) copy-start(f32[2,320,128]{2,1,0:T(8,128)} %refs_6_.1) | copy-start | bytes 983044
  2.2 0.8 %collective-permute-start.1 = (f32[56,128]{1,0:T(8,128)S(1)}, f32[56,128]{1,0:T(8,128)S(1)}, u32[]{:S(2)}, u32[]{:S(2)}) collective-permute-start(f32[56,128]{1,0:T(8,128)S(1)} %get-tuple-element.31.refs_0_), channel_id=1, source_target_pairs={{1,9},{3,11},{5,13},{7,15},{9,1},{11,3},{13,5},{15,7},{17,25},{19,... | collective-permute-start | bytes 86024 | tf_op jit(solution)/shard_map/ppermute | solution.py:599
  3.5 10.7 %collective-permute-start.2 = (f32[280,128]{1,0:T(8,128)S(1)}, f32[280,128]{1,0:T(8,128)S(1)}, u32[]{:S(2)}, u32[]{:S(2)}) collective-permute-start(f32[280,128]{1,0:T(8,128)S(1)} %get-tuple-element.32), channel_id=1, source_target_pairs={{0,2},{2,0},{4,6},{6,4},{8,10},{10,8},{12,14},{14,12},{1,3},{3,1},... | collective-permute-start | bytes 430088 | tf_op jit(solution)/shard_map/ppermute | solution.py:575
  6.4 7.9 %collective-permute-start.3 = (f32[280,128]{1,0:T(8,128)S(1)}, f32[280,128]{1,0:T(8,128)S(1)}, u32[]{:S(2)}, u32[]{:S(2)}) collective-permute-start(f32[280,128]{1,0:T(8,128)S(1)} %get-tuple-element.33), channel_id=1, source_target_pairs={{2,4},{4,2},{6,8},{8,6},{10,12},{12,10},{14,0},{0,14},{3,5},{5,3},... | collective-permute-start | bytes 430088 | tf_op jit(solution)/shard_map/ppermute | solution.py:583
  10.0 4.2 %collective-permute-start.4 = (f32[112,128]{1,0:T(8,128)S(1)}, f32[112,128]{1,0:T(8,128)S(1)}, u32[]{:S(2)}, u32[]{:S(2)}) collective-permute-start(f32[112,128]{1,0:T(8,128)S(1)} %get-tuple-element.35.refs_0_), channel_id=1, source_target_pairs={{0,16},{1,5},{2,18},{3,7},{4,20},{5,1},{6,22},{7,3},{8,24},{9,13},... | collective-permute-start | bytes 172040 | tf_op jit(solution)/shard_map/ppermute | solution.py:599
  14.9 17.0 %copy-start.6 = (f32[2,320,128]{2,1,0:T(8,128)S(1)}, f32[2,320,128]{2,1,0:T(8,128)}, u32[]{:S(2)}) copy-start(f32[2,320,128]{2,1,0:T(8,128)} %refs_5_.1) | copy-start | bytes 983044
  18.1 3.6 %collective-permute-start.5 = (f32[1,128]{1,0:T(1,128)S(1)}, f32[1,128]{1,0:T(1,128)S(1)}, u32[]{:S(2)}, u32[]{:S(2)}) collective-permute-start(f32[1,128]{1,0:T(1,128)S(1)} %get-tuple-element.49.refs_0_), channel_id=1, source_target_pairs={{0,2},{2,0},{4,6},{6,4},{8,10},{10,8},{12,14},{14,12},{1,3},{3,1},... | collective-permute-start | bytes 1544 | tf_op jit(solution)/shard_map/ppermute | solution.py:575
  21.7 3.6 %collective-permute-start.6 = (f32[2,128]{1,0:T(2,128)S(1)}, f32[2,128]{1,0:T(2,128)S(1)}, u32[]{:S(2)}, u32[]{:S(2)}) collective-permute-start(f32[2,128]{1,0:T(2,128)S(1)} %pad_maximum_fusion.2), channel_id=1, source_target_pairs={{0,4},{2,6},{4,0},{6,2},{8,12},{10,14},{12,8},{14,10},{1,5},{3,7},... | collective-permute-start | bytes 3080 | tf_op jit(solution)/shard_map/ppermute | solution.py:575
  25.3 4.5 %collective-permute-start.7 = (f32[4,128]{1,0:T(4,128)S(1)}, f32[4,128]{1,0:T(4,128)S(1)}, u32[]{:S(2)}, u32[]{:S(2)}) collective-permute-start(f32[4,128]{1,0:T(4,128)S(1)} %pad_maximum_fusion.1), channel_id=1, source_target_pairs={{0,8},{2,10},{4,12},{6,14},{8,0},{10,2},{12,4},{14,6},{1,9},{3,11}... | collective-permute-start | bytes 6152 | tf_op jit(solution)/shard_map/ppermute | solution.py:575
  29.9 2.0 %collective-permute-start.8 = (f32[8,128]{1,0:T(8,128)S(1)}, f32[8,128]{1,0:T(8,128)S(1)}, u32[]{:S(2)}, u32[]{:S(2)}) collective-permute-start(f32[8,128]{1,0:T(8,128)S(1)} %pad_maximum_fusion), channel_id=1, source_target_pairs={{0,1},{1,0},{2,3},{3,2},{4,5},{5,4},{6,7},{7,6},{8,9},{9,8},{10,11... | collective-permute-start | bytes 12296 | tf_op jit(solution)/shard_map/ppermute | solution.py:575

commit v11 on v10

--- a/solution.py
+++ b/solution.py
@@ -220,7 +220,7 @@
 
 def own_coefficients(d, sea, pw, ek, nk, res, rows_in):
     full = pl.BlockSpec(memory_space=pltpu.VMEM)
-    rows = d.shape[1] + 40
+    rows = d.shape[1] + 56
     return pl.pallas_call(
         functools.partial(own_kernel, "lat"),
         out_shape=[jax.ShapeDtypeStruct((3, rows, LANES), f32)] * 5

time: 33.2 us -> 33.2 us (level)
  no operation moved by 1% of the time
where the time goes in v11:
time: 33.2 us; the launch traced here: 33 us
  waiting for transfers between devices  14 us (42%)
  starting transfers between devices  11.3 us (34%)
  Pallas kernels  6.85 us (21%)
  between operations  0.78 us (2%)
    ppermute x6, waiting for transfers between devices, swapped(): lax.ppermute(value, axis, [(i, i ^ distance) for i in range(lax.axis_size...  11.8 us
    ppermute x6, starting transfers between devices, swapped(): lax.ppermute(value, axis, [(i, i ^ distance) for i in range(lax.axis_size...  5.45 us
    ppermute x1, starting transfers between devices, odd_pairs(): return lax.ppermute(value, axis, pairs)  3.54 us
    pallas_call x1, Pallas kernels, image_and_stats(): pl.pallas_call(image_kernel, out_shape=[jax.ShapeDtypeStruct(x, f32) for...  3.16 us
    ppermute x2, starting transfers between devices, strip_swap(): lax.ppermute(value, ('member', 'lon', 'lat'), [(number(*p), other(*p)) fo...  2.27 us
    ppermute x2, waiting for transfers between devices, strip_swap(): lax.ppermute(value, ('member', 'lon', 'lat'), [(number(*p), other(*p)) fo...  2.09 us
    pallas_call x1, Pallas kernels, update(): pl.pallas_call(functools.partial(update_kernel, len(parts)), out_shape=[j...  1.16 us
    pallas_call x1, Pallas kernels, rows_to_send(): pl.pallas_call(functools.partial(rows_kernel, 'lat'), out_shape=[jax.Shap...  0.98 us
  transfers between devices with their start and end apart: 9, of which 7 were waited for; matrix products, arithmetic and copies ran while one was open for 0% of the time, Pallas kernels for 2%

profile of v11, /device:TPU:0, one launch (start us, length us, event | category | flops | bytes accessed | tf_op | source)
XLA Modules:
  0.0 33.0 jit_solution(15219592083161813798)
XLA Ops:
  0.6 0.0 copy-start
  0.6 0.0 copy-start.1
  0.7 0.0 copy-start.3
  0.7 0.0 copy-start.4
  0.7 0.0 copy-start.5
  0.7 1.0 %shard_map.103 = (f32[56,128]{1,0:T(8,128)S(1)}, f32[8,8,128]{2,1,0:T(8,128)S(1)}, s32[8,128]{1,0:T(8,128)S(1)}) custom-call(f32[2,320,128]{2,1,0:T(8,128)} %refs_7_.1, s32[2,320,128]{2,1,0:T(8,128)} %sea.7, f32[2,320,128]{2,1,0:T(8,128)} %pw.5, f32[320,128]{1,0:T(8,128)} %ek.5, f32[320,128]{1,0:T(8,128)} %nk.5, s32[8,128]{1,0:T(8,128)} %bitcast.1), custom_call_target="tpu_custom_call" | custom-call | tf_op jit(solution)/shard_map/pallas_call | solution.py:67
  1.7 0.5 %collective-permute-start = (f32[8,8,128]{2,1,0:T(8,128)S(1)}, f32[8,8,128]{2,1,0:T(8,128)S(1)}, u32[]{:S(2)}, u32[]{:S(2)}) collective-permute-start(f32[8,8,128]{2,1,0:T(8,128)S(1)} %get-tuple-element.27), channel_id=1, source_target_pairs={{0,1},{1,0},{2,3},{3,2},{4,5},{5,4},{6,7},{7,6},{8,9},{9,8},{10,11... | collective-permute-start | bytes 98312 | tf_op jit(solution)/shard_map/ppermute | solution.py:575
  2.2 0.0 copy-start.2
  2.2 0.8 %collective-permute-start.1 = (f32[56,128]{1,0:T(8,128)S(1)}, f32[56,128]{1,0:T(8,128)S(1)}, u32[]{:S(2)}, u32[]{:S(2)}) collective-permute-start(f32[56,128]{1,0:T(8,128)S(1)} %get-tuple-element.31.refs_0_), channel_id=1, source_target_pairs={{1,9},{3,11},{5,13},{7,15},{9,1},{11,3},{13,5},{15,7},{17,25},{19,... | collective-permute-start | bytes 86024 | tf_op jit(solution)/shard_map/ppermute | solution.py:599
  3.0 0.0 collective-permute-done.1.refs_1_
  3.0 0.1 collective-permute-done.rows_in
  3.0 0.0 copy-done
  3.0 0.0 copy-done.1
  3.0 0.0 copy-done.3
  3.1 0.0 copy-done.4
  3.1 0.0 copy-done.5
  3.1 0.4 %shard_map.105 = (f32[280,128]{1,0:T(8,128)S(1)}, f32[280,128]{1,0:T(8,128)S(1)}, f32[112,128]{1,0:T(8,128)S(1)}) custom-call(f32[2,320,128]{2,1,0:T(8,128)S(1)} %copy-done, s32[2,320,128]{2,1,0:T(8,128)S(1)} %copy-done.1, f32[2,320,128]{2,1,0:T(8,128)S(1)} %copy-done.3, f32[320,128]{1,0:T(8,128)S(1)} %copy-done.4, f32[320,128]{1,0:T(8,128)S(1)} %copy-done.5, ...), custom_call_target="tpu_custom_call" | custom-call | tf_op jit(solution)/shard_map/pallas_call | solution.py:132
  3.5 2.9 %collective-permute-start.2 = (f32[280,128]{1,0:T(8,128)S(1)}, f32[280,128]{1,0:T(8,128)S(1)}, u32[]{:S(2)}, u32[]{:S(2)}) collective-permute-start(f32[280,128]{1,0:T(8,128)S(1)} %get-tuple-element.32), channel_id=1, source_target_pairs={{0,2},{2,0},{4,6},{6,4},{8,10},{10,8},{12,14},{14,12},{1,3},{3,1},... | collective-permute-start | bytes 430088 | tf_op jit(solution)/shard_map/ppermute | solution.py:575
  6.4 3.5 %collective-permute-start.3 = (f32[280,128]{1,0:T(8,128)S(1)}, f32[280,128]{1,0:T(8,128)S(1)}, u32[]{:S(2)}, u32[]{:S(2)}) collective-permute-start(f32[280,128]{1,0:T(8,128)S(1)} %get-tuple-element.33), channel_id=1, source_target_pairs={{2,4},{4,2},{6,8},{8,6},{10,12},{12,10},{14,0},{0,14},{3,5},{5,3},... | collective-permute-start | bytes 430088 | tf_op jit(solution)/shard_map/ppermute | solution.py:583
  9.9 1.5 %collective-permute-start.4 = (f32[112,128]{1,0:T(8,128)S(1)}, f32[112,128]{1,0:T(8,128)S(1)}, u32[]{:S(2)}, u32[]{:S(2)}) collective-permute-start(f32[112,128]{1,0:T(8,128)S(1)} %get-tuple-element.35.refs_0_), channel_id=1, source_target_pairs={{0,16},{1,5},{2,18},{3,7},{4,20},{5,1},{6,22},{7,3},{8,24},{9,13},... | collective-permute-start | bytes 172040 | tf_op jit(solution)/shard_map/ppermute | solution.py:599
  11.4 0.0 copy-done.2
  11.4 0.6 %shard_map.104 = (f32[3,376,128]{2,1,0:T(8,128)S(1)}, f32[3,376,128]{2,1,0:T(8,128)S(1)}, f32[3,376,128]{2,1,0:T(8,128)S(1)}, f32[3,376,128]{2,1,0:T(8,128)S(1)}...) custom-call(f32[2,320,128]{2,1,0:T(8,128)S(1)} %copy-done, ...), custom_call_target="tpu_custom_call" | custom-call | tf_op jit(solution)/shard_map/pallas_call | solution.py:224
  12.0 2.1 %collective-permute-done.4.refs_1_ = f32[112,128]{1,0:T(8,128)S(1)} collective-permute-done((f32[112,128]{1,0:T(8,128)S(1)}, f32[112,128]{1,0:T(8,128)S(1)}, u32[]{:S(2)}, u32[]{:S(2)}) %collective-permute-start.4) | collective-permute-done | bytes 57376 | tf_op jit(solution)/shard_map/ppermute | solution.py:599
  14.1 0.0 collective-permute-done.2.refs_2_.halo1
  14.1 0.2 collective-permute-done.3.refs_3_.halo2
  14.3 0.6 %shard_map.107 = (f32[3,376,128]{2,1,0:T(8,128)S(1)}, f32[3,376,128]{2,1,0:T(8,128)S(1)}, f32[3,376,128]{2,1,0:T(8,128)S(1)}, f32[3,376,128]{2,1,0:T(8,128)S(1)}...) custom-call(f32[376,128]{1,0:T(8,128)S(1)} %get-tuple-element.29.oc_, ...), custom_call_target="tpu_custom_call", output_to_operand_aliasing={{0}: (5, {}), {1}: (6, {}), {2}: (7, {}), {3}: (8, {}), {4}... | custom-call | tf_op jit(solution)/shard_map/pallas_call | solution.py:286
  14.9 0.0 copy-start.6
  14.9 3.2 %shard_map.108 = (f32[2,320,128]{2,1,0:T(8,128)S(1)}, f32[1,128]{1,0:T(1,128)S(1)}, f32[3,376,128]{2,1,0:T(8,128)S(1)}) custom-call(f32[2,320,128]{2,1,0:T(8,128)S(1)} %copy-done, s32[2,320,128]{2,1,0:T(8,128)S(1)} %copy-done.1, f32[2,320,128]{2,1,0:T(8,128)S(1)} %copy-done.2, ...), custom_call_target="tpu_custom_call", output_to_operand_aliasing={{2}: (4, {})} | custom-call | tf_op jit(solution)/shard_map/pallas_call | solution.py:507
  18.1 0.1 collective-permute-start.5
  18.1 3.5 %collective-permute-done.5.refs_1_ = f32[1,128]{1,0:T(1,128)S(1)} collective-permute-done((f32[1,128]{1,0:T(1,128)S(1)}, f32[1,128]{1,0:T(1,128)S(1)}, u32[]{:S(2)}, u32[]{:S(2)}) %collective-permute-start.5) | collective-permute-done | bytes 544 | tf_op jit(solution)/shard_map/ppermute | solution.py:575
  21.7 0.0 collective-permute-start.6
  21.7 3.6 %collective-permute-done.6.refs_2_ = f32[2,128]{1,0:T(2,128)S(1)} collective-permute-done((f32[2,128]{1,0:T(2,128)S(1)}, f32[2,128]{1,0:T(2,128)S(1)}, u32[]{:S(2)}, u32[]{:S(2)}) %collective-permute-start.6) | collective-permute-done | bytes 1056 | tf_op jit(solution)/shard_map/ppermute | solution.py:575
  25.3 0.8 %collective-permute-start.7 = (f32[4,128]{1,0:T(4,128)S(1)}, f32[4,128]{1,0:T(4,128)S(1)}, u32[]{:S(2)}, u32[]{:S(2)}) collective-permute-start(f32[4,128]{1,0:T(4,128)S(1)} %pad_maximum_fusion.1), channel_id=1, source_target_pairs={{0,8},{2,10},{4,12},{6,14},{8,0},{10,2},{12,4},{14,6},{1,9},{3,11}... | collective-permute-start | bytes 6152 | tf_op jit(solution)/shard_map/ppermute | solution.py:575
  26.0 3.8 %collective-permute-done.7.refs_3_ = f32[4,128]{1,0:T(4,128)S(1)} collective-permute-done((f32[4,128]{1,0:T(4,128)S(1)}, f32[4,128]{1,0:T(4,128)S(1)}, u32[]{:S(2)}, u32[]{:S(2)}) %collective-permute-start.7) | collective-permute-done | bytes 2080 | tf_op jit(solution)/shard_map/ppermute | solution.py:575
  29.8 1.2 %collective-permute-start.8 = (f32[8,128]{1,0:T(8,128)S(1)}, f32[8,128]{1,0:T(8,128)S(1)}, u32[]{:S(2)}, u32[]{:S(2)}) collective-permute-start(f32[8,128]{1,0:T(8,128)S(1)} %pad_maximum_fusion), channel_id=1, source_target_pairs={{0,1},{1,0},{2,3},{3,2},{4,5},{5,4},{6,7},{7,6},{8,9},{9,8},{10,11... | collective-permute-start | bytes 12296 | tf_op jit(solution)/shard_map/ppermute | solution.py:575
  31.0 0.8 %collective-permute-done.8.refs_4_ = f32[8,128]{1,0:T(8,128)S(1)} collective-permute-done((f32[8,128]{1,0:T(8,128)S(1)}, f32[8,128]{1,0:T(8,128)S(1)}, u32[]{:S(2)}, u32[]{:S(2)}) %collective-permute-start.8) | collective-permute-done | bytes 4128 | tf_op jit(solution)/shard_map/ppermute | solution.py:575
  31.8 0.0 copy-done.6
  31.8 1.2 %shard_map.109 = (f32[2,320,128]{2,1,0:T(8,128)}, f32[2,320,128]{2,1,0:T(8,128)}, f32[2,320,128]{2,1,0:T(8,128)}) custom-call(f32[1,128]{1,0:T(1,128)S(1)} %get-tuple-element.49.refs_0_, f32[1,128]{1,0:T(1,128)S(1)} %collective-permute-done.5.refs_1_, f32[2,128]{1,0:T(2,128)S(1)} %collective-permute-done.6.refs_2_, ...), custom_call_target="tpu_custom_call" | custom-call | tf_op jit(solution)/shard_map/pallas_call | solution.py:564
  (4 shorter events, 0.0 us)
Async XLA Ops:
  0.6 2.4 %copy-start = (f32[2,320,128]{2,1,0:T(8,128)S(1)}, f32[2,320,128]{2,1,0:T(8,128)}, u32[]{:S(2)}) copy-start(f32[2,320,128]{2,1,0:T(8,128)} %refs_7_.1) | copy-start | bytes 983044
  0.6 2.4 %copy-start.1 = (s32[2,320,128]{2,1,0:T(8,128)S(1)}, s32[2,320,128]{2,1,0:T(8,128)}, u32[]{:S(2)}) copy-start(s32[2,320,128]{2,1,0:T(8,128)} %sea.7) | copy-start | bytes 983044
  0.7 2.4 %copy-start.3 = (f32[2,320,128]{2,1,0:T(8,128)S(1)}, f32[2,320,128]{2,1,0:T(8,128)}, u32[]{:S(2)}) copy-start(f32[2,320,128]{2,1,0:T(8,128)} %pw.5) | copy-start | bytes 983044
  0.7 2.4 %copy-start.4 = (f32[320,128]{1,0:T(8,128)S(1)}, f32[320,128]{1,0:T(8,128)}, u32[]{:S(2)}) copy-start(f32[320,128]{1,0:T(8,128)} %ek.5) | copy-start | bytes 491524
  0.7 2.4 %copy-start.5 = (f32[320,128]{1,0:T(8,128)S(1)}, f32[320,128]{1,0:T(8,128)}, u32[]{:S(2)}) copy-start(f32[320,128]{1,0:T(8,128)} %nk.5) | copy-start | bytes 491524
  1.7 1.4 %collective-permute-start = (f32[8,8,128]{2,1,0:T(8,128)S(1)}, f32[8,8,128]{2,1,0:T(8,128)S(1)}, u32[]{:S(2)}, u32[]{:S(2)}) collective-permute-start(f32[8,8,128]{2,1,0:T(8,128)S(1)} %get-tuple-element.27), channel_id=1, source_target_pairs={{0,1},{1,0},{2,3},{3,2},{4,5},{5,4},{6,7},{7,6},{8,9},{9,8},{10,11... | collective-permute-start | bytes 98312 | tf_op jit(solution)/shard_map/ppermute | solution.py:575
  2.2 9.3 %copy-start.2 = (f32[2,320,128]{2,1,0:T(8,128)S(1)}, f32[2,320,128]{2,1,0:T(8,128)}, u32[]{:S(2)}) copy-start(f32[2,320,128]{2,1,0:T(8,128)} %refs_6_.1) | copy-start | bytes 983044
  2.2 0.8 %collective-permute-start.1 = (f32[56,128]{1,0:T(8,128)S(1)}, f32[56,128]{1,0:T(8,128)S(1)}, u32[]{:S(2)}, u32[]{:S(2)}) collective-permute-start(f32[56,128]{1,0:T(8,128)S(1)} %get-tuple-element.31.refs_0_), channel_id=1, source_target_pairs={{1,9},{3,11},{5,13},{7,15},{9,1},{11,3},{13,5},{15,7},{17,25},{19,... | collective-permute-start | bytes 86024 | tf_op jit(solution)/shard_map/ppermute | solution.py:599
  3.5 10.7 %collective-permute-start.2 = (f32[280,128]{1,0:T(8,128)S(1)}, f32[280,128]{1,0:T(8,128)S(1)}, u32[]{:S(2)}, u32[]{:S(2)}) collective-permute-start(f32[280,128]{1,0:T(8,128)S(1)} %get-tuple-element.32), channel_id=1, source_target_pairs={{0,2},{2,0},{4,6},{6,4},{8,10},{10,8},{12,14},{14,12},{1,3},{3,1},... | collective-permute-start | bytes 430088 | tf_op jit(solution)/shard_map/ppermute | solution.py:575
  6.4 7.9 %collective-permute-start.3 = (f32[280,128]{1,0:T(8,128)S(1)}, f32[280,128]{1,0:T(8,128)S(1)}, u32[]{:S(2)}, u32[]{:S(2)}) collective-permute-start(f32[280,128]{1,0:T(8,128)S(1)} %get-tuple-element.33), channel_id=1, source_target_pairs={{2,4},{4,2},{6,8},{8,6},{10,12},{12,10},{14,0},{0,14},{3,5},{5,3},... | collective-permute-start | bytes 430088 | tf_op jit(solution)/shard_map/ppermute | solution.py:583
  9.9 4.2 %collective-permute-start.4 = (f32[112,128]{1,0:T(8,128)S(1)}, f32[112,128]{1,0:T(8,128)S(1)}, u32[]{:S(2)}, u32[]{:S(2)}) collective-permute-start(f32[112,128]{1,0:T(8,128)S(1)} %get-tuple-element.35.refs_0_), channel_id=1, source_target_pairs={{0,16},{1,5},{2,18},{3,7},{4,20},{5,1},{6,22},{7,3},{8,24},{9,13},... | collective-permute-start | bytes 172040 | tf_op jit(solution)/shard_map/ppermute | solution.py:599
  14.9 16.9 %copy-start.6 = (f32[2,320,128]{2,1,0:T(8,128)S(1)}, f32[2,320,128]{2,1,0:T(8,128)}, u32[]{:S(2)}) copy-start(f32[2,320,128]{2,1,0:T(8,128)} %refs_5_.1) | copy-start | bytes 983044
  18.1 3.6 %collective-permute-start.5 = (f32[1,128]{1,0:T(1,128)S(1)}, f32[1,128]{1,0:T(1,128)S(1)}, u32[]{:S(2)}, u32[]{:S(2)}) collective-permute-start(f32[1,128]{1,0:T(1,128)S(1)} %get-tuple-element.49.refs_0_), channel_id=1, source_target_pairs={{0,2},{2,0},{4,6},{6,4},{8,10},{10,8},{12,14},{14,12},{1,3},{3,1},... | collective-permute-start | bytes 1544 | tf_op jit(solution)/shard_map/ppermute | solution.py:575
  21.7 3.6 %collective-permute-start.6 = (f32[2,128]{1,0:T(2,128)S(1)}, f32[2,128]{1,0:T(2,128)S(1)}, u32[]{:S(2)}, u32[]{:S(2)}) collective-permute-start(f32[2,128]{1,0:T(2,128)S(1)} %pad_maximum_fusion.2), channel_id=1, source_target_pairs={{0,4},{2,6},{4,0},{6,2},{8,12},{10,14},{12,8},{14,10},{1,5},{3,7},... | collective-permute-start | bytes 3080 | tf_op jit(solution)/shard_map/ppermute | solution.py:575
  25.3 4.5 %collective-permute-start.7 = (f32[4,128]{1,0:T(4,128)S(1)}, f32[4,128]{1,0:T(4,128)S(1)}, u32[]{:S(2)}, u32[]{:S(2)}) collective-permute-start(f32[4,128]{1,0:T(4,128)S(1)} %pad_maximum_fusion.1), channel_id=1, source_target_pairs={{0,8},{2,10},{4,12},{6,14},{8,0},{10,2},{12,4},{14,6},{1,9},{3,11}... | collective-permute-start | bytes 6152 | tf_op jit(solution)/shard_map/ppermute | solution.py:575
  29.8 2.0 %collective-permute-start.8 = (f32[8,128]{1,0:T(8,128)S(1)}, f32[8,128]{1,0:T(8,128)S(1)}, u32[]{:S(2)}, u32[]{:S(2)}) collective-permute-start(f32[8,128]{1,0:T(8,128)S(1)} %pad_maximum_fusion), channel_id=1, source_target_pairs={{0,1},{1,0},{2,3},{3,2},{4,5},{5,4},{6,7},{7,6},{8,9},{9,8},{10,11... | collective-permute-start | bytes 12296 | tf_op jit(solution)/shard_map/ppermute | solution.py:575
